TPU v7x, 32 devices: a whole 2x2x4 slice. The times are simulated.
32 devices in a mesh: space: 8 (over z, y), tm: 4 (over x, core).
Axes of the slice: x: 2, y: 2, z: 4, core: 2. Of those that a mesh axis runs over, the one named last changes fastest.
Arguments:
- snapshots: bfloat16 [8192, 16384], P('space', 'tm'), may hold values from -1200 to 1200
- pod_basis: bfloat16 [8192, 96], P('space'), may hold values from -0.0625 to 0.0625
- inputs: bfloat16 [112, 16384], P(None, 'tm'), may hold values from -20 to 20
Outputs:
- factored: float32 [4864, 4864], P('tm', 'space')
All inputs are finite; a program needn't handle non-finite values.
Results may differ from a plain program's by a relative error of at most 0.0031.
Values may be sent and summed in bfloat16 or wider, within the bound.
No kernel may reach another device: no remote copies, remote signals or barrier semaphores. Data moves between devices by JAX's collectives and lax.ppermute only.
A program may use at most 192 MiB of HBM per device.

v0:
```python
import functools
import math

import jax
import jax.numpy as jnp
import numpy as np
from jax import lax
from jax.experimental import pallas as pl
from jax.experimental.pallas import tpu as pltpu
from jax.sharding import PartitionSpec as P

NB = 128
EPS = 1e-06
REG = 0.5
PAD = 8
LANES = 128


def feature_pairs(modes, count):
    first, second = np.triu_indices(modes)
    lead = [(f, None) for f in range(modes)]
    pairs = list(zip(first.tolist(), second.tolist()))
    tail = [(modes + k, None) for k in range(count)]
    return lead + pairs + tail


def runs_of(rows):
    runs = []
    for at, row in enumerate(rows):
        if row is None:
            continue
        a, b = row
        key = ("one", a - at) if b is None else (a, b - at)
        if runs and runs[-1][2] == key and runs[-1][1] == at:
            runs[-1][1] = at + 1
        else:
            runs.append([at, at + 1, key])
    return runs


def build_rows(x_ref, f_ref, lane, rows, base, extra=None):
    sub = lax.broadcasted_iota(jnp.int32, (8, LANES), 0)
    cache = {}

    def row_of(a):
        if a not in cache:
            cache.clear()
            cache[a] = jnp.broadcast_to(x_ref[lane, PAD + a : PAD + a + 1, :], (8, LANES))
        return cache[a]

    def eight(at):
        chunk = rows[at : at + 8]
        chunk = chunk + [None] * (8 - len(chunk))
        total = None
        for lo, hi, (a, shift) in runs_of(chunk):
            part = x_ref[lane, PAD + shift : PAD + shift + 8, :]
            if a != "one":
                part = part * row_of(a)
            if total is None and lo == 0:
                total = part
            else:
                if total is None:
                    total = jnp.zeros((8, LANES), jnp.float32)
                total = jnp.where(sub >= lo, part, total)
            last = hi
        if total is None:
            return jnp.zeros((8, LANES), jnp.float32)
        if last < 8:
            total = jnp.where(sub < last, total, 0.0)
        return total

    for at in range(0, len(rows), 16):
        value = jnp.concatenate([eight(at), eight(at + 8)], axis=0).astype(jnp.bfloat16)
        f_ref[base + at : base + at + 16, pl.ds(pl.multiple_of(lane * LANES, LANES), LANES)] = value


def gram_kernel(plan, where_ref, x_in, u_in, inv_ref, acc_in, acc_ref, x_ref, f_ref):
    step = pl.program_id(0)
    modes, row_sets, col_sets, head_set, row_count, a_rows, b_rows = plan
    depth = x_in.shape[-1]
    lanes = depth // LANES

    @pl.when(step == 0)
    def _():
        f_ref[...] = jnp.zeros_like(f_ref)
        x_ref[...] = jnp.zeros_like(x_ref)
        if acc_in is None:
            acc_ref[...] = jnp.zeros_like(acc_ref)
        else:
            acc_ref[...] = acc_in[...]

    scale = inv_ref[...]
    for lane in range(lanes):
        at = slice(lane * LANES, (lane + 1) * LANES)
        x_ref[lane, PAD : PAD + modes, :] = x_in[0, :, at].astype(jnp.float32) * scale
        x_ref[lane, PAD + modes : PAD + modes + u_in.shape[1], :] = u_in[0, :, at].astype(jnp.float32)

    for number, rows in enumerate(row_sets):
        @pl.when(where_ref[0] == number)
        def _(rows=rows):
            @pl.loop(0, lanes)
            def _(lane):
                build_rows(x_ref, f_ref, lane, rows, 0)

    @pl.loop(0, lanes)
    def _(lane):
        build_rows(x_ref, f_ref, lane, head_set, row_count)

    for number, rows in enumerate(col_sets):
        @pl.when(where_ref[1] == number)
        def _(rows=rows):
            @pl.loop(0, lanes)
            def _(lane):
                build_rows(x_ref, f_ref, lane, rows, row_count + NB)

    left = f_ref[0:a_rows, :]
    for at in range(0, b_rows, 256):
        wide = min(256, b_rows - at)
        right = f_ref[row_count + at : row_count + at + wide, :]
        acc_ref[:, at : at + wide] += lax.dot_general(
            left, right, (((1,), (1,)), ((), ())), preferred_element_type=jnp.float32
        )


def make_plan(modes, count, time_count, space_count):
    pairs = feature_pairs(modes, count)
    total = len(pairs)
    row_count, col_count = total // time_count, total // space_count
    row_sets = [pairs[t * row_count : (t + 1) * row_count] for t in range(time_count)]
    col_sets = [pairs[s * col_count : (s + 1) * col_count] for s in range(space_count)]
    a_rows = row_count + NB
    b_rows = -(-(NB + col_count) // 128) * 128
    return modes, row_sets, col_sets, pairs[:NB], row_count, a_rows, b_rows


def gram_call(plan, where, x, u, inv, acc=None):
    modes, _, col_sets, _, row_count, a_rows, b_rows = plan
    steps, _, depth = x.shape
    groups = u.shape[0]
    per = steps // groups
    inputs = u.shape[1]
    lanes = depth // LANES
    in_specs = [
        pl.BlockSpec((1, modes, depth), lambda k, w: (k, 0, 0)),
        pl.BlockSpec((1, inputs, depth), lambda k, w: (k // per, 0, w[2 + k % per])),
        pl.BlockSpec((modes, 1), lambda k, w: (0, 0)),
    ]
    args = [x, u, inv]
    body = functools.partial(gram_kernel, plan)
    if acc is None:
        inner = lambda w, a, b, c, o, s1, s2: body(w, a, b, c, None, o, s1, s2)
    else:
        inner = body
        in_specs.append(pl.BlockSpec((a_rows, b_rows), lambda k, w: (0, 0)))
        args.append(acc)
    return pl.pallas_call(
        inner,
        grid_spec=pltpu.PrefetchScalarGridSpec(
            num_scalar_prefetch=1,
            grid=(steps,),
            in_specs=in_specs,
            out_specs=pl.BlockSpec((a_rows, b_rows), lambda k, w: (0, 0)),
            scratch_shapes=[
                pltpu.VMEM((lanes, PAD + modes + inputs + 8, LANES), jnp.float32),
                pltpu.VMEM((-(-(row_count + b_rows) // 16) * 16, depth), jnp.bfloat16),
            ],
        ),
        out_shape=jax.ShapeDtypeStruct((a_rows, b_rows), jnp.float32),
        compiler_params=pltpu.CompilerParams(vmem_limit_bytes=56 * 1024 * 1024, dimension_semantics=("arbitrary",)),
        name="gram",
    )(where, *args)


def inverse_factor(corner):
    sub = lax.broadcasted_iota(jnp.int32, (8, 2 * NB), 0)
    row_ids = lax.broadcasted_iota(jnp.int32, (NB, NB), 0)
    col_ids = lax.broadcasted_iota(jnp.int32, (NB, NB), 1)
    eye = (row_ids == col_ids).astype(jnp.float32)
    joined = jnp.concatenate([corner, eye], axis=1)
    tiles = [joined[at : at + 8] for at in range(0, NB, 8)]
    for k in range(NB):
        q, r = divmod(k, 8)
        row = tiles[q][r : r + 1]
        row = row * (1.0 / row[:, k : k + 1])
        for p in range(q, NB // 8):
            column = tiles[p][:, k : k + 1]
            change = column * row
            if p == q:
                change = jnp.where(sub > r, change, 0.0)
            tiles[p] = tiles[p] - change
    done = jnp.concatenate(tiles, axis=0)
    pivots = jnp.sum(done[:, :NB] * eye, axis=1, keepdims=True)
    return done[:, NB:] * lax.rsqrt(pivots)


def dot32(a, b, dims):
    return lax.dot_general(
        a, b, (dims, ((), ())), precision=lax.Precision.HIGHEST, preferred_element_type=jnp.float32
    )


def finish_kernel(snaps, row_count, col_count, where_ref, acc_ref, out_ref):
    t, s = where_ref[0], where_ref[1]
    head = pl.ds(row_count, NB)
    row_ids = lax.broadcasted_iota(jnp.int32, (NB, NB), 0)
    col_ids = lax.broadcasted_iota(jnp.int32, (NB, NB), 1)
    eye = REG * (row_ids == col_ids).astype(jnp.float32)
    corner = acc_ref[head, 0:NB] * (1.0 / snaps) + eye
    inverse = inverse_factor(corner)
    cols = acc_ref[head, NB : NB + col_count] * (1.0 / snaps)
    all_rows = lax.broadcasted_iota(jnp.int32, (NB, col_count), 0)
    all_cols = s * col_count + lax.broadcasted_iota(jnp.int32, (NB, col_count), 1)
    cols = cols + REG * (all_rows == all_cols).astype(jnp.float32)
    cols_factor = dot32(inverse, cols, ((1,), (0,)))
    for at in range(0, row_count, NB):
        tall = min(NB, row_count - at)
        rows = slice(at, at + tall)
        ids = t * row_count + at + lax.broadcasted_iota(jnp.int32, (tall, col_count), 0)
        cids = s * col_count + lax.broadcasted_iota(jnp.int32, (tall, col_count), 1)
        side = acc_ref[rows, 0:NB] * (1.0 / snaps)
        side = side + REG * (ids[:, :NB] == lax.broadcasted_iota(jnp.int32, (tall, NB), 1)).astype(jnp.float32)
        factor = dot32(side, inverse, ((1,), (1,)))
        gram = acc_ref[rows, NB : NB + col_count] * (1.0 / snaps)
        gram = gram + REG * (ids == cids).astype(jnp.float32)
        value = gram - dot32(factor, cols_factor, ((1,), (0,)))
        value = jnp.where(ids < NB, 0.0, value)
        out_ref[rows, NB:col_count] = value[:, NB:]
        out_ref[rows, 0:NB] = jnp.where(s == 0, factor, value[:, :NB])


def finish(where, acc, snaps, row_count, col_count):
    return pl.pallas_call(
        functools.partial(finish_kernel, snaps, row_count, col_count),
        in_specs=[pl.BlockSpec(memory_space=pltpu.SMEM), pl.BlockSpec(memory_space=pltpu.VMEM)],
        out_specs=pl.BlockSpec(memory_space=pltpu.VMEM),
        out_shape=jax.ShapeDtypeStruct((row_count, col_count), jnp.float32),
        compiler_params=pltpu.CompilerParams(vmem_limit_bytes=40 * 1024 * 1024),
        name="finish",
    )(where, acc)


def swap(x, axis, bit):
    return lax.ppermute(x, axis, [(i, i ^ bit) for i in range(lax.axis_size(axis))])


def shards(snapshots, pod_basis, inputs):
    modes = pod_basis.shape[1]
    space_count, time_count = lax.axis_size("space"), lax.axis_size("tm")
    t, s = lax.axis_index("tm"), lax.axis_index("space")
    local = snapshots.shape[1]
    snaps = local * time_count
    depth = local // space_count
    plan = make_plan(modes, inputs.shape[0], time_count, space_count)
    row_count = plan[4]
    col_count = len(plan[2][0])
    last = space_count - 1

    pairs = [(a * time_count + b, a * time_count + (b ^ 2)) for a in range(space_count) for b in range(time_count) if a == last or b < 2]
    u_far = lax.ppermute(inputs, ("space", "tm"), pairs)
    pairs = [(a * time_count + b, a * time_count + (b ^ 1)) for a in range(space_count) for b in range(time_count) if a == last or b == 2]
    u_pair = lax.ppermute(jnp.stack([inputs, u_far]), ("space", "tm"), pairs)
    u_near = jnp.stack([inputs, u_pair[0]])
    u_far = jnp.stack([u_far, u_pair[1]])

    limit = 1200.0 * 0.0625 * snapshots.shape[0] * space_count
    shrink = 2.0 ** -max(0, math.ceil(math.log2(limit / 65000.0)))
    part = jnp.einsum("dr,ds->rs", pod_basis, snapshots, preferred_element_type=jnp.float32)
    part = (part * shrink).astype(jnp.float16)
    part = part.reshape(modes, space_count, depth).transpose(1, 0, 2)
    part = lax.all_to_all(part, "space", 0, 0, tiled=False)
    mine = jnp.sum(part.astype(jnp.float32), axis=0).astype(jnp.float16)[None]
    order = [0]
    bit = space_count // 2
    while bit:
        mine = jnp.concatenate([mine, swap(mine, "space", bit)], axis=0)
        order = order + [o ^ bit for o in order]
        bit //= 2
    own = mine.astype(jnp.float32)
    energy = lax.psum(jnp.sum(own * own, axis=(0, 2)), "tm") / (snaps * shrink * shrink)
    inv = (shrink ** -1 / jnp.sqrt(energy + EPS))[:, None]
    where = jnp.concatenate([jnp.stack([t, s]), s ^ jnp.asarray(order, jnp.int32)]).astype(jnp.int32)
    far = swap(mine, "tm", 2)
    x_near = jnp.concatenate([own, swap(mine, "tm", 1).astype(jnp.float32)], axis=0)
    acc = gram_call(plan, where, x_near, u_near, inv)
    x_far = jnp.concatenate([far, swap(far, "tm", 1)], axis=0).astype(jnp.float32)
    acc = gram_call(plan, where, x_far, u_far, inv, acc)
    return finish(where, acc, snaps, row_count, col_count)


def solution(mesh):
    return jax.shard_map(
        shards,
        mesh=mesh,
        in_specs=(P("space", "tm"), P("space", None), P(None, "tm")),
        out_specs=P("tm", "space"),
        check_vma=False,
    )
```

profile of v0, /device:TPU:3, one launch (start us, length us, event | category | flops | bytes accessed | tf_op | source)
XLA Modules:
  0.0 186.3 jit_solution(3217333389259694974)
XLA Ops:
  0.0 0.0 copy-start
  0.0 1.4 collective-permute-start.5
  1.4 0.0 copy-done
  1.4 4.8 %fusion = f16[96,4096]{1,0:T(8,128)(2,1)S(1)} fusion(bf16[1024,96]{0,1:T(8,128)(2,1)S(1)} %copy-done, bf16[1024,4096]{1,0:T(8,128)(2,1)} %param.4), kind=kOutput, calls=%fused_computation.1 | convolution fusion | flops 806092800 | bytes 9371648 | tf_op jit(solution)/shard_map/dr,ds->rs/dot_general | solution.py:267
  6.3 0.0 copy-start.3
  6.3 1.0 copy.12
  7.3 6.4 %all-to-all-start = ((f16[8,96,512]{2,1,0:T(8,128)(2,1)}), f16[8,96,512]{2,1,0:T(8,128)(2,1)S(1)}, u32[]{:S(2)}, u32[]{:S(2)}) async-start(f16[8,96,512]{2,1,0:T(8,128)(2,1)} %bitcast.16), calls=%async_computation | async-start | bytes 1572864 | tf_op jit(solution)/shard_map/all_to_all | solution.py:270
  13.8 9.7 %collective-permute-done.5 = bf16[112,4096]{1,0:T(8,128)(2,1)S(1)} collective-permute-done((bf16[112,4096]{1,0:T(8,128)(2,1)}, bf16[112,4096]{1,0:T(8,128)(2,1)S(1)}, u32[]{:S(2)}, u32[]{:S(2)}) %collective-permute-start.5) | collective-permute-done | bytes 917536 | tf_op jit(solution)/shard_map/ppermute | solution.py:259
  23.4 0.0 copy-done.3
  23.5 1.5 pad_maximum_fusion.2
  25.0 0.0 copy-done.4
  25.0 1.4 collective-permute-start.6
  26.4 6.2 %all-to-all-done = f16[8,96,512]{2,1,0:T(8,128)(2,1)S(1)} async-done(((f16[8,96,512]{2,1,0:T(8,128)(2,1)}), f16[8,96,512]{2,1,0:T(8,128)(2,1)S(1)}, u32[]{:S(2)}, u32[]{:S(2)}) %all-to-all-start) | async-done | bytes 786464 | tf_op jit(solution)/shard_map/all_to_all | solution.py:270
  32.7 0.1 convert_reduce_fusion
  32.8 0.0 copy-start.6
  32.8 0.8 collective-permute-start
  33.6 4.2 %collective-permute-done = f16[1,96,512]{2,1,0:T(8,128)(2,1)S(1)} collective-permute-done((f16[1,96,512]{2,1,0:T(8,128)(2,1)S(1)}, f16[1,96,512]{2,1,0:T(8,128)(2,1)S(1)}, u32[]{:S(2)}, u32[]{:S(2)}) %collective-permute-start) | collective-permute-done | bytes 98336 | tf_op jit(solution)/shard_map/ppermute | solution.py:243
  37.9 0.7 collective-permute-start.1
  38.6 4.3 %collective-permute-done.1 = f16[2,96,512]{2,1,0:T(8,128)(2,1)S(1)} collective-permute-done((f16[2,96,512]{2,1,0:T(8,128)(2,1)S(1)}, f16[2,96,512]{2,1,0:T(8,128)(2,1)S(1)}, u32[]{:S(2)}, u32[]{:S(2)}) %collective-permute-start.1) | collective-permute-done | bytes 196640 | tf_op jit(solution)/shard_map/ppermute | solution.py:243
  42.9 0.0 copy-done.6
  42.9 0.1 pad_maximum_fusion.5
  43.0 0.0 copy-done.7
  43.0 5.6 %collective-permute-start.2 = (f16[4,96,512]{2,1,0:T(8,128)(2,1)S(1)}, f16[4,96,512]{2,1,0:T(8,128)(2,1)}, u32[]{:S(2)}, u32[]{:S(2)}) collective-permute-start(f16[4,96,512]{2,1,0:T(8,128)(2,1)S(1)} %pad_maximum_fusion.5), channel_id=1, source_target_pairs={{0,4},{4,0},{8,12},{12,8},{16,20},{20,16},{24,28},{28,24},{1,5},{5... | collective-permute-start | bytes 1179656 | tf_op jit(solution)/shard_map/ppermute | solution.py:243
  48.6 0.0 copy-done.9
  48.6 0.6 pad_add_fusion.w.where_ref
  49.1 7.6 %collective-permute-done.2 = f16[4,96,512]{2,1,0:T(8,128)(2,1)} collective-permute-done((f16[4,96,512]{2,1,0:T(8,128)(2,1)S(1)}, f16[4,96,512]{2,1,0:T(8,128)(2,1)}, u32[]{:S(2)}, u32[]{:S(2)}) %collective-permute-start.2) | collective-permute-done | bytes 393248 | tf_op jit(solution)/shard_map/ppermute | solution.py:243
  56.8 1.4 fusion.1
  58.2 2.0 %collective-permute-start.7 = (f16[8,96,512]{2,1,0:T(8,128)(2,1)S(1)}, f16[8,96,512]{2,1,0:T(8,128)(2,1)}, u32[]{:S(2)}, u32[]{:S(2)}) collective-permute-start(f16[8,96,512]{2,1,0:T(8,128)(2,1)S(1)} %get-tuple-element.6), channel_id=1, source_target_pairs={{0,1},{1,0},{2,3},{3,2},{4,5},{5,4},{6,7},{7,6},{8,9},{9,8},{10,11... | collective-permute-start | bytes 2359304 | tf_op jit(solution)/shard_map/ppermute | solution.py:243
  60.2 1.2 collective-permute-start.3
  61.5 0.3 multiply_reduce_fusion
  61.7 19.0 %psum.7 = f32[96]{0:T(128)S(1)} all-reduce(f32[96]{0:T(128)S(1)} %multiply_reduce_fusion), channel_id=1, replica_groups=mesh['space'=8,'tm'=4] {'tm'}, use_global_device_ids=true, to_apply=%region_2.0 | all-reduce | flops 96 | bytes 768 | tf_op jit(solution)/shard_map/psum | solution.py:279
  80.8 0.7 copy.9.c.inv_ref
  81.5 0.0 collective-permute-done.6
  81.5 1.6 fusion.2
  83.1 0.0 collective-permute-done.3
  83.1 2.2 %collective-permute-start.4 = (f16[8,96,512]{2,1,0:T(8,128)(2,1)}, f16[8,96,512]{2,1,0:T(8,128)(2,1)S(1)}, u32[]{:S(2)}, u32[]{:S(2)}) collective-permute-start(f16[8,96,512]{2,1,0:T(8,128)(2,1)} %collective-permute-done.3), channel_id=1, source_target_pairs={{0,1},{1,0},{2,3},{3,2},{4,5},{5,4},{6,7},{7,6},{8,9},{9,8},{10,11... | collective-permute-start | bytes 2359304 | tf_op jit(solution)/shard_map/ppermute | solution.py:243
  85.3 1.5 pad_maximum_fusion.1.b
  86.8 0.0 copy-done.5
  86.8 1.4 pad_maximum_fusion.3.u_in
  88.2 0.0 collective-permute-done.7
  88.2 1.3 convert_element_type.34
  89.5 2.2 %pad_maximum_fusion.a = f32[16,96,512]{2,1,0:T(8,128)} fusion(f32[8,96,512]{2,1,0:T(8,128)S(1)} %convert_element_type.34, f32[8,96,512]{2,1,0:T(8,128)S(1)} %get-tuple-element.5), kind=kLoop, calls=%fused_computation.2 | loop fusion | flops 786432 | bytes 6291456 | tf_op jit(solution)/shard_map/concatenate | solution.py:283
  91.7 34.0 %gram.2.acc_in = f32[1344,768]{1,0:T(8,128)} custom-call(s32[10]{0:T(128)} %pad_add_fusion.w.where_ref, f32[16,96,512]{2,1,0:T(8,128)} %pad_maximum_fusion.a, bf16[2,112,4096]{2,1,0:T(8,128)(2,1)} %pad_maximum_fusion.1.b, f32[96,1]{1,0:T(8,128)} %copy.9.c.inv_ref), custom_call_target="tpu_custom_call" | custom-call | tf_op jit(solution)/shard_map/gram/pallas_call | solution.py:156
  125.8 0.0 collective-permute-done.4
  125.8 3.3 %maximum_convert_fusion.x_in = f32[16,96,512]{2,1,0:T(8,128)} fusion(f16[8,96,512]{2,1,0:T(8,128)(2,1)S(1)} %collective-permute-done.4, f16[8,96,512]{2,1,0:T(8,128)(2,1)} %collective-permute-done.3), kind=kLoop, calls=%fused_computation.6 | loop fusion | flops 1572864 | bytes 4718592 | tf_op jit(solution)/shard_map/convert_element_type | solution.py:285
  129.0 35.6 %gram.3.acc_ref = f32[1344,768]{1,0:T(8,128)} custom-call(s32[10]{0:T(128)} %pad_add_fusion.w.where_ref, f32[16,96,512]{2,1,0:T(8,128)} %maximum_convert_fusion.x_in, bf16[2,112,4096]{2,1,0:T(8,128)(2,1)} %pad_maximum_fusion.3.u_in, f32[96,1]{1,0:T(8,128)} %copy.9.c.inv_ref, f32[1344,768]{1,0:T(8,128)} %gram.2.acc_in), custom_call_target="tpu_custom_call" | custom-call | tf_op jit(solution)/shard_map/gram/pallas_call | solution.py:156
  164.6 2.2 %copy-done.1 = f32[1344,768]{1,0:T(8,128)S(1)} copy-done((f32[1344,768]{1,0:T(8,128)S(1)}, f32[1344,768]{1,0:T(8,128)}, u32[]{:S(2)}) %copy-start.1) | copy-done | bytes 4128792
  166.8 19.5 %finish.1 = f32[1216,608]{1,0:T(8,128)} custom-call(s32[10]{0:T(128)S(1)} %copy-done.2, f32[1344,768]{1,0:T(8,128)S(1)} %copy-done.1), custom_call_target="tpu_custom_call" | custom-call | tf_op jit(solution)/shard_map/finish/pallas_call | solution.py:232
  (13 shorter events, 0.1 us)
Async XLA Ops:
  0.0 1.4 copy-start
  0.0 23.4 %collective-permute-start.5 = (bf16[112,4096]{1,0:T(8,128)(2,1)}, bf16[112,4096]{1,0:T(8,128)(2,1)S(1)}, u32[]{:S(2)}, u32[]{:S(2)}) collective-permute-start(bf16[112,4096]{1,0:T(8,128)(2,1)} %param.6), channel_id=1, source_target_pairs={{0,2},{1,3},{4,6},{5,7},{8,10},{9,11},{12,14},{13,15},{16,18},{17,... | collective-permute-start | bytes 2752520 | tf_op jit(solution)/shard_map/ppermute | solution.py:259
  6.3 17.2 %copy-start.3 = (bf16[112,4096]{1,0:T(8,128)(2,1)S(1)}, bf16[112,4096]{1,0:T(8,128)(2,1)}, u32[]{:S(2)}) copy-start(bf16[112,4096]{1,0:T(8,128)(2,1)} %param.6) | copy-start | bytes 2752516
  7.3 25.3 %all-to-all-start = ((f16[8,96,512]{2,1,0:T(8,128)(2,1)}), f16[8,96,512]{2,1,0:T(8,128)(2,1)S(1)}, u32[]{:S(2)}, u32[]{:S(2)}) async-start(f16[8,96,512]{2,1,0:T(8,128)(2,1)} %bitcast.16), calls=%async_computation | async-start | bytes 1572864 | tf_op jit(solution)/shard_map/all_to_all | solution.py:270
  23.4 1.5 copy-start.4
  25.0 23.6 %copy-start.9 = (s32[8]{0:T(128)S(1)}, s32[8]{0:T(128)}, u32[]{:S(2)}) copy-start(s32[8]{0:T(128)} %constant.22.clone) | copy-start | bytes 100
  25.0 56.5 %collective-permute-start.6 = (bf16[2,112,4096]{2,1,0:T(8,128)(2,1)}, bf16[2,112,4096]{2,1,0:T(8,128)(2,1)}, u32[]{:S(2)}, u32[]{:S(2)}) collective-permute-start(bf16[2,112,4096]{2,1,0:T(8,128)(2,1)} %pad_maximum_fusion.2), channel_id=1, source_target_pairs={{2,3},{6,7},{10,11},{14,15},{18,19},{22,23},{26,27},{28,29},{29,28... | collective-permute-start | bytes 5505032 | tf_op jit(solution)/shard_map/ppermute | solution.py:261
  32.8 10.1 %copy-start.6 = (f16[1,96,512]{2,1,0:T(8,128)(2,1)}, f16[1,96,512]{2,1,0:T(8,128)(2,1)S(1)}, u32[]{:S(2)}) copy-start(f16[1,96,512]{2,1,0:T(8,128)(2,1)S(1)} %convert_bitcast_fusion) | copy-start | bytes 294916
  32.8 5.1 %collective-permute-start = (f16[1,96,512]{2,1,0:T(8,128)(2,1)S(1)}, f16[1,96,512]{2,1,0:T(8,128)(2,1)S(1)}, u32[]{:S(2)}, u32[]{:S(2)}) collective-permute-start(f16[1,96,512]{2,1,0:T(8,128)(2,1)S(1)} %convert_bitcast_fusion), channel_id=1, source_target_pairs={{0,16},{4,20},{8,24},{12,28},{16,0},{20,4},{24,8},{28,12},{1,17},{... | collective-permute-start | bytes 294920 | tf_op jit(solution)/shard_map/ppermute | solution.py:243
  37.9 5.1 %copy-start.7 = (f16[1,96,512]{2,1,0:T(8,128)(2,1)}, f16[1,96,512]{2,1,0:T(8,128)(2,1)S(1)}, u32[]{:S(2)}) copy-start(f16[1,96,512]{2,1,0:T(8,128)(2,1)S(1)} %collective-permute-done) | copy-start | bytes 294916
  37.9 5.0 %collective-permute-start.1 = (f16[2,96,512]{2,1,0:T(8,128)(2,1)S(1)}, f16[2,96,512]{2,1,0:T(8,128)(2,1)S(1)}, u32[]{:S(2)}, u32[]{:S(2)}) collective-permute-start(f16[2,96,512]{2,1,0:T(8,128)(2,1)S(1)} %pad_maximum_fusion.6), channel_id=1, source_target_pairs={{0,8},{4,12},{8,0},{12,4},{16,24},{20,28},{24,16},{28,20},{1,9},{5... | collective-permute-start | bytes 589832 | tf_op jit(solution)/shard_map/ppermute | solution.py:243
  42.9 5.7 %copy-start.8 = (f16[2,96,512]{2,1,0:T(8,128)(2,1)}, f16[2,96,512]{2,1,0:T(8,128)(2,1)S(1)}, u32[]{:S(2)}) copy-start(f16[2,96,512]{2,1,0:T(8,128)(2,1)S(1)} %collective-permute-done.1) | copy-start | bytes 589828
  43.0 13.8 %collective-permute-start.2 = (f16[4,96,512]{2,1,0:T(8,128)(2,1)S(1)}, f16[4,96,512]{2,1,0:T(8,128)(2,1)}, u32[]{:S(2)}, u32[]{:S(2)}) collective-permute-start(f16[4,96,512]{2,1,0:T(8,128)(2,1)S(1)} %pad_maximum_fusion.5), channel_id=1, source_target_pairs={{0,4},{4,0},{8,12},{12,8},{16,20},{20,16},{24,28},{28,24},{1,5},{5... | collective-permute-start | bytes 1179656 | tf_op jit(solution)/shard_map/ppermute | solution.py:243
  58.2 30.0 %collective-permute-start.7 = (f16[8,96,512]{2,1,0:T(8,128)(2,1)S(1)}, f16[8,96,512]{2,1,0:T(8,128)(2,1)}, u32[]{:S(2)}, u32[]{:S(2)}) collective-permute-start(f16[8,96,512]{2,1,0:T(8,128)(2,1)S(1)} %get-tuple-element.6), channel_id=1, source_target_pairs={{0,1},{1,0},{2,3},{3,2},{4,5},{5,4},{6,7},{7,6},{8,9},{9,8},{10,11... | collective-permute-start | bytes 2359304 | tf_op jit(solution)/shard_map/ppermute | solution.py:243
  60.2 22.9 %collective-permute-start.3 = (f16[8,96,512]{2,1,0:T(8,128)(2,1)S(1)}, f16[8,96,512]{2,1,0:T(8,128)(2,1)}, u32[]{:S(2)}, u32[]{:S(2)}) collective-permute-start(f16[8,96,512]{2,1,0:T(8,128)(2,1)S(1)} %get-tuple-element.6), channel_id=1, source_target_pairs={{0,2},{1,3},{2,0},{3,1},{4,6},{5,7},{6,4},{7,5},{8,10},{9,11},{10,... | collective-permute-start | bytes 2359304 | tf_op jit(solution)/shard_map/ppermute | solution.py:243
  83.1 42.6 %collective-permute-start.4 = (f16[8,96,512]{2,1,0:T(8,128)(2,1)}, f16[8,96,512]{2,1,0:T(8,128)(2,1)S(1)}, u32[]{:S(2)}, u32[]{:S(2)}) collective-permute-start(f16[8,96,512]{2,1,0:T(8,128)(2,1)} %collective-permute-done.3), channel_id=1, source_target_pairs={{0,1},{1,0},{2,3},{3,2},{4,5},{5,4},{6,7},{7,6},{8,9},{9,8},{10,11... | collective-permute-start | bytes 2359304 | tf_op jit(solution)/shard_map/ppermute | solution.py:243
  85.3 1.5 copy-start.5
  129.0 35.6 %copy-start.2 = (s32[10]{0:T(128)S(1)}, s32[10]{0:T(128)}, u32[]{:S(2)}) copy-start(s32[10]{0:T(128)} %pad_add_fusion.w.where_ref) | copy-start | bytes 124
  164.6 2.2 %copy-start.1 = (f32[1344,768]{1,0:T(8,128)S(1)}, f32[1344,768]{1,0:T(8,128)}, u32[]{:S(2)}) copy-start(f32[1344,768]{1,0:T(8,128)} %gram.3.acc_ref) | copy-start | bytes 12386308
where the time goes:
time: 187 us; the launch traced here: 186 us
  Pallas kernels  89.1 us (48%)
  waiting for transfers between devices  32.1 us (17%)
  starting transfers between devices  21.8 us (12%)
  blocking collectives  19 us (10%)
  other arithmetic  13.7 us (7%)
  local copies, waits for them, and re-layouts  5.61 us (3%)
  matrix products  4.85 us (3%)
    pallas_call x2, Pallas kernels, gram_call(): pl.pallas_call(inner, grid_spec=pltpu.PrefetchScalarGridSpec(num_scalar_p...  69.6 us
    pallas_call x1, Pallas kernels, finish(): pl.pallas_call(functools.partial(finish_kernel, snaps, row_count, col_cou...  19.5 us
    psum x1, blocking collectives, shards(): lax.psum(jnp.sum(own * own, axis=(0, 2)), 'tm') / (snaps * shrink * shrink)  19 us
    ppermute x6, waiting for transfers between devices, swap(): lax.ppermute(x, axis, [(i, i ^ bit) for i in range(lax.axis_size(axis))])  16.2 us
    ppermute x6, starting transfers between devices, swap(): lax.ppermute(x, axis, [(i, i ^ bit) for i in range(lax.axis_size(axis))])  12.5 us
    ppermute x1, waiting for transfers between devices, shards(): u_far = lax.ppermute(inputs, ('space', 'tm'), pairs)  9.68 us
    all_to_all x1, starting transfers between devices, shards(): part = lax.all_to_all(part, 'space', 0, 0, tiled=False)  6.43 us
    all_to_all x1, waiting for transfers between devices, shards(): part = lax.all_to_all(part, 'space', 0, 0, tiled=False)  6.25 us
  transfers between devices with their start and end apart: 9, of which 5 were waited for; matrix products, arithmetic and copies ran while one was open for 10% of the time, Pallas kernels for 18%

commit v1 on v0

v1 whole, which is shorter than its diff:
```python
import functools
import math

import jax
import jax.numpy as jnp
import numpy as np
from jax import lax
from jax.experimental import pallas as pl
from jax.experimental.pallas import tpu as pltpu
from jax.sharding import PartitionSpec as P

NB = 128
EPS = 1e-06
REG = 0.5
PAD = 8
LANES = 128


def feature_pairs(modes, count):
    first, second = np.triu_indices(modes)
    lead = [(f, None) for f in range(modes)]
    pairs = list(zip(first.tolist(), second.tolist()))
    tail = [(modes + k, None) for k in range(count)]
    return lead + pairs + tail


def runs_of(rows):
    runs = []
    for at, row in enumerate(rows):
        if row is None:
            continue
        a, b = row
        key = ("one", a - at) if b is None else (a, b - at)
        if runs and runs[-1][2] == key and runs[-1][1] == at:
            runs[-1][1] = at + 1
        else:
            runs.append([at, at + 1, key])
    return runs


def build_rows(x_ref, f_ref, lane, rows, base):
    sub = lax.broadcasted_iota(jnp.int32, (8, LANES), 0)
    cache = {}

    def row_of(a):
        if a not in cache:
            cache.clear()
            cache[a] = jnp.broadcast_to(x_ref[lane, PAD + a : PAD + a + 1, :], (8, LANES))
        return cache[a]

    def eight(at):
        chunk = rows[at : at + 8]
        chunk = chunk + [None] * (8 - len(chunk))
        total = None
        for lo, hi, (a, shift) in runs_of(chunk):
            part = x_ref[lane, PAD + shift : PAD + shift + 8, :]
            if a != "one":
                part = part * row_of(a)
            if total is None and lo == 0:
                total = part
            else:
                if total is None:
                    total = jnp.zeros((8, LANES), jnp.float32)
                total = jnp.where(sub >= lo, part, total)
            last = hi
        if total is None:
            return jnp.zeros((8, LANES), jnp.float32)
        if last < 8:
            total = jnp.where(sub < last, total, 0.0)
        return total

    for at in range(0, len(rows), 16):
        value = jnp.concatenate([eight(at), eight(at + 8)], axis=0).astype(jnp.bfloat16)
        f_ref[base + at : base + at + 16, pl.ds(pl.multiple_of(lane * LANES, LANES), LANES)] = value


def gram_kernel(plan, snaps, closing, where_ref, own_ref, near_ref, u_own, u_near, inv_ref, *refs):
    modes, row_sets, col_sets, head_set, row_count, a_rows, b_rows = plan
    if closing:
        acc_in, out_ref, acc_ref, prior_ref, sem, x_ref, f_ref = refs
    else:
        acc_ref, x_ref, f_ref = refs
    step, steps = pl.program_id(0), pl.num_programs(0)
    slots, _, slot_depth = own_ref.shape
    per = slot_depth // LANES
    lanes = slots * per
    inputs = u_own.shape[0]

    @pl.when(step == 0)
    def _():
        if closing:
            pltpu.make_async_copy(acc_in, prior_ref, sem).start()
        f_ref[...] = jnp.zeros_like(f_ref)
        x_ref[...] = jnp.zeros_like(x_ref)
        acc_ref[...] = jnp.zeros_like(acc_ref)

    scale = inv_ref[...]

    def prepare(x_in, u_in, first_slot):
        for slot in range(slots):
            source = where_ref[2 + first_slot + slot] * slot_depth
            for lane in range(per):
                at = slice(lane * LANES, (lane + 1) * LANES)
                x_ref[slot * per + lane, PAD : PAD + modes, :] = x_in[slot, :, at] * scale
                u_at = pl.ds(pl.multiple_of(source + lane * LANES, LANES), LANES)
                x_ref[slot * per + lane, PAD + modes : PAD + modes + inputs, :] = u_in[:, u_at].astype(jnp.float32)

    half = steps // 2
    pl.when(step < half)(lambda: prepare(own_ref, u_own, step * slots))
    pl.when(step >= half)(lambda: prepare(near_ref, u_near, (step - half) * slots))

    def build(rows, base):
        @pl.loop(0, lanes)
        def _(lane):
            build_rows(x_ref, f_ref, lane, rows, base)

    for number, rows in enumerate(row_sets):
        pl.when(where_ref[0] == number)(lambda rows=rows: build(rows, 0))
    build(head_set, row_count)
    for number, rows in enumerate(col_sets):
        pl.when(where_ref[1] == number)(lambda rows=rows: build(rows, a_rows))

    left = f_ref[0:a_rows, :]
    for at in range(0, b_rows, 256):
        wide = min(256, b_rows - at)
        right = f_ref[row_count + at : row_count + at + wide, :]
        acc_ref[:, at : at + wide] += lax.dot_general(
            left, right, (((1,), (1,)), ((), ())), preferred_element_type=jnp.float32
        )

    if closing:
        @pl.when(step == steps - 1)
        def _():
            pltpu.make_async_copy(acc_in, prior_ref, sem).wait()
            finish(snaps, row_count, len(col_sets[0]), where_ref, acc_ref, prior_ref, out_ref)


def make_plan(modes, count, time_count, space_count):
    pairs = feature_pairs(modes, count)
    total = len(pairs)
    row_count, col_count = total // time_count, total // space_count
    row_sets = [pairs[t * row_count : (t + 1) * row_count] for t in range(time_count)]
    col_sets = [pairs[s * col_count : (s + 1) * col_count] for s in range(space_count)]
    a_rows = row_count + NB
    b_rows = -(-(NB + col_count) // 128) * 128
    return modes, row_sets, col_sets, pairs[:NB], row_count, a_rows, b_rows


def gram_call(plan, snaps, where, own, near, u_own, u_near, inv, acc=None, depth=2048):
    modes, _, col_sets, _, row_count, a_rows, b_rows = plan
    total, _, slot_depth = own.shape
    inputs = u_own.shape[0]
    slots = depth // slot_depth
    half = total // slots
    lanes = depth // LANES
    closing = acc is not None
    whole = lambda shape: pl.BlockSpec(shape, lambda k, w: (0,) * len(shape))
    block = (slots, modes, slot_depth)
    in_specs = [
        pl.BlockSpec(block, lambda k, w: (jnp.minimum(k, half - 1), 0, 0)),
        pl.BlockSpec(block, lambda k, w: (jnp.maximum(k - half, 0), 0, 0)),
        whole(u_own.shape),
        whole(u_near.shape),
        whole((modes, 1)),
    ]
    args = [own, near, u_own, u_near, inv]
    acc_shape = (a_rows, b_rows)
    scratch = [
        pltpu.VMEM((lanes, PAD + modes + inputs + 8, LANES), jnp.float32),
        pltpu.VMEM((-(-(row_count + b_rows) // 16) * 16, depth), jnp.bfloat16),
    ]
    out_shape = acc_shape
    if closing:
        in_specs.append(pl.BlockSpec(memory_space=pl.ANY))
        args.append(acc)
        scratch = [pltpu.VMEM(acc_shape, jnp.float32)] * 2 + [pltpu.SemaphoreType.DMA] + scratch
        out_shape = (row_count, len(col_sets[0]))
    flops = 2 * a_rows * b_rows * 2 * total * slot_depth
    return pl.pallas_call(
        functools.partial(gram_kernel, plan, snaps, closing),
        grid_spec=pltpu.PrefetchScalarGridSpec(
            num_scalar_prefetch=1,
            grid=(2 * half,),
            in_specs=in_specs,
            out_specs=whole(out_shape),
            scratch_shapes=scratch,
        ),
        out_shape=jax.ShapeDtypeStruct(out_shape, jnp.float32),
        compiler_params=pltpu.CompilerParams(
            vmem_limit_bytes=56 * 1024 * 1024, dimension_semantics=("arbitrary",)
        ),
        cost_estimate=pl.CostEstimate(flops=2 * flops, bytes_accessed=20_000_000, transcendentals=0),
        name="close" if closing else "gram",
    )(where, *args)


def inverse_factor(corner):
    sub = lax.broadcasted_iota(jnp.int32, (8, 2 * NB), 0)
    row_ids = lax.broadcasted_iota(jnp.int32, (NB, NB), 0)
    col_ids = lax.broadcasted_iota(jnp.int32, (NB, NB), 1)
    eye = (row_ids == col_ids).astype(jnp.float32)
    joined = jnp.concatenate([corner, eye], axis=1)
    tiles = [joined[at : at + 8] for at in range(0, NB, 8)]
    for k in range(NB):
        q, r = divmod(k, 8)
        row = tiles[q][r : r + 1]
        row = row * (1.0 / row[:, k : k + 1])
        for p in range(q, NB // 8):
            column = tiles[p][:, k : k + 1]
            change = column * row
            if p == q:
                change = jnp.where(sub > r, change, 0.0)
            tiles[p] = tiles[p] - change
    done = jnp.concatenate(tiles, axis=0)
    pivots = jnp.sum(done[:, :NB] * eye, axis=1, keepdims=True)
    return done[:, NB:] * lax.rsqrt(pivots)


def dot32(a, b, dims):
    return lax.dot_general(
        a, b, (dims, ((), ())), precision=lax.Precision.HIGHEST, preferred_element_type=jnp.float32
    )


def finish(snaps, row_count, col_count, where_ref, acc_ref, prior_ref, out_ref):
    t, s = where_ref[0], where_ref[1]
    head = slice(row_count, row_count + NB)

    def gram_part(rows, cols, row_start, col_start):
        value = (acc_ref[rows, cols] + prior_ref[rows, cols]) * (1.0 / snaps)
        row_ids = row_start + lax.broadcasted_iota(jnp.int32, value.shape, 0)
        col_ids = col_start + lax.broadcasted_iota(jnp.int32, value.shape, 1)
        return value + REG * (row_ids == col_ids).astype(jnp.float32), row_ids

    own = slice(NB, NB + col_count)
    inverse = inverse_factor(gram_part(head, slice(0, NB), 0, 0)[0])
    cols_factor = dot32(inverse, gram_part(head, own, 0, s * col_count)[0], ((1,), (0,)))
    for at in range(0, row_count, NB):
        rows = slice(at, min(at + NB, row_count))
        factor = dot32(gram_part(rows, slice(0, NB), t * row_count + at, 0)[0], inverse, ((1,), (1,)))
        value, row_ids = gram_part(rows, own, t * row_count + at, s * col_count)
        value = value - dot32(factor, cols_factor, ((1,), (0,)))
        value = jnp.where(row_ids < NB, 0.0, value)
        out_ref[rows, NB:col_count] = value[:, NB:]
        out_ref[rows, 0:NB] = jnp.where(s == 0, factor, value[:, :NB])


def swap(x, axis, bit):
    return lax.ppermute(x, axis, [(i, i ^ bit) for i in range(lax.axis_size(axis))])


def shards(snapshots, pod_basis, inputs):
    modes = pod_basis.shape[1]
    space_count, time_count = lax.axis_size("space"), lax.axis_size("tm")
    t, s = lax.axis_index("tm"), lax.axis_index("space")
    local = snapshots.shape[1]
    snaps = local * time_count
    depth = local // space_count
    plan = make_plan(modes, inputs.shape[0], time_count, space_count)

    def some(x, bit, wanted):
        pairs = [
            (a * time_count + b, a * time_count + (b ^ bit))
            for a in range(space_count)
            for b in range(time_count)
            if a == space_count - 1 or b in wanted
        ]
        return lax.ppermute(x, ("space", "tm"), pairs)

    u_near = some(inputs, 1, (2,))
    u_far = some(inputs, 2, (0, 1))
    u_far_near = some(u_far, 1, (2,))

    limit = 1200.0 * 0.0625 * snapshots.shape[0] * space_count
    shrink = 2.0 ** -max(0, math.ceil(math.log2(limit / 65000.0)))
    part = jnp.einsum("dr,ds->rs", pod_basis, snapshots, preferred_element_type=jnp.float32)
    part = (part * shrink).astype(jnp.float16)
    part = part.reshape(modes, space_count, depth).transpose(1, 0, 2)
    part = lax.all_to_all(part, "space", 0, 0, tiled=False)
    mine = jnp.sum(part.astype(jnp.float32), axis=0).astype(jnp.float16)[None]
    order = [0]
    bit = space_count // 2
    while bit:
        if bit == 1:
            wide = mine.astype(jnp.float32)
            energy = jnp.sum(wide * wide, axis=(0, 2))
            for axis, step in (("space", 1), ("tm", 1), ("tm", 2)):
                energy = energy + swap(energy, axis, step)
        mine = jnp.concatenate([mine, swap(mine, "space", bit)], axis=0)
        order = order + [o ^ bit for o in order]
        bit //= 2
    mine, energy = lax.optimization_barrier((mine, energy))
    inv = (shrink ** -1 / jnp.sqrt(energy / (snaps * shrink * shrink) + EPS))[:, None]
    where = jnp.concatenate([jnp.stack([t, s]), s ^ jnp.asarray(order, jnp.int32)]).astype(jnp.int32)
    far = swap(mine, "tm", 2)
    near = swap(mine, "tm", 1)
    acc = gram_call(plan, snaps, where, mine.astype(jnp.float32), near.astype(jnp.float32), inputs, u_near, inv)
    far_near = swap(far, "tm", 1)
    return gram_call(
        plan, snaps, where, far.astype(jnp.float32), far_near.astype(jnp.float32), u_far, u_far_near, inv, acc
    )


def solution(mesh):
    return jax.shard_map(
        shards,
        mesh=mesh,
        in_specs=(P("space", "tm"), P("space", None), P(None, "tm")),
        out_specs=P("tm", "space"),
        check_vma=False,
    )
```

time: 187 us -> 176 us (0.941)
  other arithmetic: 13.7 us -> 6.75 us
  blocking collectives: 19 us -> 24.7 us
  local copies, waits for them, and re-layouts: 5.61 us -> 1.84 us
  Pallas kernels: 89.1 us -> 85.6 us
  starting transfers between devices: 21.8 us -> 19.1 us
    all_to_all x0 -> x1, blocking collectives: none -> 24.7 us  [shards(): part = lax.all_to_all(part, 'space', 0, 0, tiled=False)]
    psum x1 -> x0, blocking collectives: 19 us -> none  [shards(): lax.psum(jnp.sum(own * own, axis=(0, 2)), 'tm') / (snaps * shrink * shrink)]
    ppermute x6 -> x9, waiting for transfers between devices: 16.2 us -> 32.4 us  [swap(): lax.ppermute(x, axis, [(i, i ^ bit) for i in range(lax.axis_size(axis))])]
    ppermute x2 -> x3, waiting for transfers between devices: 9.68 us -> 0.01 us  [some(): return lax.ppermute(x, ('space', 'tm'), pairs)]
    all_to_all x1 -> x0, starting transfers between devices: 6.43 us -> none  [shards(): part = lax.all_to_all(part, 'space', 0, 0, tiled=False)]
    all_to_all x1 -> x0, waiting for transfers between devices: 6.25 us -> none  [shards(): part = lax.all_to_all(part, 'space', 0, 0, tiled=False)]
    another operation x3 -> x0, other arithmetic: 4.37 us -> none  [the longest x1 1.53 us: shards(): u_pair = lax.ppermute(jnp.stack([inputs, u_far]), ('space', 'tm'), pairs)]
    pallas_call x3 -> x2, Pallas kernels: 89.1 us -> 85.6 us  [gram_call(): pl.pallas_call(functools.partial(gram_kernel, plan, snaps, closing), grid...]
  transfers between devices with their start and end apart: 9 -> 12, of which waited for: 5 -> 6; matrix products, arithmetic and copies ran while one was open for 10% -> 4% of each run, Pallas kernels for 18% -> 19%
where the time goes in v1:
time: 176 us; the launch traced here: 175 us
  Pallas kernels  85.6 us (49%)
  waiting for transfers between devices  32.4 us (18%)
  blocking collectives  24.7 us (14%)
  starting transfers between devices  19.1 us (11%)
  other arithmetic  6.75 us (4%)
  matrix products  4.84 us (3%)
  local copies, waits for them, and re-layouts  1.84 us (1%)
    pallas_call x2, Pallas kernels, gram_call(): pl.pallas_call(functools.partial(gram_kernel, plan, snaps, closing), grid...  85.6 us
    ppermute x9, waiting for transfers between devices, swap(): lax.ppermute(x, axis, [(i, i ^ bit) for i in range(lax.axis_size(axis))])  32.4 us
    all_to_all x1, blocking collectives, shards(): part = lax.all_to_all(part, 'space', 0, 0, tiled=False)  24.7 us
    ppermute x9, starting transfers between devices, swap(): lax.ppermute(x, axis, [(i, i ^ bit) for i in range(lax.axis_size(axis))])  15.3 us
    dot_general x1, matrix products, shards(): jnp.einsum('dr,ds->rs', pod_basis, snapshots, preferred_element_type=jnp....  4.84 us
    ppermute x3, starting transfers between devices, some(): return lax.ppermute(x, ('space', 'tm'), pairs)  3.84 us
  transfers between devices with their start and end apart: 12, of which 6 were waited for; matrix products, arithmetic and copies ran while one was open for 4% of the time, Pallas kernels for 19%

profile of v1, /device:TPU:3, one launch (start us, length us, event | category | flops | bytes accessed | tf_op | source)
XLA Modules:
  0.0 175.5 jit_solution(15027632656000308162)
XLA Ops:
  0.0 0.0 copy-start
  0.0 0.9 copy-done
  0.9 4.8 %fusion = f16[96,4096]{1,0:T(8,128)(2,1)S(1)} fusion(bf16[1024,96]{0,1:T(8,128)(2,1)S(1)} %copy-done, bf16[1024,4096]{1,0:T(8,128)(2,1)} %param.4), kind=kOutput, calls=%fused_computation.1 | convolution fusion | flops 806092800 | bytes 9371648 | tf_op jit(solution)/shard_map/dr,ds->rs/dot_general | solution.py:276
  5.8 0.2 copy.12
  5.9 24.7 %all_to_all.5 = f16[8,96,512]{2,1,0:T(8,128)(2,1)S(1)} all-to-all(f16[8,96,512]{2,1,0:T(8,128)(2,1)S(1)} %bitcast.16), channel_id=1, replica_groups=mesh['space'=8,'tm'=4] {'space'}, dimensions={0} | all-to-all | bytes 1572864 | tf_op jit(solution)/shard_map/all_to_all | solution.py:279
  30.6 0.0 copy-start.1
  30.6 0.1 convert_reduce_fusion
  30.7 0.0 copy-start.2
  30.7 1.2 collective-permute-start
  31.9 4.3 %collective-permute-done = f16[1,96,512]{2,1,0:T(8,128)(2,1)S(1)} collective-permute-done((f16[1,96,512]{2,1,0:T(8,128)(2,1)S(1)}, f16[1,96,512]{2,1,0:T(8,128)(2,1)S(1)}, u32[]{:S(2)}, u32[]{:S(2)}) %collective-permute-start) | collective-permute-done | bytes 98336 | tf_op jit(solution)/shard_map/ppermute | solution.py:249
  36.3 0.1 collective-permute-start.1
  36.4 4.5 %collective-permute-done.1 = f16[2,96,512]{2,1,0:T(8,128)(2,1)S(1)} collective-permute-done((f16[2,96,512]{2,1,0:T(8,128)(2,1)S(1)}, f16[2,96,512]{2,1,0:T(8,128)(2,1)S(1)}, u32[]{:S(2)}, u32[]{:S(2)}) %collective-permute-start.1) | collective-permute-done | bytes 196640 | tf_op jit(solution)/shard_map/ppermute | solution.py:249
  40.9 0.2 multiply_reduce_fusion
  41.1 0.8 collective-permute-start.2
  41.9 0.0 copy-done.1
  41.9 1.3 collective-permute-start.8
  43.2 0.8 collective-permute-start.3
  44.0 3.9 %collective-permute-done.3 = f32[96]{0:T(128)S(1)} collective-permute-done((f32[96]{0:T(128)S(1)}, f32[96]{0:T(128)S(1)}, u32[]{:S(2)}, u32[]{:S(2)}) %collective-permute-start.3) | collective-permute-done | bytes 416 | tf_op jit(solution)/shard_map/ppermute | solution.py:249
  47.9 5.3 %collective-permute-start.4 = (f32[96]{0:T(128)S(1)}, f32[96]{0:T(128)S(1)}, u32[]{:S(2)}, u32[]{:S(2)}) collective-permute-start(f32[96]{0:T(128)S(1)} %add.15), channel_id=1, source_target_pairs={{0,1},{1,0},{2,3},{3,2},{4,5},{5,4},{6,7},{7,6},{8,9},{9,8},{10,11... | collective-permute-start | bytes 1160 | tf_op jit(solution)/shard_map/ppermute | solution.py:249
  53.1 0.8 collective-permute-done.4
  53.9 1.1 collective-permute-start.5
  55.1 1.3 collective-permute-start.11
  56.4 5.2 %collective-permute-done.5 = f32[96]{0:T(128)S(1)} collective-permute-done((f32[96]{0:T(128)S(1)}, f32[96]{0:T(128)S(1)}, u32[]{:S(2)}, u32[]{:S(2)}) %collective-permute-start.5) | collective-permute-done | bytes 416 | tf_op jit(solution)/shard_map/ppermute | solution.py:249
  61.5 0.0 collective-permute-done.2
  61.5 0.2 pad_maximum_fusion
  61.8 5.2 %collective-permute-start.10 = (f16[8,96,512]{2,1,0:T(8,128)(2,1)S(1)}, f16[8,96,512]{2,1,0:T(8,128)(2,1)S(1)}, u32[]{:S(2)}, u32[]{:S(2)}) collective-permute-start(f16[8,96,512]{2,1,0:T(8,128)(2,1)S(1)} %pad_maximum_fusion), channel_id=1, source_target_pairs={{0,1},{1,0},{2,3},{3,2},{4,5},{5,4},{6,7},{7,6},{8,9},{9,8},{10,11... | collective-permute-start | bytes 2359304 | tf_op jit(solution)/shard_map/ppermute | solution.py:249
  67.0 0.0 collective-permute-start.6
  67.0 0.0 copy-done.2
  67.0 0.6 pad_add_fusion.where_ref
  67.6 0.0 collective-permute-done.8.u_own
  67.6 1.3 collective-permute-start.9
  68.9 1.4 convert_element_type.41.own_ref
  70.2 0.7 copy.9.inv_ref
  71.0 0.0 collective-permute-done.10
  71.0 1.4 convert_element_type.42.near_ref
  72.4 13.7 %collective-permute-done.6 = f16[8,96,512]{2,1,0:T(8,128)(2,1)S(1)} collective-permute-done((f16[8,96,512]{2,1,0:T(8,128)(2,1)S(1)}, f16[8,96,512]{2,1,0:T(8,128)(2,1)S(1)}, u32[]{:S(2)}, u32[]{:S(2)}) %collective-permute-start.6) | collective-permute-done | bytes 786464 | tf_op jit(solution)/shard_map/ppermute | solution.py:249
  86.1 0.8 collective-permute-start.7
  87.0 0.0 collective-permute-done.11.u_near
  87.0 34.2 %gram.1.refs_0_ = f32[1344,768]{1,0:T(8,128)} custom-call(s32[10]{0:T(128)} %pad_add_fusion.where_ref, f32[8,96,512]{2,1,0:T(8,128)} %convert_element_type.41.own_ref, f32[8,96,512]{2,1,0:T(8,128)} %convert_element_type.42.near_ref, bf16[112,4096]{1,0:T(8,128)(2,1)} %u_own.1, bf16[112,4096]{1,0:T(8,128)(2,1)} %collective-permute-done.11.u_near, ...), custom_call_target="tpu_custom_call" | custom-call | flops 33822867456 | bytes 20000000 | tf_op jit(solution)/shard_map/gram/pallas_call | solution.py:179
  121.1 1.4 convert_element_type.39.own_ref
  122.5 0.0 collective-permute-done.7
  122.5 1.4 convert_element_type.40.near_ref
  123.9 0.0 collective-permute-done.9.u_near
  123.9 51.4 %close.1 = f32[1216,608]{1,0:T(8,128)} custom-call(s32[10]{0:T(128)} %pad_add_fusion.where_ref, f32[8,96,512]{2,1,0:T(8,128)} %convert_element_type.39.own_ref, f32[8,96,512]{2,1,0:T(8,128)} %convert_element_type.40.near_ref, bf16[112,4096]{1,0:T(8,128)(2,1)} %collective-permute-done.8.u_own, bf16[112,4096]{1,0:T(8,128)(2,1)} %collective-permute-done.9.u_near, ...), custom_call_target="tpu_custom_call" | custom-call | flops 33822867456 | bytes 20000000 | tf_op jit(solution)/shard_map/close/pallas_call | solution.py:179
  (7 shorter events, 0.1 us)
Async XLA Ops:
  0.0 0.9 copy-start
  30.6 11.3 %copy-start.1 = (bf16[112,4096]{1,0:T(8,128)(2,1)S(1)}, bf16[112,4096]{1,0:T(8,128)(2,1)}, u32[]{:S(2)}) copy-start(bf16[112,4096]{1,0:T(8,128)(2,1)} %u_own.1) | copy-start | bytes 2752516
  30.7 36.3 %copy-start.2 = (s32[8]{0:T(128)S(1)}, s32[8]{0:T(128)}, u32[]{:S(2)}) copy-start(s32[8]{0:T(128)} %constant.22.clone) | copy-start | bytes 100
  30.7 5.5 %collective-permute-start = (f16[1,96,512]{2,1,0:T(8,128)(2,1)S(1)}, f16[1,96,512]{2,1,0:T(8,128)(2,1)S(1)}, u32[]{:S(2)}, u32[]{:S(2)}) collective-permute-start(f16[1,96,512]{2,1,0:T(8,128)(2,1)S(1)} %convert_bitcast_fusion), channel_id=1, source_target_pairs={{0,16},{4,20},{8,24},{12,28},{16,0},{20,4},{24,8},{28,12},{1,17},{... | collective-permute-start | bytes 294920 | tf_op jit(solution)/shard_map/ppermute | solution.py:249
  36.3 4.6 %collective-permute-start.1 = (f16[2,96,512]{2,1,0:T(8,128)(2,1)S(1)}, f16[2,96,512]{2,1,0:T(8,128)(2,1)S(1)}, u32[]{:S(2)}, u32[]{:S(2)}) collective-permute-start(f16[2,96,512]{2,1,0:T(8,128)(2,1)S(1)} %pad_maximum_fusion.2), channel_id=1, source_target_pairs={{0,8},{4,12},{8,0},{12,4},{16,24},{20,28},{24,16},{28,20},{1,9},{5... | collective-permute-start | bytes 589832 | tf_op jit(solution)/shard_map/ppermute | solution.py:249
  41.1 20.4 %collective-permute-start.2 = (f16[4,96,512]{2,1,0:T(8,128)(2,1)S(1)}, f16[4,96,512]{2,1,0:T(8,128)(2,1)S(1)}, u32[]{:S(2)}, u32[]{:S(2)}) collective-permute-start(f16[4,96,512]{2,1,0:T(8,128)(2,1)S(1)} %get-tuple-element.10), channel_id=1, source_target_pairs={{0,4},{4,0},{8,12},{12,8},{16,20},{20,16},{24,28},{28,24},{1,5},{5... | collective-permute-start | bytes 1179656 | tf_op jit(solution)/shard_map/ppermute | solution.py:249
  41.9 25.7 %collective-permute-start.8 = (bf16[112,4096]{1,0:T(8,128)(2,1)S(1)}, bf16[112,4096]{1,0:T(8,128)(2,1)}, u32[]{:S(2)}, u32[]{:S(2)}) collective-permute-start(bf16[112,4096]{1,0:T(8,128)(2,1)S(1)} %copy-done.1), channel_id=1, source_target_pairs={{0,2},{1,3},{4,6},{5,7},{8,10},{9,11},{12,14},{13,15},{16,18},{17,... | collective-permute-start | bytes 2752520 | tf_op jit(solution)/shard_map/ppermute | solution.py:268
  43.2 4.6 %collective-permute-start.3 = (f32[96]{0:T(128)S(1)}, f32[96]{0:T(128)S(1)}, u32[]{:S(2)}, u32[]{:S(2)}) collective-permute-start(f32[96]{0:T(128)S(1)} %get-tuple-element.9), channel_id=1, source_target_pairs={{0,4},{4,0},{8,12},{12,8},{16,20},{20,16},{24,28},{28,24},{1,5},{5... | collective-permute-start | bytes 1160 | tf_op jit(solution)/shard_map/ppermute | solution.py:249
  47.9 6.1 %collective-permute-start.4 = (f32[96]{0:T(128)S(1)}, f32[96]{0:T(128)S(1)}, u32[]{:S(2)}, u32[]{:S(2)}) collective-permute-start(f32[96]{0:T(128)S(1)} %add.15), channel_id=1, source_target_pairs={{0,1},{1,0},{2,3},{3,2},{4,5},{5,4},{6,7},{7,6},{8,9},{9,8},{10,11... | collective-permute-start | bytes 1160 | tf_op jit(solution)/shard_map/ppermute | solution.py:249
  53.9 7.6 %collective-permute-start.5 = (f32[96]{0:T(128)S(1)}, f32[96]{0:T(128)S(1)}, u32[]{:S(2)}, u32[]{:S(2)}) collective-permute-start(f32[96]{0:T(128)S(1)} %add.16), channel_id=1, source_target_pairs={{0,2},{1,3},{2,0},{3,1},{4,6},{5,7},{6,4},{7,5},{8,10},{9,11},{10,... | collective-permute-start | bytes 1160 | tf_op jit(solution)/shard_map/ppermute | solution.py:249
  55.1 31.9 %collective-permute-start.11 = (bf16[112,4096]{1,0:T(8,128)(2,1)S(1)}, bf16[112,4096]{1,0:T(8,128)(2,1)}, u32[]{:S(2)}, u32[]{:S(2)}) collective-permute-start(bf16[112,4096]{1,0:T(8,128)(2,1)S(1)} %copy-done.1), channel_id=1, source_target_pairs={{2,3},{6,7},{10,11},{14,15},{18,19},{22,23},{26,27},{28,29},{29,28... | collective-permute-start | bytes 2752520 | tf_op jit(solution)/shard_map/ppermute | solution.py:268
  61.8 9.2 %collective-permute-start.10 = (f16[8,96,512]{2,1,0:T(8,128)(2,1)S(1)}, f16[8,96,512]{2,1,0:T(8,128)(2,1)S(1)}, u32[]{:S(2)}, u32[]{:S(2)}) collective-permute-start(f16[8,96,512]{2,1,0:T(8,128)(2,1)S(1)} %pad_maximum_fusion), channel_id=1, source_target_pairs={{0,1},{1,0},{2,3},{3,2},{4,5},{5,4},{6,7},{7,6},{8,9},{9,8},{10,11... | collective-permute-start | bytes 2359304 | tf_op jit(solution)/shard_map/ppermute | solution.py:249
  67.0 19.1 %collective-permute-start.6 = (f16[8,96,512]{2,1,0:T(8,128)(2,1)S(1)}, f16[8,96,512]{2,1,0:T(8,128)(2,1)S(1)}, u32[]{:S(2)}, u32[]{:S(2)}) collective-permute-start(f16[8,96,512]{2,1,0:T(8,128)(2,1)S(1)} %pad_maximum_fusion), channel_id=1, source_target_pairs={{0,2},{1,3},{2,0},{3,1},{4,6},{5,7},{6,4},{7,5},{8,10},{9,11},{10,... | collective-permute-start | bytes 2359304 | tf_op jit(solution)/shard_map/ppermute | solution.py:249
  67.6 56.3 %collective-permute-start.9 = (bf16[112,4096]{1,0:T(8,128)(2,1)}, bf16[112,4096]{1,0:T(8,128)(2,1)}, u32[]{:S(2)}, u32[]{:S(2)}) collective-permute-start(bf16[112,4096]{1,0:T(8,128)(2,1)} %collective-permute-done.8.u_own), channel_id=1, source_target_pairs={{2,3},{6,7},{10,11},{14,15},{18,19},{22,23},{26,27},{28,29},{29,28... | collective-permute-start | bytes 2752520 | tf_op jit(solution)/shard_map/ppermute | solution.py:268
  86.1 36.4 %collective-permute-start.7 = (f16[8,96,512]{2,1,0:T(8,128)(2,1)S(1)}, f16[8,96,512]{2,1,0:T(8,128)(2,1)S(1)}, u32[]{:S(2)}, u32[]{:S(2)}) collective-permute-start(f16[8,96,512]{2,1,0:T(8,128)(2,1)S(1)} %collective-permute-done.6), channel_id=1, source_target_pairs={{0,1},{1,0},{2,3},{3,2},{4,5},{5,4},{6,7},{7,6},{8,9},{9,8},{10,11... | collective-permute-start | bytes 2359304 | tf_op jit(solution)/shard_map/ppermute | solution.py:249

commit v2 on v1

--- a/solution.py
+++ b/solution.py
@@ -74,40 +74,78 @@
         f_ref[base + at : base + at + 16, pl.ds(pl.multiple_of(lane * LANES, LANES), LANES)] = value
 
 
-def gram_kernel(plan, snaps, closing, where_ref, own_ref, near_ref, u_own, u_near, inv_ref, *refs):
+def gram_kernel(plan, snaps, closing, feed, where_ref, *refs):
     modes, row_sets, col_sets, head_set, row_count, a_rows, b_rows = plan
+    pieces, sources, tables = feed
+    x_ins, refs = refs[: sum(pieces)], refs[sum(pieces) :]
+    u_ins, refs = refs[: max(sources) + 1], refs[max(sources) + 1 :]
+    inv_ref, refs = refs[0], refs[1:]
     if closing:
-        acc_in, out_ref, acc_ref, prior_ref, sem, x_ref, f_ref = refs
+        acc_in, out_ref, acc_ref, acc_sem = refs[:4]
+        prior = pltpu.make_async_copy(acc_in, acc_ref, acc_sem)
     else:
-        acc_ref, x_ref, f_ref = refs
-    step, steps = pl.program_id(0), pl.num_programs(0)
-    slots, _, slot_depth = own_ref.shape
+        acc_ref = refs[0]
+    x_buf, x_sem, u_buf, u_sem, x_ref, f_ref = refs[-6:]
+    step, steps = pl.program_id(0), len(pieces)
+    _, slots, inputs, slot_depth = u_buf.shape
     per = slot_depth // LANES
     lanes = slots * per
-    inputs = u_own.shape[0]
+    wanted = jnp.logical_or(where_ref[0] == len(row_sets) - 1, where_ref[1] == len(col_sets) - 1)
+
+    def x_copies(number):
+        copies, at = [], 0
+        for piece in range(pieces[number]):
+            ref = x_ins[sum(pieces[:number]) + piece]
+            copies.append(
+                pltpu.make_async_copy(ref, x_buf.at[number % 2, at : at + ref.shape[0]], x_sem.at[number % 2, piece])
+            )
+            at += ref.shape[0]
+        return copies
+
+    def u_copies(number):
+        for slot in range(slots):
+            chunk = where_ref[2 + tables[number] * slots + slot]
+            at = pl.ds(pl.multiple_of(chunk * slot_depth, slot_depth), slot_depth)
+            yield pltpu.make_async_copy(
+                u_ins[sources[number]].at[:, at], u_buf.at[number % 2, slot], u_sem.at[number % 2, slot]
+            )
+
+    def fetch(number):
+        for copy in x_copies(number):
+            copy.start()
+        pl.when(wanted)(lambda: [copy.start() for copy in u_copies(number)] and None)
+
+    def arrive(number):
+        for copy in x_copies(number):
+            copy.wait()
+        pl.when(wanted)(lambda: [copy.wait() for copy in u_copies(number)] and None)
 
     @pl.when(step == 0)
     def _():
+        fetch(0)
         if closing:
-            pltpu.make_async_copy(acc_in, prior_ref, sem).start()
-        f_ref[...] = jnp.zeros_like(f_ref)
-        x_ref[...] = jnp.zeros_like(x_ref)
-        acc_ref[...] = jnp.zeros_like(acc_ref)
+            prior.start()
+        else:
+            acc_ref[...] = jnp.zeros_like(acc_ref)
 
     scale = inv_ref[...]
-
-    def prepare(x_in, u_in, first_slot):
-        for slot in range(slots):
-            source = where_ref[2 + first_slot + slot] * slot_depth
-            for lane in range(per):
-                at = slice(lane * LANES, (lane + 1) * LANES)
-                x_ref[slot * per + lane, PAD : PAD + modes, :] = x_in[slot, :, at] * scale
-                u_at = pl.ds(pl.multiple_of(source + lane * LANES, LANES), LANES)
-                x_ref[slot * per + lane, PAD + modes : PAD + modes + inputs, :] = u_in[:, u_at].astype(jnp.float32)
-
-    half = steps // 2
-    pl.when(step < half)(lambda: prepare(own_ref, u_own, step * slots))
-    pl.when(step >= half)(lambda: prepare(near_ref, u_near, (step - half) * slots))
+    for number in range(steps):
+        @pl.when(step == number)
+        def _(number=number):
+            if number + 1 < steps:
+                fetch(number + 1)
+            arrive(number)
+            now = number % 2
+            for lane in range(lanes):
+                at = slice(lane % per * LANES, (lane % per + 1) * LANES)
+                x_ref[lane, PAD : PAD + modes, :] = x_buf[now, lane // per, :, at] * scale
+
+            @pl.when(wanted)
+            def _():
+                for lane in range(lanes):
+                    at = slice(lane % per * LANES, (lane % per + 1) * LANES)
+                    rows = slice(PAD + modes, PAD + modes + inputs)
+                    x_ref[lane, rows, :] = u_buf[now, lane // per, :, at].astype(jnp.float32)
 
     def build(rows, base):
         @pl.loop(0, lanes)
@@ -120,6 +158,8 @@
     for number, rows in enumerate(col_sets):
         pl.when(where_ref[1] == number)(lambda rows=rows: build(rows, a_rows))
 
+    if closing:
+        pl.when(step == 0)(prior.wait)
     left = f_ref[0:a_rows, :]
     for at in range(0, b_rows, 256):
         wide = min(256, b_rows - at)
@@ -131,8 +171,7 @@
     if closing:
         @pl.when(step == steps - 1)
         def _():
-            pltpu.make_async_copy(acc_in, prior_ref, sem).wait()
-            finish(snaps, row_count, len(col_sets[0]), where_ref, acc_ref, prior_ref, out_ref)
+            finish(snaps, row_count, len(col_sets[0]), where_ref, acc_ref, out_ref)
 
 
 def make_plan(modes, count, time_count, space_count):
@@ -146,43 +185,42 @@
     return modes, row_sets, col_sets, pairs[:NB], row_count, a_rows, b_rows
 
 
-def gram_call(plan, snaps, where, own, near, u_own, u_near, inv, acc=None, depth=2048):
+def gram_call(plan, snaps, where, xs, us, sources, tables, inv, acc=None):
     modes, _, col_sets, _, row_count, a_rows, b_rows = plan
-    total, _, slot_depth = own.shape
-    inputs = u_own.shape[0]
-    slots = depth // slot_depth
-    half = total // slots
+    inputs = us[0].shape[0]
+    slot_depth = xs[0][0].shape[2]
+    slots = sum(piece.shape[0] for piece in xs[0])
+    depth = slots * slot_depth
     lanes = depth // LANES
+    steps = len(xs)
+    pieces = [len(x) for x in xs]
     closing = acc is not None
-    whole = lambda shape: pl.BlockSpec(shape, lambda k, w: (0,) * len(shape))
-    block = (slots, modes, slot_depth)
-    in_specs = [
-        pl.BlockSpec(block, lambda k, w: (jnp.minimum(k, half - 1), 0, 0)),
-        pl.BlockSpec(block, lambda k, w: (jnp.maximum(k - half, 0), 0, 0)),
-        whole(u_own.shape),
-        whole(u_near.shape),
-        whole((modes, 1)),
-    ]
-    args = [own, near, u_own, u_near, inv]
-    acc_shape = (a_rows, b_rows)
+    args = [piece for x in xs for piece in x] + list(us)
+    in_specs = [pl.BlockSpec(memory_space=pl.ANY)] * len(args)
+    args.append(inv)
+    in_specs.append(pl.BlockSpec((modes, 1), lambda k, w: (0, 0)))
+    acc_shape = out_shape = (a_rows, b_rows)
     scratch = [
+        pltpu.VMEM((2, slots, modes, slot_depth), jnp.float32),
+        pltpu.SemaphoreType.DMA((2, max(pieces))),
+        pltpu.VMEM((2, slots, inputs, slot_depth), jnp.bfloat16),
+        pltpu.SemaphoreType.DMA((2, slots)),
         pltpu.VMEM((lanes, PAD + modes + inputs + 8, LANES), jnp.float32),
         pltpu.VMEM((-(-(row_count + b_rows) // 16) * 16, depth), jnp.bfloat16),
     ]
-    out_shape = acc_shape
     if closing:
         in_specs.append(pl.BlockSpec(memory_space=pl.ANY))
         args.append(acc)
-        scratch = [pltpu.VMEM(acc_shape, jnp.float32)] * 2 + [pltpu.SemaphoreType.DMA] + scratch
+        scratch = [pltpu.VMEM(acc_shape, jnp.float32), pltpu.SemaphoreType.DMA] + scratch
         out_shape = (row_count, len(col_sets[0]))
-    flops = 2 * a_rows * b_rows * 2 * total * slot_depth
+    flops = 2 * a_rows * b_rows * steps * depth
     return pl.pallas_call(
-        functools.partial(gram_kernel, plan, snaps, closing),
+        functools.partial(gram_kernel, plan, snaps, closing, (pieces, sources, tables)),
         grid_spec=pltpu.PrefetchScalarGridSpec(
             num_scalar_prefetch=1,
-            grid=(2 * half,),
+            grid=(steps,),
             in_specs=in_specs,
-            out_specs=whole(out_shape),
+            out_specs=pl.BlockSpec(out_shape, lambda k, w: (0, 0)),
             scratch_shapes=scratch,
         ),
         out_shape=jax.ShapeDtypeStruct(out_shape, jnp.float32),
@@ -195,25 +233,54 @@
 
 
 def inverse_factor(corner):
-    sub = lax.broadcasted_iota(jnp.int32, (8, 2 * NB), 0)
     row_ids = lax.broadcasted_iota(jnp.int32, (NB, NB), 0)
     col_ids = lax.broadcasted_iota(jnp.int32, (NB, NB), 1)
     eye = (row_ids == col_ids).astype(jnp.float32)
-    joined = jnp.concatenate([corner, eye], axis=1)
-    tiles = [joined[at : at + 8] for at in range(0, NB, 8)]
-    for k in range(NB):
-        q, r = divmod(k, 8)
-        row = tiles[q][r : r + 1]
-        row = row * (1.0 / row[:, k : k + 1])
-        for p in range(q, NB // 8):
-            column = tiles[p][:, k : k + 1]
-            change = column * row
-            if p == q:
-                change = jnp.where(sub > r, change, 0.0)
-            tiles[p] = tiles[p] - change
-    done = jnp.concatenate(tiles, axis=0)
-    pivots = jnp.sum(done[:, :NB] * eye, axis=1, keepdims=True)
-    return done[:, NB:] * lax.rsqrt(pivots)
+    sub = lax.broadcasted_iota(jnp.int32, (8, NB), 0)
+    left = [corner[at : at + 8] for at in range(0, NB, 8)]
+    right = [eye[at : at + 8] for at in range(0, NB, 8)]
+    spread = lambda x: jnp.broadcast_to(x, (8, NB))
+    out = []
+    for q in range(NB // 8):
+        columns = [spread(left[q][:, 8 * q + c : 8 * q + c + 1]) for c in range(8)]
+        a = {(r, c): spread(columns[c][r : r + 1, :]) for r in range(8) for c in range(r + 1)}
+        low = {}
+        invd = []
+        for k in range(8):
+            inv = 1.0 / a[k, k]
+            invd.append(inv)
+            for r in range(k + 1, 8):
+                low[r, k] = a[r, k] * inv
+            for r in range(k + 1, 8):
+                for c in range(k + 1, r + 1):
+                    a[r, c] = a[r, c] - low[r, k] * a[c, k]
+            w = {}
+        for c in range(8):
+            for r in range(c + 1, 8):
+                v = low[r, c]
+                for m in range(c + 1, r):
+                    v = v + low[r, m] * w[m, c]
+                w[r, c] = -v
+        roots = [lax.rsqrt(a[k, k]) for k in range(8)]
+        ul, ur = None, None
+        for c in range(8):
+            m = jnp.where(sub == c, roots[c], 0.0)
+            for r in range(c + 1, 8):
+                m = jnp.where(sub == r, w[r, c] * roots[r], m)
+            tl, tr = m * spread(left[q][c : c + 1, :]), m * spread(right[q][c : c + 1, :])
+            ul, ur = (tl, tr) if ul is None else (ul + tl, ur + tr)
+        out.append(ur)
+        if q == NB // 8 - 1:
+            break
+        turned = ul.T
+        rows_l = [spread(ul[c : c + 1, :]) for c in range(8)]
+        rows_r = [spread(ur[c : c + 1, :]) for c in range(8)]
+        for p in range(q + 1, NB // 8):
+            for c in range(8):
+                m = spread(turned[8 * p : 8 * p + 8, c : c + 1])
+                left[p] = left[p] - m * rows_l[c]
+                right[p] = right[p] - m * rows_r[c]
+    return jnp.concatenate(out, axis=0)
 
 
 def dot32(a, b, dims):
@@ -222,12 +289,12 @@
     )
 
 
-def finish(snaps, row_count, col_count, where_ref, acc_ref, prior_ref, out_ref):
+def finish(snaps, row_count, col_count, where_ref, acc_ref, out_ref):
     t, s = where_ref[0], where_ref[1]
     head = slice(row_count, row_count + NB)
 
     def gram_part(rows, cols, row_start, col_start):
-        value = (acc_ref[rows, cols] + prior_ref[rows, cols]) * (1.0 / snaps)
+        value = acc_ref[rows, cols] * (1.0 / snaps)
         row_ids = row_start + lax.broadcasted_iota(jnp.int32, value.shape, 0)
         col_ids = col_start + lax.broadcasted_iota(jnp.int32, value.shape, 1)
         return value + REG * (row_ids == col_ids).astype(jnp.float32), row_ids
@@ -269,7 +336,6 @@
 
     u_near = some(inputs, 1, (2,))
     u_far = some(inputs, 2, (0, 1))
-    u_far_near = some(u_far, 1, (2,))
 
     limit = 1200.0 * 0.0625 * snapshots.shape[0] * space_count
     shrink = 2.0 ** -max(0, math.ceil(math.log2(limit / 65000.0)))
@@ -278,27 +344,36 @@
     part = part.reshape(modes, space_count, depth).transpose(1, 0, 2)
     part = lax.all_to_all(part, "space", 0, 0, tiled=False)
     mine = jnp.sum(part.astype(jnp.float32), axis=0).astype(jnp.float16)[None]
+    mine, u_near, u_far = lax.optimization_barrier((mine, u_near, u_far))
+    u_far_near = some(u_far, 1, (2,))
+
+    bits = [1 << b for b in reversed(range(space_count.bit_length() - 1))]
+    wide = mine[0].astype(jnp.float32)
+    energy = jnp.sum(wide * wide, axis=1)
+    for axis, bit in [("tm", 2), ("tm", 1)] + [("space", bit) for bit in bits]:
+        energy = energy + swap(energy, axis, bit)
     order = [0]
-    bit = space_count // 2
-    while bit:
-        if bit == 1:
-            wide = mine.astype(jnp.float32)
-            energy = jnp.sum(wide * wide, axis=(0, 2))
-            for axis, step in (("space", 1), ("tm", 1), ("tm", 2)):
-                energy = energy + swap(energy, axis, step)
+    for bit in bits[:-1]:
         mine = jnp.concatenate([mine, swap(mine, "space", bit)], axis=0)
         order = order + [o ^ bit for o in order]
-        bit //= 2
-    mine, energy = lax.optimization_barrier((mine, energy))
     inv = (shrink ** -1 / jnp.sqrt(energy / (snaps * shrink * shrink) + EPS))[:, None]
-    where = jnp.concatenate([jnp.stack([t, s]), s ^ jnp.asarray(order, jnp.int32)]).astype(jnp.int32)
+    order = jnp.asarray(order + [o ^ 1 for o in order], jnp.int32)
+    where = jnp.concatenate([jnp.stack([t, s]), s ^ order]).astype(jnp.int32)
+
+    def both(x):
+        return x.astype(jnp.float32), swap(x, "tm", 1).astype(jnp.float32)
+
+    diagonal = [
+        (a * time_count + b, (a ^ 1) * time_count + (b ^ 2)) for a in range(space_count) for b in range(time_count)
+    ]
+    beside = swap(mine, "space", 1)
     far = swap(mine, "tm", 2)
-    near = swap(mine, "tm", 1)
-    acc = gram_call(plan, snaps, where, mine.astype(jnp.float32), near.astype(jnp.float32), inputs, u_near, inv)
-    far_near = swap(far, "tm", 1)
-    return gram_call(
-        plan, snaps, where, far.astype(jnp.float32), far_near.astype(jnp.float32), u_far, u_far_near, inv, acc
-    )
+    cross = lax.ppermute(mine, ("space", "tm"), diagonal)
+    us = [inputs, u_near, u_far, u_far_near]
+    acc = gram_call(plan, snaps, where, [[x] for x in both(mine)], us[:2], [0, 1], [0, 0], inv)
+    acc, beside, far, cross = lax.optimization_barrier((acc, beside, far, cross))
+    xs = [[x] for x in both(beside) + both(far) + both(cross)]
+    return gram_call(plan, snaps, where, xs, us, [0, 1, 2, 3, 2, 3], [1, 1, 0, 0, 1, 1], inv, acc)
 
 
 def solution(mesh):

time: 176 us -> 150 us (0.85)
  blocking collectives: 24.7 us -> 0 us
  starting transfers between devices: 19.1 us -> 25.8 us
  waiting for transfers between devices: 32.4 us -> 26.5 us
  Pallas kernels: 85.6 us -> 79.8 us
  other arithmetic: 6.75 us -> 8.99 us
  local copies, waits for them, and re-layouts: 1.84 us -> 3.72 us
    ppermute x9 -> x13, waiting for transfers between devices: 32.4 us -> 6.43 us  [swap(): lax.ppermute(x, axis, [(i, i ^ bit) for i in range(lax.axis_size(axis))])]
    all_to_all x1 -> x0, blocking collectives: 24.7 us -> none  [shards(): part = lax.all_to_all(part, 'space', 0, 0, tiled=False)]
    all_to_all x0 -> x1, waiting for transfers between devices: none -> 16.4 us  [shards(): part = lax.all_to_all(part, 'space', 0, 0, tiled=False)]
    pallas_call x2, Pallas kernels: 85.6 us -> 79.8 us  [gram_call(): pl.pallas_call(functools.partial(gram_kernel, plan, snaps, closing, (piec...]
    all_to_all x0 -> x1, starting transfers between devices: none -> 5.55 us  [shards(): part = lax.all_to_all(part, 'space', 0, 0, tiled=False)]
    ppermute x3, waiting for transfers between devices: 0.01 us -> 3.62 us  [some(): return lax.ppermute(x, ('space', 'tm'), pairs)]
    convert_element_type x4 -> x8, other arithmetic: 5.5 us -> 8.06 us  [both(): return (x.astype(jnp.float32), swap(x, 'tm', 1).astype(jnp.float32))]
    ppermute x9 -> x13, starting transfers between devices: 15.3 us -> 16.4 us  [swap(): lax.ppermute(x, axis, [(i, i ^ bit) for i in range(lax.axis_size(axis))])]
  transfers between devices with their start and end apart: 12 -> 18, of which waited for: 6 -> 6; matrix products, arithmetic and copies ran while one was open for 4% -> 7% of each run, Pallas kernels for 19% -> 13%
where the time goes in v2:
time: 150 us
  Pallas kernels  79.8 us (53%)
  waiting for transfers between devices  26.5 us (18%)
  starting transfers between devices  25.8 us (17%)
  other arithmetic  8.99 us (6%)
  matrix products  4.93 us (3%)
  local copies, waits for them, and re-layouts  3.72 us (2%)
    pallas_call x2, Pallas kernels, gram_call(): pl.pallas_call(functools.partial(gram_kernel, plan, snaps, closing, (piec...  79.8 us
    all_to_all x1, waiting for transfers between devices, shards(): part = lax.all_to_all(part, 'space', 0, 0, tiled=False)  16.4 us
    ppermute x13, starting transfers between devices, swap(): lax.ppermute(x, axis, [(i, i ^ bit) for i in range(lax.axis_size(axis))])  16.4 us
    convert_element_type x8, other arithmetic, both(): return (x.astype(jnp.float32), swap(x, 'tm', 1).astype(jnp.float32))  8.06 us
    ppermute x13, waiting for transfers between devices, swap(): lax.ppermute(x, axis, [(i, i ^ bit) for i in range(lax.axis_size(axis))])  6.43 us
    all_to_all x1, starting transfers between devices, shards(): part = lax.all_to_all(part, 'space', 0, 0, tiled=False)  5.55 us
    dot_general x1, matrix products, shards(): jnp.einsum('dr,ds->rs', pod_basis, snapshots, preferred_element_type=jnp....  4.93 us
    ppermute x3, starting transfers between devices, some(): return lax.ppermute(x, ('space', 'tm'), pairs)  3.86 us
  transfers between devices with their start and end apart: 18, of which 6 were waited for; matrix products, arithmetic and copies ran while one was open for 7% of the time, Pallas kernels for 13%

profile of v2, /device:TPU:3, one launch (start us, length us, event | category | flops | bytes accessed | tf_op | source)
XLA Modules:
  0.0 150.0 jit_solution(12611403711387331853)
XLA Ops:
  0.0 0.9 copy-done
  0.9 4.9 %fusion = f16[96,4096]{1,0:T(8,128)(2,1)S(1)} fusion(bf16[1024,96]{0,1:T(8,128)(2,1)S(1)} %copy-done, bf16[1024,4096]{1,0:T(8,128)(2,1)} %param.4), kind=kOutput, calls=%fused_computation.1 | convolution fusion | flops 806092800 | bytes 9371648 | tf_op jit(solution)/shard_map/dr,ds->rs/dot_general | solution.py:342
  5.9 0.0 copy-start.4
  5.9 1.0 copy.12
  6.9 5.6 %all-to-all-start = ((f16[8,96,512]{2,1,0:T(8,128)(2,1)}), f16[8,96,512]{2,1,0:T(8,128)(2,1)S(1)}, u32[]{:S(2)}, u32[]{:S(2)}) async-start(f16[8,96,512]{2,1,0:T(8,128)(2,1)} %bitcast.14), calls=%async_computation | async-start | bytes 1572864 | tf_op jit(solution)/shard_map/all_to_all | solution.py:345
  12.5 1.3 collective-permute-start.1
  13.8 1.3 collective-permute-start
  15.1 16.4 %all-to-all-done = f16[8,96,512]{2,1,0:T(8,128)(2,1)S(1)} async-done(((f16[8,96,512]{2,1,0:T(8,128)(2,1)}), f16[8,96,512]{2,1,0:T(8,128)(2,1)S(1)}, u32[]{:S(2)}, u32[]{:S(2)}) %all-to-all-start) | async-done | bytes 786464 | tf_op jit(solution)/shard_map/all_to_all | solution.py:345
  31.5 0.1 convert_reduce_fusion
  31.7 3.6 %collective-permute-done.1.refs_8_ = bf16[112,4096]{1,0:T(8,128)(2,1)S(1)} collective-permute-done((bf16[112,4096]{1,0:T(8,128)(2,1)S(1)}, bf16[112,4096]{1,0:T(8,128)(2,1)S(1)}, u32[]{:S(2)}, u32[]{:S(2)}) %collective-permute-start.1) | collective-permute-done | bytes 917536 | tf_op jit(solution)/shard_map/ppermute | solution.py:335
  35.3 2.1 %collective-permute-start.2 = (f16[1,96,512]{2,1,0:T(8,128)(2,1)S(1)}, f16[1,96,512]{2,1,0:T(8,128)(2,1)S(1)}, u32[]{:S(2)}, u32[]{:S(2)}) collective-permute-start(f16[1,96,512]{2,1,0:T(8,128)(2,1)S(1)} %convert_bitcast_fusion), channel_id=1, source_target_pairs={{0,16},{4,20},{8,24},{12,28},{16,0},{20,4},{24,8},{28,12},{1,17},{... | collective-permute-start | bytes 294920 | tf_op jit(solution)/shard_map/ppermute | solution.py:316
  37.3 0.1 multiply_reduce_fusion
  37.4 0.1 collective-permute-start.5
  37.5 2.4 %collective-permute-done.5 = f32[96]{0:T(128)S(1)} collective-permute-done((f32[96]{0:T(128)S(1)}, f32[96]{0:T(128)S(1)}, u32[]{:S(2)}, u32[]{:S(2)}) %collective-permute-start.5) | collective-permute-done | bytes 416 | tf_op jit(solution)/shard_map/ppermute | solution.py:316
  39.9 3.6 %collective-permute-start.6 = (f32[96]{0:T(128)S(1)}, f32[96]{0:T(128)S(1)}, u32[]{:S(2)}, u32[]{:S(2)}) collective-permute-start(f32[96]{0:T(128)S(1)} %add.21), channel_id=1, source_target_pairs={{0,1},{1,0},{2,3},{3,2},{4,5},{5,4},{6,7},{7,6},{8,9},{9,8},{10,11... | collective-permute-start | bytes 1160 | tf_op jit(solution)/shard_map/ppermute | solution.py:316
  43.5 0.8 collective-permute-done.6
  44.3 0.0 collective-permute-start.7
  44.3 0.0 collective-permute-done.2
  44.4 1.5 %collective-permute-start.3 = (f16[2,96,512]{2,1,0:T(8,128)(2,1)S(1)}, f16[2,96,512]{2,1,0:T(8,128)(2,1)S(1)}, u32[]{:S(2)}, u32[]{:S(2)}) collective-permute-start(f16[2,96,512]{2,1,0:T(8,128)(2,1)S(1)} %pad_maximum_fusion), channel_id=1, source_target_pairs={{0,8},{4,12},{8,0},{12,4},{16,24},{20,28},{24,16},{28,20},{1,9},{5... | collective-permute-start | bytes 589832 | tf_op jit(solution)/shard_map/ppermute | solution.py:316
  45.9 1.7 %collective-permute-done.7 = f32[96]{0:T(128)S(1)} collective-permute-done((f32[96]{0:T(128)S(1)}, f32[96]{0:T(128)S(1)}, u32[]{:S(2)}, u32[]{:S(2)}) %collective-permute-start.7) | collective-permute-done | bytes 416 | tf_op jit(solution)/shard_map/ppermute | solution.py:316
  47.6 1.2 collective-permute-start.8
  48.8 1.5 %collective-permute-done.3 = f16[2,96,512]{2,1,0:T(8,128)(2,1)S(1)} collective-permute-done((f16[2,96,512]{2,1,0:T(8,128)(2,1)S(1)}, f16[2,96,512]{2,1,0:T(8,128)(2,1)S(1)}, u32[]{:S(2)}, u32[]{:S(2)}) %collective-permute-start.3) | collective-permute-done | bytes 196640 | tf_op jit(solution)/shard_map/ppermute | solution.py:316
  50.4 1.5 %collective-permute-start.4 = (f16[4,96,512]{2,1,0:T(8,128)(2,1)S(1)}, f16[4,96,512]{2,1,0:T(8,128)(2,1)S(1)}, u32[]{:S(2)}, u32[]{:S(2)}) collective-permute-start(f16[4,96,512]{2,1,0:T(8,128)(2,1)S(1)} %constant_dynamic-update-slice_fusion), channel_id=1, source_target_pairs={{0,1},{1,0},{2,3},{3,2},{4,5},{5,4},{6,7},{7,6},{8,9},{9,8},{10,11... | collective-permute-start | bytes 1179656 | tf_op jit(solution)/shard_map/ppermute | solution.py:316
  51.9 1.5 %collective-permute-start.9 = (f32[96]{0:T(128)S(1)}, f32[96]{0:T(128)S(1)}, u32[]{:S(2)}, u32[]{:S(2)}) collective-permute-start(f32[96]{0:T(128)S(1)} %add.24), channel_id=1, source_target_pairs={{0,4},{4,0},{8,12},{12,8},{16,20},{20,16},{24,28},{28,24},{1,5},{5... | collective-permute-start | bytes 1160 | tf_op jit(solution)/shard_map/ppermute | solution.py:316
  53.4 0.6 pad_add_fusion.where_ref
  54.0 1.3 collective-permute-start.16
  55.4 0.7 copy.8.refs_4_.refs_10_
  56.1 0.0 collective-permute-start.12
  56.1 1.7 %collective-permute-start.11 = (f16[4,96,512]{2,1,0:T(8,128)(2,1)S(1)}, f16[4,96,512]{2,1,0:T(8,128)(2,1)S(1)}, u32[]{:S(2)}, u32[]{:S(2)}) collective-permute-start(f16[4,96,512]{2,1,0:T(8,128)(2,1)S(1)} %constant_dynamic-update-slice_fusion), channel_id=1, source_target_pairs={{0,2},{1,3},{2,0},{3,1},{4,6},{5,7},{6,4},{7,5},{8,10},{9,11},{10,... | collective-permute-start | bytes 1179656 | tf_op jit(solution)/shard_map/ppermute | solution.py:316
  57.7 1.0 collective-permute-start.10
  58.7 1.0 convert_element_type.51.refs_0_
  59.7 1.0 convert_element_type.52.refs_1_
  60.7 19.1 %gram.1.refs_11_ = f32[1344,768]{1,0:T(8,128)} custom-call(s32[10]{0:T(128)} %pad_add_fusion.where_ref, f32[4,96,512]{2,1,0:T(8,128)} %convert_element_type.51.refs_0_, f32[4,96,512]{2,1,0:T(8,128)} %convert_element_type.52.refs_1_, bf16[112,4096]{1,0:T(8,128)(2,1)} %refs_6_.1, bf16[112,4096]{1,0:T(8,128)(2,1)} %collective-permute-done.refs_3_.refs_7_, ...), custom_call_target="tpu_custom_call" | custom-call | flops 16911433728 | bytes 20000000 | tf_op jit(solution)/shard_map/gram/pallas_call | solution.py:217
  79.8 0.0 collective-permute-done.12
  79.9 0.0 collective-permute-done.11
  79.9 1.8 %collective-permute-start.13 = (f16[4,96,512]{2,1,0:T(8,128)(2,1)S(1)}, f16[4,96,512]{2,1,0:T(8,128)(2,1)S(1)}, u32[]{:S(2)}, u32[]{:S(2)}) collective-permute-start(f16[4,96,512]{2,1,0:T(8,128)(2,1)S(1)} %collective-permute-done.10), channel_id=1, source_target_pairs={{0,1},{1,0},{2,3},{3,2},{4,5},{5,4},{6,7},{7,6},{8,9},{9,8},{10,11... | collective-permute-start | bytes 1179656 | tf_op jit(solution)/shard_map/ppermute | solution.py:316
  81.6 0.1 collective-permute-start.14
  81.7 0.4 collective-permute-start.15
  82.2 1.0 convert_element_type.54.refs_0_
  83.1 1.1 convert_element_type.56.refs_2_
  84.2 1.0 convert_element_type.58.refs_4_
  85.2 1.1 convert_element_type.55.refs_1_
  86.3 0.0 collective-permute-done.14
  86.3 1.0 convert_element_type.57.refs_3_
  87.3 0.0 collective-permute-done.15
  87.3 1.0 convert_element_type.59.refs_5_
  88.3 0.9 copy-done.3
  89.2 60.7 %close.1 = f32[1216,608]{1,0:T(8,128)} custom-call(s32[10]{0:T(128)} %pad_add_fusion.where_ref, f32[4,96,512]{2,1,0:T(8,128)} %convert_element_type.54.refs_0_, f32[4,96,512]{2,1,0:T(8,128)} %convert_element_type.55.refs_1_, f32[4,96,512]{2,1,0:T(8,128)} %convert_element_type.56.refs_2_, f32[4,96,512]{2,1,0:T(8,128)} %convert_element_type.57.refs_3_, ...), custom_call_target="tpu_custom_call" | custom-call | flops 50734301184 | bytes 20000000 | tf_op jit(solution)/shard_map/close/pallas_call | solution.py:217
  (25 shorter events, 0.2 us)
Async XLA Ops:
  0.0 0.9 copy-start
  0.9 11.5 %copy-start.1 = (bf16[112,4096]{1,0:T(8,128)(2,1)S(1)}, bf16[112,4096]{1,0:T(8,128)(2,1)}, u32[]{:S(2)}) copy-start(bf16[112,4096]{1,0:T(8,128)(2,1)} %refs_6_.1) | copy-start | bytes 2752516
  5.9 46.0 %copy-start.4 = (s32[8]{0:T(128)S(1)}, s32[8]{0:T(128)}, u32[]{:S(2)}) copy-start(s32[8]{0:T(128)} %constant.22.clone) | copy-start | bytes 100
  6.9 24.6 %all-to-all-start = ((f16[8,96,512]{2,1,0:T(8,128)(2,1)}), f16[8,96,512]{2,1,0:T(8,128)(2,1)S(1)}, u32[]{:S(2)}, u32[]{:S(2)}) async-start(f16[8,96,512]{2,1,0:T(8,128)(2,1)} %bitcast.14), calls=%async_computation | async-start | bytes 1572864 | tf_op jit(solution)/shard_map/all_to_all | solution.py:345
  12.5 22.8 %collective-permute-start.1 = (bf16[112,4096]{1,0:T(8,128)(2,1)S(1)}, bf16[112,4096]{1,0:T(8,128)(2,1)S(1)}, u32[]{:S(2)}, u32[]{:S(2)}) collective-permute-start(bf16[112,4096]{1,0:T(8,128)(2,1)S(1)} %copy-done.1), channel_id=1, source_target_pairs={{0,2},{1,3},{4,6},{5,7},{8,10},{9,11},{12,14},{13,15},{16,18},{17,... | collective-permute-start | bytes 2752520 | tf_op jit(solution)/shard_map/ppermute | solution.py:335
  13.8 21.5 %collective-permute-start = (bf16[112,4096]{1,0:T(8,128)(2,1)S(1)}, bf16[112,4096]{1,0:T(8,128)(2,1)}, u32[]{:S(2)}, u32[]{:S(2)}) collective-permute-start(bf16[112,4096]{1,0:T(8,128)(2,1)S(1)} %copy-done.1), channel_id=1, source_target_pairs={{2,3},{6,7},{10,11},{14,15},{18,19},{22,23},{26,27},{28,29},{29,28... | collective-permute-start | bytes 2752520 | tf_op jit(solution)/shard_map/ppermute | solution.py:335
  35.3 44.6 %copy-start.2 = (bf16[112,4096]{1,0:T(8,128)(2,1)}, bf16[112,4096]{1,0:T(8,128)(2,1)S(1)}, u32[]{:S(2)}) copy-start(bf16[112,4096]{1,0:T(8,128)(2,1)S(1)} %collective-permute-done.1.refs_8_) | copy-start | bytes 2752516
  35.3 9.1 %collective-permute-start.2 = (f16[1,96,512]{2,1,0:T(8,128)(2,1)S(1)}, f16[1,96,512]{2,1,0:T(8,128)(2,1)S(1)}, u32[]{:S(2)}, u32[]{:S(2)}) collective-permute-start(f16[1,96,512]{2,1,0:T(8,128)(2,1)S(1)} %convert_bitcast_fusion), channel_id=1, source_target_pairs={{0,16},{4,20},{8,24},{12,28},{16,0},{20,4},{24,8},{28,12},{1,17},{... | collective-permute-start | bytes 294920 | tf_op jit(solution)/shard_map/ppermute | solution.py:316
  37.4 2.5 %collective-permute-start.5 = (f32[96]{0:T(128)S(1)}, f32[96]{0:T(128)S(1)}, u32[]{:S(2)}, u32[]{:S(2)}) collective-permute-start(f32[96]{0:T(128)S(1)} %multiply_reduce_fusion), channel_id=1, source_target_pairs={{0,2},{1,3},{2,0},{3,1},{4,6},{5,7},{6,4},{7,5},{8,10},{9,11},{10,... | collective-permute-start | bytes 1160 | tf_op jit(solution)/shard_map/ppermute | solution.py:316
  39.9 4.4 %collective-permute-start.6 = (f32[96]{0:T(128)S(1)}, f32[96]{0:T(128)S(1)}, u32[]{:S(2)}, u32[]{:S(2)}) collective-permute-start(f32[96]{0:T(128)S(1)} %add.21), channel_id=1, source_target_pairs={{0,1},{1,0},{2,3},{3,2},{4,5},{5,4},{6,7},{7,6},{8,9},{9,8},{10,11... | collective-permute-start | bytes 1160 | tf_op jit(solution)/shard_map/ppermute | solution.py:316
  44.3 3.3 %collective-permute-start.7 = (f32[96]{0:T(128)S(1)}, f32[96]{0:T(128)S(1)}, u32[]{:S(2)}, u32[]{:S(2)}) collective-permute-start(f32[96]{0:T(128)S(1)} %add.22), channel_id=1, source_target_pairs={{0,16},{4,20},{8,24},{12,28},{16,0},{20,4},{24,8},{28,12},{1,17},{... | collective-permute-start | bytes 1160 | tf_op jit(solution)/shard_map/ppermute | solution.py:316
  44.4 6.0 %collective-permute-start.3 = (f16[2,96,512]{2,1,0:T(8,128)(2,1)S(1)}, f16[2,96,512]{2,1,0:T(8,128)(2,1)S(1)}, u32[]{:S(2)}, u32[]{:S(2)}) collective-permute-start(f16[2,96,512]{2,1,0:T(8,128)(2,1)S(1)} %pad_maximum_fusion), channel_id=1, source_target_pairs={{0,8},{4,12},{8,0},{12,4},{16,24},{20,28},{24,16},{28,20},{1,9},{5... | collective-permute-start | bytes 589832 | tf_op jit(solution)/shard_map/ppermute | solution.py:316
  47.6 4.3 %collective-permute-start.8 = (f32[96]{0:T(128)S(1)}, f32[96]{0:T(128)S(1)}, u32[]{:S(2)}, u32[]{:S(2)}) collective-permute-start(f32[96]{0:T(128)S(1)} %add.23), channel_id=1, source_target_pairs={{0,8},{4,12},{8,0},{12,4},{16,24},{20,28},{24,16},{28,20},{1,9},{5... | collective-permute-start | bytes 1160 | tf_op jit(solution)/shard_map/ppermute | solution.py:316
  50.4 9.3 %collective-permute-start.4 = (f16[4,96,512]{2,1,0:T(8,128)(2,1)S(1)}, f16[4,96,512]{2,1,0:T(8,128)(2,1)S(1)}, u32[]{:S(2)}, u32[]{:S(2)}) collective-permute-start(f16[4,96,512]{2,1,0:T(8,128)(2,1)S(1)} %constant_dynamic-update-slice_fusion), channel_id=1, source_target_pairs={{0,1},{1,0},{2,3},{3,2},{4,5},{5,4},{6,7},{7,6},{8,9},{9,8},{10,11... | collective-permute-start | bytes 1179656 | tf_op jit(solution)/shard_map/ppermute | solution.py:316
  51.9 3.4 %collective-permute-start.9 = (f32[96]{0:T(128)S(1)}, f32[96]{0:T(128)S(1)}, u32[]{:S(2)}, u32[]{:S(2)}) collective-permute-start(f32[96]{0:T(128)S(1)} %add.24), channel_id=1, source_target_pairs={{0,4},{4,0},{8,12},{12,8},{16,20},{20,16},{24,28},{28,24},{1,5},{5... | collective-permute-start | bytes 1160 | tf_op jit(solution)/shard_map/ppermute | solution.py:316
  54.0 34.2 %collective-permute-start.16 = (bf16[112,4096]{1,0:T(8,128)(2,1)S(1)}, bf16[112,4096]{1,0:T(8,128)(2,1)S(1)}, u32[]{:S(2)}, u32[]{:S(2)}) collective-permute-start(bf16[112,4096]{1,0:T(8,128)(2,1)S(1)} %collective-permute-done.1.refs_8_), channel_id=1, source_target_pairs={{2,3},{6,7},{10,11},{14,15},{18,19},{22,23},{26,27},{28,29},{29,28... | collective-permute-start | bytes 2752520 | tf_op jit(solution)/shard_map/ppermute | solution.py:335
  56.1 23.8 %collective-permute-start.12 = (f16[4,96,512]{2,1,0:T(8,128)(2,1)S(1)}, f16[4,96,512]{2,1,0:T(8,128)(2,1)S(1)}, u32[]{:S(2)}, u32[]{:S(2)}) collective-permute-start(f16[4,96,512]{2,1,0:T(8,128)(2,1)S(1)} %constant_dynamic-update-slice_fusion), channel_id=1, source_target_pairs={{0,6},{1,7},{2,4},{3,5},{4,2},{5,3},{6,0},{7,1},{8,14},{9,15},{10,... | collective-permute-start | bytes 1179656 | tf_op jit(solution)/shard_map/ppermute | solution.py:371
  56.1 23.8 %collective-permute-start.11 = (f16[4,96,512]{2,1,0:T(8,128)(2,1)S(1)}, f16[4,96,512]{2,1,0:T(8,128)(2,1)S(1)}, u32[]{:S(2)}, u32[]{:S(2)}) collective-permute-start(f16[4,96,512]{2,1,0:T(8,128)(2,1)S(1)} %constant_dynamic-update-slice_fusion), channel_id=1, source_target_pairs={{0,2},{1,3},{2,0},{3,1},{4,6},{5,7},{6,4},{7,5},{8,10},{9,11},{10,... | collective-permute-start | bytes 1179656 | tf_op jit(solution)/shard_map/ppermute | solution.py:316
  57.7 22.1 %collective-permute-start.10 = (f16[4,96,512]{2,1,0:T(8,128)(2,1)S(1)}, f16[4,96,512]{2,1,0:T(8,128)(2,1)S(1)}, u32[]{:S(2)}, u32[]{:S(2)}) collective-permute-start(f16[4,96,512]{2,1,0:T(8,128)(2,1)S(1)} %constant_dynamic-update-slice_fusion), channel_id=1, source_target_pairs={{0,4},{4,0},{8,12},{12,8},{16,20},{20,16},{24,28},{28,24},{1,5},{5... | collective-permute-start | bytes 1179656 | tf_op jit(solution)/shard_map/ppermute | solution.py:316
  79.9 5.4 %collective-permute-start.13 = (f16[4,96,512]{2,1,0:T(8,128)(2,1)S(1)}, f16[4,96,512]{2,1,0:T(8,128)(2,1)S(1)}, u32[]{:S(2)}, u32[]{:S(2)}) collective-permute-start(f16[4,96,512]{2,1,0:T(8,128)(2,1)S(1)} %collective-permute-done.10), channel_id=1, source_target_pairs={{0,1},{1,0},{2,3},{3,2},{4,5},{5,4},{6,7},{7,6},{8,9},{9,8},{10,11... | collective-permute-start | bytes 1179656 | tf_op jit(solution)/shard_map/ppermute | solution.py:316
  81.6 4.6 %collective-permute-start.14 = (f16[4,96,512]{2,1,0:T(8,128)(2,1)S(1)}, f16[4,96,512]{2,1,0:T(8,128)(2,1)S(1)}, u32[]{:S(2)}, u32[]{:S(2)}) collective-permute-start(f16[4,96,512]{2,1,0:T(8,128)(2,1)S(1)} %collective-permute-done.11), channel_id=1, source_target_pairs={{0,1},{1,0},{2,3},{3,2},{4,5},{5,4},{6,7},{7,6},{8,9},{9,8},{10,11... | collective-permute-start | bytes 1179656 | tf_op jit(solution)/shard_map/ppermute | solution.py:316
  81.7 5.6 %collective-permute-start.15 = (f16[4,96,512]{2,1,0:T(8,128)(2,1)S(1)}, f16[4,96,512]{2,1,0:T(8,128)(2,1)S(1)}, u32[]{:S(2)}, u32[]{:S(2)}) collective-permute-start(f16[4,96,512]{2,1,0:T(8,128)(2,1)S(1)} %collective-permute-done.12), channel_id=1, source_target_pairs={{0,1},{1,0},{2,3},{3,2},{4,5},{5,4},{6,7},{7,6},{8,9},{9,8},{10,11... | collective-permute-start | bytes 1179656 | tf_op jit(solution)/shard_map/ppermute | solution.py:316
  88.3 0.9 copy-start.3

commit v3 on v2

--- a/solution.py
+++ b/solution.py
@@ -74,12 +74,12 @@
         f_ref[base + at : base + at + 16, pl.ds(pl.multiple_of(lane * LANES, LANES), LANES)] = value
 
 
-def gram_kernel(plan, snaps, closing, feed, where_ref, *refs):
+def gram_kernel(plan, snaps, shrink, closing, feed, where_ref, *refs):
     modes, row_sets, col_sets, head_set, row_count, a_rows, b_rows = plan
     pieces, sources, tables = feed
     x_ins, refs = refs[: sum(pieces)], refs[sum(pieces) :]
     u_ins, refs = refs[: max(sources) + 1], refs[max(sources) + 1 :]
-    inv_ref, refs = refs[0], refs[1:]
+    energy_ref, refs = refs[0], refs[1:]
     if closing:
         acc_in, out_ref, acc_ref, acc_sem = refs[:4]
         prior = pltpu.make_async_copy(acc_in, acc_ref, acc_sem)
@@ -128,7 +128,9 @@
         else:
             acc_ref[...] = jnp.zeros_like(acc_ref)
 
-    scale = inv_ref[...]
+    scale = lax.rsqrt(energy_ref[...] * (1.0 / (snaps * shrink * shrink)) + EPS) * (1.0 / shrink)
+    ids = lax.broadcasted_iota(jnp.int32, (modes, modes), 0), lax.broadcasted_iota(jnp.int32, (modes, modes), 1)
+    scale = jnp.sum(jnp.where(ids[0] == ids[1], scale, 0.0), axis=1, keepdims=True)
     for number in range(steps):
         @pl.when(step == number)
         def _(number=number):
@@ -160,18 +162,29 @@
 
     if closing:
         pl.when(step == 0)(prior.wait)
-    left = f_ref[0:a_rows, :]
-    for at in range(0, b_rows, 256):
-        wide = min(256, b_rows - at)
-        right = f_ref[row_count + at : row_count + at + wide, :]
-        acc_ref[:, at : at + wide] += lax.dot_general(
-            left, right, (((1,), (1,)), ((), ())), preferred_element_type=jnp.float32
-        )
-
-    if closing:
-        @pl.when(step == steps - 1)
-        def _():
-            finish(snaps, row_count, len(col_sets[0]), where_ref, acc_ref, out_ref)
+    def contract():
+        left = f_ref[0:a_rows, :]
+        for at in range(0, b_rows, 256):
+            wide = min(256, b_rows - at)
+            right = f_ref[row_count + at : row_count + at + wide, :]
+            acc_ref[:, at : at + wide] += lax.dot_general(
+                left, right, (((1,), (1,)), ((), ())), preferred_element_type=jnp.float32
+            )
+
+    if not closing:
+        contract()
+        return
+    pl.when(step < steps - 1)(contract)
+
+    @pl.when(step == steps - 1)
+    def _():
+        head = f_ref[row_count:a_rows, :]
+        corner = lax.dot_general(head, head, (((1,), (1,)), ((), ())), preferred_element_type=jnp.float32)
+        corner = (acc_ref[row_count:a_rows, 0:NB] + corner) * (1.0 / snaps)
+        ids = lax.broadcasted_iota(jnp.int32, (NB, NB), 0), lax.broadcasted_iota(jnp.int32, (NB, NB), 1)
+        inverse = inverse_factor(corner + REG * (ids[0] == ids[1]).astype(jnp.float32))
+        contract()
+        finish(snaps, row_count, len(col_sets[0]), where_ref, inverse, acc_ref, out_ref)
 
 
 def make_plan(modes, count, time_count, space_count):
@@ -185,7 +198,7 @@
     return modes, row_sets, col_sets, pairs[:NB], row_count, a_rows, b_rows
 
 
-def gram_call(plan, snaps, where, xs, us, sources, tables, inv, acc=None):
+def gram_call(plan, snaps, shrink, where, xs, us, sources, tables, energy, acc=None):
     modes, _, col_sets, _, row_count, a_rows, b_rows = plan
     inputs = us[0].shape[0]
     slot_depth = xs[0][0].shape[2]
@@ -197,8 +210,8 @@
     closing = acc is not None
     args = [piece for x in xs for piece in x] + list(us)
     in_specs = [pl.BlockSpec(memory_space=pl.ANY)] * len(args)
-    args.append(inv)
-    in_specs.append(pl.BlockSpec((modes, 1), lambda k, w: (0, 0)))
+    args.append(energy)
+    in_specs.append(pl.BlockSpec((1, modes), lambda k, w: (0, 0)))
     acc_shape = out_shape = (a_rows, b_rows)
     scratch = [
         pltpu.VMEM((2, slots, modes, slot_depth), jnp.float32),
@@ -215,7 +228,7 @@
         out_shape = (row_count, len(col_sets[0]))
     flops = 2 * a_rows * b_rows * steps * depth
     return pl.pallas_call(
-        functools.partial(gram_kernel, plan, snaps, closing, (pieces, sources, tables)),
+        functools.partial(gram_kernel, plan, snaps, shrink, closing, (pieces, sources, tables)),
         grid_spec=pltpu.PrefetchScalarGridSpec(
             num_scalar_prefetch=1,
             grid=(steps,),
@@ -283,13 +296,22 @@
     return jnp.concatenate(out, axis=0)
 
 
-def dot32(a, b, dims):
-    return lax.dot_general(
-        a, b, (dims, ((), ())), precision=lax.Precision.HIGHEST, preferred_element_type=jnp.float32
+def halves(x):
+    high = x.astype(jnp.bfloat16)
+    return high, (x - high.astype(jnp.float32)).astype(jnp.bfloat16)
+
+
+def dot32(a, b):
+    (a_high, a_low), (b_high, b_low) = a, b
+    both = jnp.dot(
+        jnp.concatenate([a_high, a_high], axis=1),
+        jnp.concatenate([b_high, b_low], axis=0),
+        preferred_element_type=jnp.float32,
     )
-
-
-def finish(snaps, row_count, col_count, where_ref, acc_ref, out_ref):
+    return both + jnp.dot(a_low, b_high, preferred_element_type=jnp.float32)
+
+
+def finish(snaps, row_count, col_count, where_ref, inverse, acc_ref, out_ref):
     t, s = where_ref[0], where_ref[1]
     head = slice(row_count, row_count + NB)
 
@@ -300,13 +322,14 @@
         return value + REG * (row_ids == col_ids).astype(jnp.float32), row_ids
 
     own = slice(NB, NB + col_count)
-    inverse = inverse_factor(gram_part(head, slice(0, NB), 0, 0)[0])
-    cols_factor = dot32(inverse, gram_part(head, own, 0, s * col_count)[0], ((1,), (0,)))
-    for at in range(0, row_count, NB):
-        rows = slice(at, min(at + NB, row_count))
-        factor = dot32(gram_part(rows, slice(0, NB), t * row_count + at, 0)[0], inverse, ((1,), (1,)))
+    cols_factor = dot32(halves(inverse), halves(gram_part(head, own, 0, s * col_count)[0]))
+    cols_factor, turned = halves(cols_factor), halves(inverse.T)
+    tall = row_count // 4
+    for at in range(0, row_count, tall):
+        rows = slice(at, at + tall)
+        factor = dot32(halves(gram_part(rows, slice(0, NB), t * row_count + at, 0)[0]), turned)
         value, row_ids = gram_part(rows, own, t * row_count + at, s * col_count)
-        value = value - dot32(factor, cols_factor, ((1,), (0,)))
+        value = value - dot32(halves(factor), cols_factor)
         value = jnp.where(row_ids < NB, 0.0, value)
         out_ref[rows, NB:col_count] = value[:, NB:]
         out_ref[rows, 0:NB] = jnp.where(s == 0, factor, value[:, :NB])
@@ -344,36 +367,47 @@
     part = part.reshape(modes, space_count, depth).transpose(1, 0, 2)
     part = lax.all_to_all(part, "space", 0, 0, tiled=False)
     mine = jnp.sum(part.astype(jnp.float32), axis=0).astype(jnp.float16)[None]
-    mine, u_near, u_far = lax.optimization_barrier((mine, u_near, u_far))
-    u_far_near = some(u_far, 1, (2,))
-
-    bits = [1 << b for b in reversed(range(space_count.bit_length() - 1))]
-    wide = mine[0].astype(jnp.float32)
-    energy = jnp.sum(wide * wide, axis=1)
-    for axis, bit in [("tm", 2), ("tm", 1)] + [("space", bit) for bit in bits]:
-        energy = energy + swap(energy, axis, bit)
+    mine, u_near = lax.optimization_barrier((mine, u_near))
+
+    def partners(axes):
+        return [a ^ b for a in (0, axes[0]) for b in (0, axes[-1])][1:] if len(axes) > 1 else axes
+
+    def crossing(a_bit, b_bit):
+        return [
+            (a * time_count + b, (a ^ a_bit) * time_count + (b ^ b_bit))
+            for a in range(space_count)
+            for b in range(time_count)
+        ]
+
+    bits = [1 << b for b in reversed(range(1, space_count.bit_length() - 1))]
+    levels = [bits[at : at + 2] for at in range(0, len(bits), 2)]
     order = [0]
-    for bit in bits[:-1]:
-        mine = jnp.concatenate([mine, swap(mine, "space", bit)], axis=0)
-        order = order + [o ^ bit for o in order]
-    inv = (shrink ** -1 / jnp.sqrt(energy / (snaps * shrink * shrink) + EPS))[:, None]
+    for level in levels:
+        mine = jnp.concatenate([mine] + [swap(mine, "space", bit) for bit in partners(level)], axis=0)
+        order = order + [o ^ bit for bit in partners(level) for o in order]
+    mine, u_far = lax.optimization_barrier((mine, u_far))
+    wide = mine.astype(jnp.float32)
+    energy = jnp.sum(wide * wide, axis=(0, 2))[None]
+    moves = [(0, 2), (1, 0), (1, 2)]
+    energy = energy + sum(lax.ppermute(energy, ("space", "tm"), crossing(*move)) for move in moves)
+    energy = energy + swap(energy, "tm", 1)
+    mine, energy = lax.optimization_barrier((mine, energy))
     order = jnp.asarray(order + [o ^ 1 for o in order], jnp.int32)
     where = jnp.concatenate([jnp.stack([t, s]), s ^ order]).astype(jnp.int32)
 
     def both(x):
-        return x.astype(jnp.float32), swap(x, "tm", 1).astype(jnp.float32)
-
-    diagonal = [
-        (a * time_count + b, (a ^ 1) * time_count + (b ^ 2)) for a in range(space_count) for b in range(time_count)
-    ]
+        x = x.astype(jnp.float32)
+        return x, swap(x, "tm", 1)
+
     beside = swap(mine, "space", 1)
     far = swap(mine, "tm", 2)
-    cross = lax.ppermute(mine, ("space", "tm"), diagonal)
-    us = [inputs, u_near, u_far, u_far_near]
-    acc = gram_call(plan, snaps, where, [[x] for x in both(mine)], us[:2], [0, 1], [0, 0], inv)
-    acc, beside, far, cross = lax.optimization_barrier((acc, beside, far, cross))
+    cross = lax.ppermute(mine, ("space", "tm"), crossing(1, 2))
+    us = [inputs, u_near]
+    acc = gram_call(plan, snaps, shrink, where, [[x] for x in both(mine)], us, [0, 1], [0, 0], energy)
+    acc, beside, far, cross, u_far = lax.optimization_barrier((acc, beside, far, cross, u_far))
+    us = us + [u_far, some(u_far, 1, (2,))]
     xs = [[x] for x in both(beside) + both(far) + both(cross)]
-    return gram_call(plan, snaps, where, xs, us, [0, 1, 2, 3, 2, 3], [1, 1, 0, 0, 1, 1], inv, acc)
+    return gram_call(plan, snaps, shrink, where, xs, us, [0, 1, 2, 3, 2, 3], [1, 1, 0, 0, 1, 1], energy, acc)
 
 
 def solution(mesh):

time: 150 us -> 139 us (0.927)
  Pallas kernels: 79.8 us -> 72.3 us
  other arithmetic: 8.99 us -> 2.01 us
  waiting for transfers between devices: 26.5 us -> 30.3 us
  starting transfers between devices: 25.8 us -> 23.5 us
    convert_element_type x8 -> x4, other arithmetic: 8.06 us -> 0.35 us  [both(): x = x.astype(jnp.float32)]
    pallas_call x2, Pallas kernels: 79.8 us -> 72.3 us  [gram_call(): pl.pallas_call(functools.partial(gram_kernel, plan, snaps, shrink, closin...]
    ppermute x13 -> x10, starting transfers between devices: 16.4 us -> 9.65 us  [swap(): lax.ppermute(x, axis, [(i, i ^ bit) for i in range(lax.axis_size(axis))])]
    ppermute x13 -> x10, waiting for transfers between devices: 6.43 us -> 12.5 us  [swap(): lax.ppermute(x, axis, [(i, i ^ bit) for i in range(lax.axis_size(axis))])]
    ppermute x1 -> x4, starting transfers between devices: 0.01 us -> 4.43 us  [the longest x3 2.82 us: shards(): lax.ppermute(energy, ('space', 'tm'), crossing(*move))]
    ppermute x3, waiting for transfers between devices: 3.62 us -> 0.01 us  [some(): return lax.ppermute(x, ('space', 'tm'), pairs)]
    unnamed x12 -> x26, local copies, waits for them, and re-layouts: 1.92 us -> 3.71 us
  transfers between devices with their start and end apart: 18 -> 18, of which waited for: 6 -> 10; matrix products, arithmetic and copies ran while one was open for 7% -> 1% of each run, Pallas kernels for 13% -> 14%
where the time goes in v3:
time: 139 us; the launch traced here: 138 us
  Pallas kernels  72.3 us (52%)
  waiting for transfers between devices  30.3 us (22%)
  starting transfers between devices  23.5 us (17%)
  matrix products  4.93 us (4%)
  local copies, waits for them, and re-layouts  4.76 us (3%)
  other arithmetic  2.01 us (1%)
    pallas_call x2, Pallas kernels, gram_call(): pl.pallas_call(functools.partial(gram_kernel, plan, snaps, shrink, closin...  72.3 us
    all_to_all x1, waiting for transfers between devices, shards(): part = lax.all_to_all(part, 'space', 0, 0, tiled=False)  16.4 us
    ppermute x10, waiting for transfers between devices, swap(): lax.ppermute(x, axis, [(i, i ^ bit) for i in range(lax.axis_size(axis))])  12.5 us
    ppermute x10, starting transfers between devices, swap(): lax.ppermute(x, axis, [(i, i ^ bit) for i in range(lax.axis_size(axis))])  9.65 us
    all_to_all x1, starting transfers between devices, shards(): part = lax.all_to_all(part, 'space', 0, 0, tiled=False)  5.55 us
    dot_general x1, matrix products, shards(): jnp.einsum('dr,ds->rs', pod_basis, snapshots, preferred_element_type=jnp....  4.93 us
    ppermute x3, starting transfers between devices, some(): return lax.ppermute(x, ('space', 'tm'), pairs)  3.88 us
    unnamed x26, local copies, waits for them, and re-layouts  3.71 us
  transfers between devices with their start and end apart: 18, of which 10 were waited for; matrix products, arithmetic and copies ran while one was open for 1% of the time, Pallas kernels for 14%

profile of v3, /device:TPU:3, one launch (start us, length us, event | category | flops | bytes accessed | tf_op | source)
XLA Modules:
  0.0 138.1 jit_solution(8158750226466898571)
XLA Ops:
  0.0 0.9 copy-done
  0.9 4.9 %fusion = f16[96,4096]{1,0:T(8,128)(2,1)S(1)} fusion(bf16[1024,96]{0,1:T(8,128)(2,1)S(1)} %copy-done, bf16[1024,4096]{1,0:T(8,128)(2,1)} %param.4), kind=kOutput, calls=%fused_computation.1 | convolution fusion | flops 806092800 | bytes 9371648 | tf_op jit(solution)/shard_map/dr,ds->rs/dot_general | solution.py:365
  5.9 0.0 copy-start.12
  5.9 1.0 copy.8
  6.9 5.6 %all-to-all-start = ((f16[8,96,512]{2,1,0:T(8,128)(2,1)}), f16[8,96,512]{2,1,0:T(8,128)(2,1)S(1)}, u32[]{:S(2)}, u32[]{:S(2)}) async-start(f16[8,96,512]{2,1,0:T(8,128)(2,1)} %bitcast.14), calls=%async_computation | async-start | bytes 1572864 | tf_op jit(solution)/shard_map/all_to_all | solution.py:368
  12.5 1.3 collective-permute-start
  13.8 1.3 collective-permute-start.4
  15.1 16.4 %all-to-all-done = f16[8,96,512]{2,1,0:T(8,128)(2,1)S(1)} async-done(((f16[8,96,512]{2,1,0:T(8,128)(2,1)}), f16[8,96,512]{2,1,0:T(8,128)(2,1)S(1)}, u32[]{:S(2)}, u32[]{:S(2)}) %all-to-all-start) | async-done | bytes 786464 | tf_op jit(solution)/shard_map/all_to_all | solution.py:368
  31.5 0.1 convert_reduce_fusion
  31.7 2.2 %collective-permute-start.3 = (f16[1,96,512]{2,1,0:T(8,128)(2,1)S(1)}, f16[1,96,512]{2,1,0:T(8,128)(2,1)S(1)}, u32[]{:S(2)}, u32[]{:S(2)}) collective-permute-start(f16[1,96,512]{2,1,0:T(8,128)(2,1)S(1)} %convert_bitcast_fusion), channel_id=1, source_target_pairs={{0,24},{4,28},{8,16},{12,20},{16,8},{20,12},{24,0},{28,4},{1,25},{... | collective-permute-start | bytes 294920 | tf_op jit(solution)/shard_map/ppermute | solution.py:339
  33.8 0.0 collective-permute-start.2
  33.8 1.5 %collective-permute-start.1 = (f16[1,96,512]{2,1,0:T(8,128)(2,1)S(1)}, f16[1,96,512]{2,1,0:T(8,128)(2,1)S(1)}, u32[]{:S(2)}, u32[]{:S(2)}) collective-permute-start(f16[1,96,512]{2,1,0:T(8,128)(2,1)S(1)} %convert_bitcast_fusion), channel_id=1, source_target_pairs={{0,8},{4,12},{8,0},{12,4},{16,24},{20,28},{24,16},{28,20},{1,9},{5... | collective-permute-start | bytes 294920 | tf_op jit(solution)/shard_map/ppermute | solution.py:339
  35.3 1.8 %collective-permute-done.3 = f16[1,96,512]{2,1,0:T(8,128)(2,1)S(1)} collective-permute-done((f16[1,96,512]{2,1,0:T(8,128)(2,1)S(1)}, f16[1,96,512]{2,1,0:T(8,128)(2,1)S(1)}, u32[]{:S(2)}, u32[]{:S(2)}) %collective-permute-start.3) | collective-permute-done | bytes 98336 | tf_op jit(solution)/shard_map/ppermute | solution.py:339
  37.1 5.5 %collective-permute-done.2 = f16[1,96,512]{2,1,0:T(8,128)(2,1)S(1)} collective-permute-done((f16[1,96,512]{2,1,0:T(8,128)(2,1)S(1)}, f16[1,96,512]{2,1,0:T(8,128)(2,1)S(1)}, u32[]{:S(2)}, u32[]{:S(2)}) %collective-permute-start.2) | collective-permute-done | bytes 98336 | tf_op jit(solution)/shard_map/ppermute | solution.py:339
  42.6 0.1 pad_maximum_fusion
  42.8 0.0 collective-permute-done.4.refs_8_
  42.8 0.2 multiply_reduce_fusion
  42.9 1.6 %collective-permute-start.7 = (f32[1,96]{1,0:T(1,128)S(1)}, f32[1,96]{1,0:T(1,128)S(1)}, u32[]{:S(2)}, u32[]{:S(2)}) collective-permute-start(f32[1,96]{1,0:T(1,128)S(1)} %bitcast.16), channel_id=1, source_target_pairs={{0,6},{1,7},{2,4},{3,5},{4,2},{5,3},{6,0},{7,1},{8,14},{9,15},{10,... | collective-permute-start | bytes 1160 | tf_op jit(solution)/shard_map/ppermute | solution.py:392
  44.6 0.1 collective-permute-start.6
  44.7 1.1 collective-permute-start.5
  45.8 0.5 collective-permute-done.7
  46.3 0.6 collective-permute-done.6
  46.9 0.1 collective-permute-done.5
  47.1 2.9 %collective-permute-start.8 = (f32[1,96]{1,0:T(1,128)S(1)}, f32[1,96]{1,0:T(1,128)S(1)}, u32[]{:S(2)}, u32[]{:S(2)}) collective-permute-start(f32[1,96]{1,0:T(1,128)S(1)} %add_add_fusion), channel_id=1, source_target_pairs={{0,1},{1,0},{2,3},{3,2},{4,5},{5,4},{6,7},{7,6},{8,9},{9,8},{10,11... | collective-permute-start | bytes 1160 | tf_op jit(solution)/shard_map/ppermute | solution.py:339
  49.9 0.8 collective-permute-done.8
  50.8 0.6 add.15.refs_4_.refs_10_
  51.3 0.1 convert_element_type.39.refs_0_
  51.4 0.0 copy-start.1
  51.4 0.4 collective-permute-start.9
  51.8 0.7 pad_add_fusion.where_ref
  52.5 1.6 %collective-permute-start.12 = (f16[4,96,512]{2,1,0:T(8,128)(2,1)S(1)}, f16[4,96,512]{2,1,0:T(8,128)(2,1)S(1)}, u32[]{:S(2)}, u32[]{:S(2)}) collective-permute-start(f16[4,96,512]{2,1,0:T(8,128)(2,1)S(1)} %pad_maximum_fusion), channel_id=1, source_target_pairs={{0,6},{1,7},{2,4},{3,5},{4,2},{5,3},{6,0},{7,1},{8,14},{9,15},{10,... | collective-permute-start | bytes 1179656 | tf_op jit(solution)/shard_map/ppermute | solution.py:404
  54.1 0.3 collective-permute-start.11
  54.3 0.8 collective-permute-start.10
  55.1 0.9 copy-done.8
  56.0 18.9 %gram.1.refs_11_ = f32[1344,768]{1,0:T(8,128)} custom-call(s32[10]{0:T(128)} %pad_add_fusion.where_ref, f32[4,96,512]{2,1,0:T(8,128)} %copy-done.1, f32[4,96,512]{2,1,0:T(8,128)} %copy-done.8, bf16[112,4096]{1,0:T(8,128)(2,1)} %refs_6_.1, bf16[112,4096]{1,0:T(8,128)(2,1)} %copy-done.6, f32[1,96]{1,0:T(1,128)} %add.15.refs_4_.refs_10_), custom_call_target="tpu_custom_call" | custom-call | flops 16911433728 | bytes 20000000 | tf_op jit(solution)/shard_map/gram/pallas_call | solution.py:230
  74.9 1.3 collective-permute-start.16
  76.2 0.1 convert_element_type.40.refs_0_
  76.3 0.1 convert_element_type.41.refs_2_
  76.4 0.1 convert_element_type.42.refs_4_
  76.5 1.2 collective-permute-start.15
  77.8 0.1 collective-permute-start.14
  77.9 0.4 collective-permute-start.13
  78.3 2.1 %collective-permute-done.15.refs_5_ = f32[4,96,512]{2,1,0:T(8,128)S(1)} collective-permute-done((f32[4,96,512]{2,1,0:T(8,128)S(1)}, f32[4,96,512]{2,1,0:T(8,128)S(1)}, u32[]{:S(2)}, u32[]{:S(2)}) %collective-permute-start.15) | collective-permute-done | bytes 786464 | tf_op jit(solution)/shard_map/ppermute | solution.py:339
  80.4 1.1 collective-permute-done.14.refs_3_
  81.5 1.1 collective-permute-done.13.refs_1_
  82.7 0.9 copy-done.11
  83.6 0.9 copy-done.7
  84.6 53.4 %close.1 = f32[1216,608]{1,0:T(8,128)} custom-call(s32[10]{0:T(128)} %pad_add_fusion.where_ref, f32[4,96,512]{2,1,0:T(8,128)} %copy-done.2, f32[4,96,512]{2,1,0:T(8,128)} %copy-done.11, f32[4,96,512]{2,1,0:T(8,128)} %copy-done.3, f32[4,96,512]{2,1,0:T(8,128)} %copy-done.10, f32[4,96,512]{2,1,0:T(8,128)} %copy-done.4, f32[4,96,512]{2,1,0:T(8,128)} %copy-done.9, ...), custom_call_target="tpu_custom_call" | custom-call | flops 50734301184 | bytes 20000000 | tf_op jit(solution)/shard_map/close/pallas_call | solution.py:230
  (30 shorter events, 0.1 us)
Async XLA Ops:
  0.0 0.9 copy-start
  0.9 11.5 %copy-start.5 = (bf16[112,4096]{1,0:T(8,128)(2,1)S(1)}, bf16[112,4096]{1,0:T(8,128)(2,1)}, u32[]{:S(2)}) copy-start(bf16[112,4096]{1,0:T(8,128)(2,1)} %refs_6_.1) | copy-start | bytes 2752516
  5.9 46.0 %copy-start.12 = (s32[8]{0:T(128)S(1)}, s32[8]{0:T(128)}, u32[]{:S(2)}) copy-start(s32[8]{0:T(128)} %constant.15.clone) | copy-start | bytes 100
  6.9 24.6 %all-to-all-start = ((f16[8,96,512]{2,1,0:T(8,128)(2,1)}), f16[8,96,512]{2,1,0:T(8,128)(2,1)S(1)}, u32[]{:S(2)}, u32[]{:S(2)}) async-start(f16[8,96,512]{2,1,0:T(8,128)(2,1)} %bitcast.14), calls=%async_computation | async-start | bytes 1572864 | tf_op jit(solution)/shard_map/all_to_all | solution.py:368
  12.5 19.2 %collective-permute-start = (bf16[112,4096]{1,0:T(8,128)(2,1)S(1)}, bf16[112,4096]{1,0:T(8,128)(2,1)S(1)}, u32[]{:S(2)}, u32[]{:S(2)}) collective-permute-start(bf16[112,4096]{1,0:T(8,128)(2,1)S(1)} %copy-done.5), channel_id=1, source_target_pairs={{2,3},{6,7},{10,11},{14,15},{18,19},{22,23},{26,27},{28,29},{29,28... | collective-permute-start | bytes 2752520 | tf_op jit(solution)/shard_map/ppermute | solution.py:358
  13.8 29.0 %collective-permute-start.4 = (bf16[112,4096]{1,0:T(8,128)(2,1)S(1)}, bf16[112,4096]{1,0:T(8,128)(2,1)}, u32[]{:S(2)}, u32[]{:S(2)}) collective-permute-start(bf16[112,4096]{1,0:T(8,128)(2,1)S(1)} %copy-done.5), channel_id=1, source_target_pairs={{0,2},{1,3},{4,6},{5,7},{8,10},{9,11},{12,14},{13,15},{16,18},{17,... | collective-permute-start | bytes 2752520 | tf_op jit(solution)/shard_map/ppermute | solution.py:358
  31.7 23.5 %copy-start.6 = (bf16[112,4096]{1,0:T(8,128)(2,1)}, bf16[112,4096]{1,0:T(8,128)(2,1)S(1)}, u32[]{:S(2)}) copy-start(bf16[112,4096]{1,0:T(8,128)(2,1)S(1)} %collective-permute-done.refs_3_.refs_7_) | copy-start | bytes 2752516
  31.7 5.4 %collective-permute-start.3 = (f16[1,96,512]{2,1,0:T(8,128)(2,1)S(1)}, f16[1,96,512]{2,1,0:T(8,128)(2,1)S(1)}, u32[]{:S(2)}, u32[]{:S(2)}) collective-permute-start(f16[1,96,512]{2,1,0:T(8,128)(2,1)S(1)} %convert_bitcast_fusion), channel_id=1, source_target_pairs={{0,24},{4,28},{8,16},{12,20},{16,8},{20,12},{24,0},{28,4},{1,25},{... | collective-permute-start | bytes 294920 | tf_op jit(solution)/shard_map/ppermute | solution.py:339
  33.8 8.8 %collective-permute-start.2 = (f16[1,96,512]{2,1,0:T(8,128)(2,1)S(1)}, f16[1,96,512]{2,1,0:T(8,128)(2,1)S(1)}, u32[]{:S(2)}, u32[]{:S(2)}) collective-permute-start(f16[1,96,512]{2,1,0:T(8,128)(2,1)S(1)} %convert_bitcast_fusion), channel_id=1, source_target_pairs={{0,16},{4,20},{8,24},{12,28},{16,0},{20,4},{24,8},{28,12},{1,17},{... | collective-permute-start | bytes 294920 | tf_op jit(solution)/shard_map/ppermute | solution.py:339
  33.8 8.8 %collective-permute-start.1 = (f16[1,96,512]{2,1,0:T(8,128)(2,1)S(1)}, f16[1,96,512]{2,1,0:T(8,128)(2,1)S(1)}, u32[]{:S(2)}, u32[]{:S(2)}) collective-permute-start(f16[1,96,512]{2,1,0:T(8,128)(2,1)S(1)} %convert_bitcast_fusion), channel_id=1, source_target_pairs={{0,8},{4,12},{8,0},{12,4},{16,24},{20,28},{24,16},{28,20},{1,9},{5... | collective-permute-start | bytes 294920 | tf_op jit(solution)/shard_map/ppermute | solution.py:339
  42.9 3.3 %collective-permute-start.7 = (f32[1,96]{1,0:T(1,128)S(1)}, f32[1,96]{1,0:T(1,128)S(1)}, u32[]{:S(2)}, u32[]{:S(2)}) collective-permute-start(f32[1,96]{1,0:T(1,128)S(1)} %bitcast.16), channel_id=1, source_target_pairs={{0,6},{1,7},{2,4},{3,5},{4,2},{5,3},{6,0},{7,1},{8,14},{9,15},{10,... | collective-permute-start | bytes 1160 | tf_op jit(solution)/shard_map/ppermute | solution.py:392
  44.6 2.4 %collective-permute-start.6 = (f32[1,96]{1,0:T(1,128)S(1)}, f32[1,96]{1,0:T(1,128)S(1)}, u32[]{:S(2)}, u32[]{:S(2)}) collective-permute-start(f32[1,96]{1,0:T(1,128)S(1)} %bitcast.17), channel_id=1, source_target_pairs={{0,4},{1,5},{2,6},{3,7},{4,0},{5,1},{6,2},{7,3},{8,12},{9,13},{10,... | collective-permute-start | bytes 1160 | tf_op jit(solution)/shard_map/ppermute | solution.py:392
  44.7 2.4 %collective-permute-start.5 = (f32[1,96]{1,0:T(1,128)S(1)}, f32[1,96]{1,0:T(1,128)S(1)}, u32[]{:S(2)}, u32[]{:S(2)}) collective-permute-start(f32[1,96]{1,0:T(1,128)S(1)} %bitcast.18), channel_id=1, source_target_pairs={{0,2},{1,3},{2,0},{3,1},{4,6},{5,7},{6,4},{7,5},{8,10},{9,11},{10,... | collective-permute-start | bytes 1160 | tf_op jit(solution)/shard_map/ppermute | solution.py:392
  47.1 3.7 %collective-permute-start.8 = (f32[1,96]{1,0:T(1,128)S(1)}, f32[1,96]{1,0:T(1,128)S(1)}, u32[]{:S(2)}, u32[]{:S(2)}) collective-permute-start(f32[1,96]{1,0:T(1,128)S(1)} %add_add_fusion), channel_id=1, source_target_pairs={{0,1},{1,0},{2,3},{3,2},{4,5},{5,4},{6,7},{7,6},{8,9},{9,8},{10,11... | collective-permute-start | bytes 1160 | tf_op jit(solution)/shard_map/ppermute | solution.py:339
  51.4 3.7 %copy-start.1 = (f32[4,96,512]{2,1,0:T(8,128)}, f32[4,96,512]{2,1,0:T(8,128)S(1)}, u32[]{:S(2)}) copy-start(f32[4,96,512]{2,1,0:T(8,128)S(1)} %convert_element_type.39.refs_0_) | copy-start | bytes 2359300
  51.4 3.7 %collective-permute-start.9 = (f32[4,96,512]{2,1,0:T(8,128)S(1)}, f32[4,96,512]{2,1,0:T(8,128)S(1)}, u32[]{:S(2)}, u32[]{:S(2)}) collective-permute-start(f32[4,96,512]{2,1,0:T(8,128)S(1)} %convert_element_type.39.refs_0_), channel_id=1, source_target_pairs={{0,1},{1,0},{2,3},{3,2},{4,5},{5,4},{6,7},{7,6},{8,9},{9,8},{10,11... | collective-permute-start | bytes 2359304 | tf_op jit(solution)/shard_map/ppermute | solution.py:339
  52.5 22.4 %collective-permute-start.12 = (f16[4,96,512]{2,1,0:T(8,128)(2,1)S(1)}, f16[4,96,512]{2,1,0:T(8,128)(2,1)S(1)}, u32[]{:S(2)}, u32[]{:S(2)}) collective-permute-start(f16[4,96,512]{2,1,0:T(8,128)(2,1)S(1)} %pad_maximum_fusion), channel_id=1, source_target_pairs={{0,6},{1,7},{2,4},{3,5},{4,2},{5,3},{6,0},{7,1},{8,14},{9,15},{10,... | collective-permute-start | bytes 1179656 | tf_op jit(solution)/shard_map/ppermute | solution.py:404
  54.1 20.8 %collective-permute-start.11 = (f16[4,96,512]{2,1,0:T(8,128)(2,1)S(1)}, f16[4,96,512]{2,1,0:T(8,128)(2,1)S(1)}, u32[]{:S(2)}, u32[]{:S(2)}) collective-permute-start(f16[4,96,512]{2,1,0:T(8,128)(2,1)S(1)} %pad_maximum_fusion), channel_id=1, source_target_pairs={{0,2},{1,3},{2,0},{3,1},{4,6},{5,7},{6,4},{7,5},{8,10},{9,11},{10,... | collective-permute-start | bytes 1179656 | tf_op jit(solution)/shard_map/ppermute | solution.py:339
  54.3 20.6 %collective-permute-start.10 = (f16[4,96,512]{2,1,0:T(8,128)(2,1)S(1)}, f16[4,96,512]{2,1,0:T(8,128)(2,1)S(1)}, u32[]{:S(2)}, u32[]{:S(2)}) collective-permute-start(f16[4,96,512]{2,1,0:T(8,128)(2,1)S(1)} %pad_maximum_fusion), channel_id=1, source_target_pairs={{0,4},{4,0},{8,12},{12,8},{16,20},{20,16},{24,28},{28,24},{1,5},{5... | collective-permute-start | bytes 1179656 | tf_op jit(solution)/shard_map/ppermute | solution.py:339
  55.1 0.9 copy-start.8
  74.9 7.7 %collective-permute-start.16 = (bf16[112,4096]{1,0:T(8,128)(2,1)}, bf16[112,4096]{1,0:T(8,128)(2,1)S(1)}, u32[]{:S(2)}, u32[]{:S(2)}) collective-permute-start(bf16[112,4096]{1,0:T(8,128)(2,1)} %collective-permute-done.4.refs_8_), channel_id=1, source_target_pairs={{2,3},{6,7},{10,11},{14,15},{18,19},{22,23},{26,27},{28,29},{29,28... | collective-permute-start | bytes 2752520 | tf_op jit(solution)/shard_map/ppermute | solution.py:358
  76.3 6.4 %copy-start.2 = (f32[4,96,512]{2,1,0:T(8,128)}, f32[4,96,512]{2,1,0:T(8,128)S(1)}, u32[]{:S(2)}) copy-start(f32[4,96,512]{2,1,0:T(8,128)S(1)} %convert_element_type.40.refs_0_) | copy-start | bytes 2359300
  76.4 6.3 %copy-start.3 = (f32[4,96,512]{2,1,0:T(8,128)}, f32[4,96,512]{2,1,0:T(8,128)S(1)}, u32[]{:S(2)}) copy-start(f32[4,96,512]{2,1,0:T(8,128)S(1)} %convert_element_type.41.refs_2_) | copy-start | bytes 2359300
  76.5 6.2 %copy-start.4 = (f32[4,96,512]{2,1,0:T(8,128)}, f32[4,96,512]{2,1,0:T(8,128)S(1)}, u32[]{:S(2)}) copy-start(f32[4,96,512]{2,1,0:T(8,128)S(1)} %convert_element_type.42.refs_4_) | copy-start | bytes 2359300
  76.5 3.9 %collective-permute-start.15 = (f32[4,96,512]{2,1,0:T(8,128)S(1)}, f32[4,96,512]{2,1,0:T(8,128)S(1)}, u32[]{:S(2)}, u32[]{:S(2)}) collective-permute-start(f32[4,96,512]{2,1,0:T(8,128)S(1)} %convert_element_type.42.refs_4_), channel_id=1, source_target_pairs={{0,1},{1,0},{2,3},{3,2},{4,5},{5,4},{6,7},{7,6},{8,9},{9,8},{10,11... | collective-permute-start | bytes 2359304 | tf_op jit(solution)/shard_map/ppermute | solution.py:339
  77.8 3.8 %collective-permute-start.14 = (f32[4,96,512]{2,1,0:T(8,128)S(1)}, f32[4,96,512]{2,1,0:T(8,128)S(1)}, u32[]{:S(2)}, u32[]{:S(2)}) collective-permute-start(f32[4,96,512]{2,1,0:T(8,128)S(1)} %convert_element_type.41.refs_2_), channel_id=1, source_target_pairs={{0,1},{1,0},{2,3},{3,2},{4,5},{5,4},{6,7},{7,6},{8,9},{9,8},{10,11... | collective-permute-start | bytes 2359304 | tf_op jit(solution)/shard_map/ppermute | solution.py:339
  77.9 4.8 %collective-permute-start.13 = (f32[4,96,512]{2,1,0:T(8,128)S(1)}, f32[4,96,512]{2,1,0:T(8,128)S(1)}, u32[]{:S(2)}, u32[]{:S(2)}) collective-permute-start(f32[4,96,512]{2,1,0:T(8,128)S(1)} %convert_element_type.40.refs_0_), channel_id=1, source_target_pairs={{0,1},{1,0},{2,3},{3,2},{4,5},{5,4},{6,7},{7,6},{8,9},{9,8},{10,11... | collective-permute-start | bytes 2359304 | tf_op jit(solution)/shard_map/ppermute | solution.py:339
  80.4 2.3 %copy-start.9 = (f32[4,96,512]{2,1,0:T(8,128)}, f32[4,96,512]{2,1,0:T(8,128)S(1)}, u32[]{:S(2)}) copy-start(f32[4,96,512]{2,1,0:T(8,128)S(1)} %collective-permute-done.15.refs_5_) | copy-start | bytes 2359300
  81.5 1.2 copy-start.10
  82.7 1.0 copy-start.11
  83.6 0.9 copy-start.7

commit v4 on v3

--- a/solution.py
+++ b/solution.py
@@ -70,7 +70,7 @@
         return total
 
     for at in range(0, len(rows), 16):
-        value = jnp.concatenate([eight(at), eight(at + 8)], axis=0).astype(jnp.bfloat16)
+        value = jnp.concatenate([eight(at), eight(at + 8)], axis=0)
         f_ref[base + at : base + at + 16, pl.ds(pl.multiple_of(lane * LANES, LANES), LANES)] = value
 
 
@@ -79,7 +79,7 @@
     pieces, sources, tables = feed
     x_ins, refs = refs[: sum(pieces)], refs[sum(pieces) :]
     u_ins, refs = refs[: max(sources) + 1], refs[max(sources) + 1 :]
-    energy_ref, refs = refs[0], refs[1:]
+    energy_refs, refs = refs[:4], refs[4:]
     if closing:
         acc_in, out_ref, acc_ref, acc_sem = refs[:4]
         prior = pltpu.make_async_copy(acc_in, acc_ref, acc_sem)
@@ -128,7 +128,8 @@
         else:
             acc_ref[...] = jnp.zeros_like(acc_ref)
 
-    scale = lax.rsqrt(energy_ref[...] * (1.0 / (snaps * shrink * shrink)) + EPS) * (1.0 / shrink)
+    energy = sum(ref[...] for ref in energy_refs)
+    scale = lax.rsqrt(energy * (1.0 / (snaps * shrink * shrink)) + EPS) * (1.0 / shrink)
     ids = lax.broadcasted_iota(jnp.int32, (modes, modes), 0), lax.broadcasted_iota(jnp.int32, (modes, modes), 1)
     scale = jnp.sum(jnp.where(ids[0] == ids[1], scale, 0.0), axis=1, keepdims=True)
     for number in range(steps):
@@ -210,8 +211,8 @@
     closing = acc is not None
     args = [piece for x in xs for piece in x] + list(us)
     in_specs = [pl.BlockSpec(memory_space=pl.ANY)] * len(args)
-    args.append(energy)
-    in_specs.append(pl.BlockSpec((1, modes), lambda k, w: (0, 0)))
+    args += energy
+    in_specs += [pl.BlockSpec((1, modes), lambda k, w: (0, 0))] * 4
     acc_shape = out_shape = (a_rows, b_rows)
     scratch = [
         pltpu.VMEM((2, slots, modes, slot_depth), jnp.float32),
@@ -219,7 +220,7 @@
         pltpu.VMEM((2, slots, inputs, slot_depth), jnp.bfloat16),
         pltpu.SemaphoreType.DMA((2, slots)),
         pltpu.VMEM((lanes, PAD + modes + inputs + 8, LANES), jnp.float32),
-        pltpu.VMEM((-(-(row_count + b_rows) // 16) * 16, depth), jnp.bfloat16),
+        pltpu.VMEM((-(-(row_count + b_rows) // 16) * 16, depth), jnp.float32),
     ]
     if closing:
         in_specs.append(pl.BlockSpec(memory_space=pl.ANY))
@@ -238,7 +239,7 @@
         ),
         out_shape=jax.ShapeDtypeStruct(out_shape, jnp.float32),
         compiler_params=pltpu.CompilerParams(
-            vmem_limit_bytes=56 * 1024 * 1024, dimension_semantics=("arbitrary",)
+            vmem_limit_bytes=40 * 1024 * 1024, dimension_semantics=("arbitrary",)
         ),
         cost_estimate=pl.CostEstimate(flops=2 * flops, bytes_accessed=20_000_000, transcendentals=0),
         name="close" if closing else "gram",
@@ -367,7 +368,6 @@
     part = part.reshape(modes, space_count, depth).transpose(1, 0, 2)
     part = lax.all_to_all(part, "space", 0, 0, tiled=False)
     mine = jnp.sum(part.astype(jnp.float32), axis=0).astype(jnp.float16)[None]
-    mine, u_near = lax.optimization_barrier((mine, u_near))
 
     def partners(axes):
         return [a ^ b for a in (0, axes[0]) for b in (0, axes[-1])][1:] if len(axes) > 1 else axes
@@ -383,17 +383,19 @@
     levels = [bits[at : at + 2] for at in range(0, len(bits), 2)]
     order = [0]
     for level in levels:
+        order = order + [o ^ bit for bit in partners(level) for o in order]
+    order = jnp.asarray(order + [o ^ 1 for o in order], jnp.int32)
+    where = jnp.concatenate([jnp.stack([t, s]), s ^ order]).astype(jnp.int32)
+    mine, u_near, where = lax.optimization_barrier((mine, u_near, where))
+    for level in levels:
         mine = jnp.concatenate([mine] + [swap(mine, "space", bit) for bit in partners(level)], axis=0)
-        order = order + [o ^ bit for bit in partners(level) for o in order]
     mine, u_far = lax.optimization_barrier((mine, u_far))
     wide = mine.astype(jnp.float32)
     energy = jnp.sum(wide * wide, axis=(0, 2))[None]
     moves = [(0, 2), (1, 0), (1, 2)]
-    energy = energy + sum(lax.ppermute(energy, ("space", "tm"), crossing(*move)) for move in moves)
     energy = energy + swap(energy, "tm", 1)
+    energy = [energy] + [lax.ppermute(energy, ("space", "tm"), crossing(*move)) for move in moves]
     mine, energy = lax.optimization_barrier((mine, energy))
-    order = jnp.asarray(order + [o ^ 1 for o in order], jnp.int32)
-    where = jnp.concatenate([jnp.stack([t, s]), s ^ order]).astype(jnp.int32)
 
     def both(x):
         x = x.astype(jnp.float32)

time: 139 us -> 133 us (0.957)
  Pallas kernels: 72.3 us -> 67.2 us
  local copies, waits for them, and re-layouts: 4.76 us -> 1.98 us
  waiting for transfers between devices: 30.3 us -> 32.5 us
    pallas_call x2, Pallas kernels: 72.3 us -> 67.2 us  [gram_call(): pl.pallas_call(functools.partial(gram_kernel, plan, snaps, shrink, closin...]
    unnamed x26 -> x6, local copies, waits for them, and re-layouts: 3.71 us -> 0.93 us
    ppermute x10, waiting for transfers between devices: 12.5 us -> 14.9 us  [swap(): lax.ppermute(x, axis, [(i, i ^ bit) for i in range(lax.axis_size(axis))])]
  transfers between devices with their start and end apart: 18 -> 18, of which waited for: 10 -> 11; matrix products, arithmetic and copies ran while one was open for 1% -> 1% of each run, Pallas kernels for 14% -> 12%
where the time goes in v4:
time: 133 us
  Pallas kernels  67.2 us (51%)
  waiting for transfers between devices  32.5 us (24%)
  starting transfers between devices  23.6 us (18%)
  matrix products  4.93 us (4%)
  other arithmetic  2.02 us (2%)
  local copies, waits for them, and re-layouts  1.98 us (1%)
    pallas_call x2, Pallas kernels, gram_call(): pl.pallas_call(functools.partial(gram_kernel, plan, snaps, shrink, closin...  67.2 us
    all_to_all x1, waiting for transfers between devices, shards(): part = lax.all_to_all(part, 'space', 0, 0, tiled=False)  16.4 us
    ppermute x10, waiting for transfers between devices, swap(): lax.ppermute(x, axis, [(i, i ^ bit) for i in range(lax.axis_size(axis))])  14.9 us
    ppermute x10, starting transfers between devices, swap(): lax.ppermute(x, axis, [(i, i ^ bit) for i in range(lax.axis_size(axis))])  9.92 us
    all_to_all x1, starting transfers between devices, shards(): part = lax.all_to_all(part, 'space', 0, 0, tiled=False)  5.56 us
    dot_general x1, matrix products, shards(): jnp.einsum('dr,ds->rs', pod_basis, snapshots, preferred_element_type=jnp....  4.93 us
    ppermute x3, starting transfers between devices, some(): return lax.ppermute(x, ('space', 'tm'), pairs)  3.86 us
  transfers between devices with their start and end apart: 18, of which 11 were waited for; matrix products, arithmetic and copies ran while one was open for 1% of the time, Pallas kernels for 12%

profile of v4, /device:TPU:3, one launch (start us, length us, event | category | flops | bytes accessed | tf_op | source)
XLA Modules:
  0.0 132.5 jit_solution(12023724902107807122)
XLA Ops:
  0.0 0.9 copy-done
  0.9 4.9 %fusion = f16[96,4096]{1,0:T(8,128)(2,1)S(1)} fusion(bf16[1024,96]{0,1:T(8,128)(2,1)S(1)} %copy-done, bf16[1024,4096]{1,0:T(8,128)(2,1)} %param.4), kind=kOutput, calls=%fused_computation.1 | convolution fusion | flops 806092800 | bytes 9371648 | tf_op jit(solution)/shard_map/dr,ds->rs/dot_general | solution.py:366
  5.9 1.0 copy.8
  6.9 5.6 %all-to-all-start = ((f16[8,96,512]{2,1,0:T(8,128)(2,1)}), f16[8,96,512]{2,1,0:T(8,128)(2,1)}, u32[]{:S(2)}, u32[]{:S(2)}) async-start(f16[8,96,512]{2,1,0:T(8,128)(2,1)} %bitcast.14), calls=%async_computation | async-start | bytes 1572864 | tf_op jit(solution)/shard_map/all_to_all | solution.py:369
  12.5 1.3 collective-permute-start
  13.8 1.3 collective-permute-start.4
  15.1 0.1 pad_add_fusion.where_ref
  15.2 16.4 %all-to-all-done = f16[8,96,512]{2,1,0:T(8,128)(2,1)} async-done(((f16[8,96,512]{2,1,0:T(8,128)(2,1)}), f16[8,96,512]{2,1,0:T(8,128)(2,1)}, u32[]{:S(2)}, u32[]{:S(2)}) %all-to-all-start) | async-done | bytes 786464 | tf_op jit(solution)/shard_map/all_to_all | solution.py:369
  31.6 1.3 convert_reduce_fusion
  32.9 0.0 collective-permute-done.refs_3_.refs_7_
  32.9 2.2 %collective-permute-start.3 = (f16[1,96,512]{2,1,0:T(8,128)(2,1)S(1)}, f16[1,96,512]{2,1,0:T(8,128)(2,1)S(1)}, u32[]{:S(2)}, u32[]{:S(2)}) collective-permute-start(f16[1,96,512]{2,1,0:T(8,128)(2,1)S(1)} %convert_bitcast_fusion), channel_id=1, source_target_pairs={{0,24},{4,28},{8,16},{12,20},{16,8},{20,12},{24,0},{28,4},{1,25},{... | collective-permute-start | bytes 294920 | tf_op jit(solution)/shard_map/ppermute | solution.py:340
  35.1 0.0 collective-permute-start.2
  35.1 1.5 %collective-permute-start.1 = (f16[1,96,512]{2,1,0:T(8,128)(2,1)S(1)}, f16[1,96,512]{2,1,0:T(8,128)(2,1)S(1)}, u32[]{:S(2)}, u32[]{:S(2)}) collective-permute-start(f16[1,96,512]{2,1,0:T(8,128)(2,1)S(1)} %convert_bitcast_fusion), channel_id=1, source_target_pairs={{0,8},{4,12},{8,0},{12,4},{16,24},{20,28},{24,16},{28,20},{1,9},{5... | collective-permute-start | bytes 294920 | tf_op jit(solution)/shard_map/ppermute | solution.py:340
  36.5 1.8 %collective-permute-done.3 = f16[1,96,512]{2,1,0:T(8,128)(2,1)S(1)} collective-permute-done((f16[1,96,512]{2,1,0:T(8,128)(2,1)S(1)}, f16[1,96,512]{2,1,0:T(8,128)(2,1)S(1)}, u32[]{:S(2)}, u32[]{:S(2)}) %collective-permute-start.3) | collective-permute-done | bytes 98336 | tf_op jit(solution)/shard_map/ppermute | solution.py:340
  38.3 5.5 %collective-permute-done.2 = f16[1,96,512]{2,1,0:T(8,128)(2,1)S(1)} collective-permute-done((f16[1,96,512]{2,1,0:T(8,128)(2,1)S(1)}, f16[1,96,512]{2,1,0:T(8,128)(2,1)S(1)}, u32[]{:S(2)}, u32[]{:S(2)}) %collective-permute-start.2) | collective-permute-done | bytes 98336 | tf_op jit(solution)/shard_map/ppermute | solution.py:340
  43.9 0.0 collective-permute-done.1
  43.9 0.1 pad_maximum_fusion
  44.0 0.0 collective-permute-done.4.refs_8_
  44.0 0.2 multiply_reduce_fusion
  44.2 1.4 %collective-permute-start.5 = (f32[1,96]{1,0:T(1,128)S(1)}, f32[1,96]{1,0:T(1,128)S(1)}, u32[]{:S(2)}, u32[]{:S(2)}) collective-permute-start(f32[1,96]{1,0:T(1,128)S(1)} %bitcast.16), channel_id=1, source_target_pairs={{0,1},{1,0},{2,3},{3,2},{4,5},{5,4},{6,7},{7,6},{8,9},{9,8},{10,11... | collective-permute-start | bytes 1160 | tf_op jit(solution)/shard_map/ppermute | solution.py:340
  45.6 0.8 collective-permute-done.5
  46.5 0.6 collective-permute-start.8
  47.1 0.8 collective-permute-start.7
  47.9 1.2 collective-permute-start.6
  49.1 0.6 collective-permute-done.8.refs_7_.refs_13_
  49.7 0.0 collective-permute-done.7.refs_6_.refs_12_
  49.7 0.5 collective-permute-done.6.refs_5_.refs_11_
  50.3 0.1 convert_element_type.39.refs_0_
  50.4 2.1 %collective-permute-start.9 = (f32[4,96,512]{2,1,0:T(8,128)S(1)}, f32[4,96,512]{2,1,0:T(8,128)S(1)}, u32[]{:S(2)}, u32[]{:S(2)}) collective-permute-start(f32[4,96,512]{2,1,0:T(8,128)S(1)} %convert_element_type.39.refs_0_), channel_id=1, source_target_pairs={{0,1},{1,0},{2,3},{3,2},{4,5},{5,4},{6,7},{7,6},{8,9},{9,8},{10,11... | collective-permute-start | bytes 2359304 | tf_op jit(solution)/shard_map/ppermute | solution.py:340
  52.4 1.6 %collective-permute-start.12 = (f16[4,96,512]{2,1,0:T(8,128)(2,1)S(1)}, f16[4,96,512]{2,1,0:T(8,128)(2,1)S(1)}, u32[]{:S(2)}, u32[]{:S(2)}) collective-permute-start(f16[4,96,512]{2,1,0:T(8,128)(2,1)S(1)} %pad_maximum_fusion), channel_id=1, source_target_pairs={{0,6},{1,7},{2,4},{3,5},{4,2},{5,3},{6,0},{7,1},{8,14},{9,15},{10,... | collective-permute-start | bytes 1179656 | tf_op jit(solution)/shard_map/ppermute | solution.py:406
  54.1 0.2 collective-permute-start.11
  54.3 0.8 collective-permute-start.10
  55.1 0.0 collective-permute-done.9.refs_1_
  55.1 15.4 %gram.1.refs_14_ = f32[1344,768]{1,0:T(8,128)S(1)} custom-call(s32[10]{0:T(128)S(1)} %pad_add_fusion.where_ref, f32[4,96,512]{2,1,0:T(8,128)S(1)} %convert_element_type.39.refs_0_, f32[4,96,512]{2,1,0:T(8,128)S(1)} %collective-permute-done.9.refs_1_, bf16[112,4096]{1,0:T(8,128)(2,1)S(1)} %copy-done.1, ...), custom_call_target="tpu_custom_call" | custom-call | flops 16911433728 | bytes 20000000 | tf_op jit(solution)/shard_map/gram/pallas_call | solution.py:231
  70.5 1.5 %collective-permute-done.11 = f16[4,96,512]{2,1,0:T(8,128)(2,1)S(1)} collective-permute-done((f16[4,96,512]{2,1,0:T(8,128)(2,1)S(1)}, f16[4,96,512]{2,1,0:T(8,128)(2,1)S(1)}, u32[]{:S(2)}, u32[]{:S(2)}) %collective-permute-start.11) | collective-permute-done | bytes 393248 | tf_op jit(solution)/shard_map/ppermute | solution.py:340
  72.0 0.8 collective-permute-done.10
  72.8 1.3 collective-permute-start.16
  74.1 0.1 convert_element_type.40.refs_0_
  74.2 0.1 convert_element_type.41.refs_2_
  74.3 0.1 convert_element_type.42.refs_4_
  74.4 1.2 collective-permute-start.15
  75.7 0.1 collective-permute-start.14
  75.7 0.4 collective-permute-start.13
  76.2 2.1 %collective-permute-done.15.refs_5_ = f32[4,96,512]{2,1,0:T(8,128)S(1)} collective-permute-done((f32[4,96,512]{2,1,0:T(8,128)S(1)}, f32[4,96,512]{2,1,0:T(8,128)S(1)}, u32[]{:S(2)}, u32[]{:S(2)}) %collective-permute-start.15) | collective-permute-done | bytes 786464 | tf_op jit(solution)/shard_map/ppermute | solution.py:340
  78.3 1.1 collective-permute-done.14.refs_3_
  79.4 1.1 collective-permute-done.13.refs_1_
  80.6 0.0 collective-permute-done.16.refs_9_
  80.6 51.8 %close.1 = f32[1216,608]{1,0:T(8,128)} custom-call(s32[10]{0:T(128)S(1)} %pad_add_fusion.where_ref, f32[4,96,512]{2,1,0:T(8,128)S(1)} %convert_element_type.40.refs_0_, f32[4,96,512]{2,1,0:T(8,128)S(1)} %collective-permute-done.13.refs_1_, f32[4,96,512]{2,1,0:T(8,128)S(1)} %convert_element_type.41.refs_2_, ...), custom_call_target="tpu_custom_call" | custom-call | flops 50734301184 | bytes 20000000 | tf_op jit(solution)/shard_map/close/pallas_call | solution.py:231
  (9 shorter events, 0.0 us)
Async XLA Ops:
  0.0 0.9 copy-start
  0.0 15.1 %copy-start.2 = (s32[8]{0:T(128)S(1)}, s32[8]{0:T(128)}, u32[]{:S(2)}) copy-start(s32[8]{0:T(128)} %constant.15.clone) | copy-start | bytes 100
  0.9 11.5 %copy-start.1 = (bf16[112,4096]{1,0:T(8,128)(2,1)S(1)}, bf16[112,4096]{1,0:T(8,128)(2,1)}, u32[]{:S(2)}) copy-start(bf16[112,4096]{1,0:T(8,128)(2,1)} %refs_6_.1) | copy-start | bytes 2752516
  6.9 24.7 %all-to-all-start = ((f16[8,96,512]{2,1,0:T(8,128)(2,1)}), f16[8,96,512]{2,1,0:T(8,128)(2,1)}, u32[]{:S(2)}, u32[]{:S(2)}) async-start(f16[8,96,512]{2,1,0:T(8,128)(2,1)} %bitcast.14), calls=%async_computation | async-start | bytes 1572864 | tf_op jit(solution)/shard_map/all_to_all | solution.py:369
  12.5 20.4 %collective-permute-start = (bf16[112,4096]{1,0:T(8,128)(2,1)S(1)}, bf16[112,4096]{1,0:T(8,128)(2,1)S(1)}, u32[]{:S(2)}, u32[]{:S(2)}) collective-permute-start(bf16[112,4096]{1,0:T(8,128)(2,1)S(1)} %copy-done.1), channel_id=1, source_target_pairs={{2,3},{6,7},{10,11},{14,15},{18,19},{22,23},{26,27},{28,29},{29,28... | collective-permute-start | bytes 2752520 | tf_op jit(solution)/shard_map/ppermute | solution.py:359
  13.8 30.2 %collective-permute-start.4 = (bf16[112,4096]{1,0:T(8,128)(2,1)S(1)}, bf16[112,4096]{1,0:T(8,128)(2,1)S(1)}, u32[]{:S(2)}, u32[]{:S(2)}) collective-permute-start(bf16[112,4096]{1,0:T(8,128)(2,1)S(1)} %copy-done.1), channel_id=1, source_target_pairs={{0,2},{1,3},{4,6},{5,7},{8,10},{9,11},{12,14},{13,15},{16,18},{17,... | collective-permute-start | bytes 2752520 | tf_op jit(solution)/shard_map/ppermute | solution.py:359
  32.9 5.4 %collective-permute-start.3 = (f16[1,96,512]{2,1,0:T(8,128)(2,1)S(1)}, f16[1,96,512]{2,1,0:T(8,128)(2,1)S(1)}, u32[]{:S(2)}, u32[]{:S(2)}) collective-permute-start(f16[1,96,512]{2,1,0:T(8,128)(2,1)S(1)} %convert_bitcast_fusion), channel_id=1, source_target_pairs={{0,24},{4,28},{8,16},{12,20},{16,8},{20,12},{24,0},{28,4},{1,25},{... | collective-permute-start | bytes 294920 | tf_op jit(solution)/shard_map/ppermute | solution.py:340
  35.1 8.8 %collective-permute-start.2 = (f16[1,96,512]{2,1,0:T(8,128)(2,1)S(1)}, f16[1,96,512]{2,1,0:T(8,128)(2,1)S(1)}, u32[]{:S(2)}, u32[]{:S(2)}) collective-permute-start(f16[1,96,512]{2,1,0:T(8,128)(2,1)S(1)} %convert_bitcast_fusion), channel_id=1, source_target_pairs={{0,16},{4,20},{8,24},{12,28},{16,0},{20,4},{24,8},{28,12},{1,17},{... | collective-permute-start | bytes 294920 | tf_op jit(solution)/shard_map/ppermute | solution.py:340
  35.1 8.8 %collective-permute-start.1 = (f16[1,96,512]{2,1,0:T(8,128)(2,1)S(1)}, f16[1,96,512]{2,1,0:T(8,128)(2,1)S(1)}, u32[]{:S(2)}, u32[]{:S(2)}) collective-permute-start(f16[1,96,512]{2,1,0:T(8,128)(2,1)S(1)} %convert_bitcast_fusion), channel_id=1, source_target_pairs={{0,8},{4,12},{8,0},{12,4},{16,24},{20,28},{24,16},{28,20},{1,9},{5... | collective-permute-start | bytes 294920 | tf_op jit(solution)/shard_map/ppermute | solution.py:340
  44.2 2.3 %collective-permute-start.5 = (f32[1,96]{1,0:T(1,128)S(1)}, f32[1,96]{1,0:T(1,128)S(1)}, u32[]{:S(2)}, u32[]{:S(2)}) collective-permute-start(f32[1,96]{1,0:T(1,128)S(1)} %bitcast.16), channel_id=1, source_target_pairs={{0,1},{1,0},{2,3},{3,2},{4,5},{5,4},{6,7},{7,6},{8,9},{9,8},{10,11... | collective-permute-start | bytes 1160 | tf_op jit(solution)/shard_map/ppermute | solution.py:340
  46.5 3.3 %collective-permute-start.8 = (f32[1,96]{1,0:T(1,128)S(1)}, f32[1,96]{1,0:T(1,128)S(1)}, u32[]{:S(2)}, u32[]{:S(2)}) collective-permute-start(f32[1,96]{1,0:T(1,128)S(1)} %bitcast_add_fusion.refs_4_.refs_10_), channel_id=1, source_target_pairs={{0,6},{1,7},{2,4},{3,5},{4,2},{5,3},{6,0},{7,1},{8,14},{9,15},{10,... | collective-permute-start | bytes 1160 | tf_op jit(solution)/shard_map/ppermute | solution.py:397
  47.1 2.6 %collective-permute-start.7 = (f32[1,96]{1,0:T(1,128)S(1)}, f32[1,96]{1,0:T(1,128)S(1)}, u32[]{:S(2)}, u32[]{:S(2)}) collective-permute-start(f32[1,96]{1,0:T(1,128)S(1)} %bitcast_add_fusion.refs_4_.refs_10_), channel_id=1, source_target_pairs={{0,4},{1,5},{2,6},{3,7},{4,0},{5,1},{6,2},{7,3},{8,12},{9,13},{10,... | collective-permute-start | bytes 1160 | tf_op jit(solution)/shard_map/ppermute | solution.py:397
  47.9 2.4 %collective-permute-start.6 = (f32[1,96]{1,0:T(1,128)S(1)}, f32[1,96]{1,0:T(1,128)S(1)}, u32[]{:S(2)}, u32[]{:S(2)}) collective-permute-start(f32[1,96]{1,0:T(1,128)S(1)} %bitcast_add_fusion.refs_4_.refs_10_), channel_id=1, source_target_pairs={{0,2},{1,3},{2,0},{3,1},{4,6},{5,7},{6,4},{7,5},{8,10},{9,11},{10,... | collective-permute-start | bytes 1160 | tf_op jit(solution)/shard_map/ppermute | solution.py:397
  50.4 4.7 %collective-permute-start.9 = (f32[4,96,512]{2,1,0:T(8,128)S(1)}, f32[4,96,512]{2,1,0:T(8,128)S(1)}, u32[]{:S(2)}, u32[]{:S(2)}) collective-permute-start(f32[4,96,512]{2,1,0:T(8,128)S(1)} %convert_element_type.39.refs_0_), channel_id=1, source_target_pairs={{0,1},{1,0},{2,3},{3,2},{4,5},{5,4},{6,7},{7,6},{8,9},{9,8},{10,11... | collective-permute-start | bytes 2359304 | tf_op jit(solution)/shard_map/ppermute | solution.py:340
  52.4 18.1 %collective-permute-start.12 = (f16[4,96,512]{2,1,0:T(8,128)(2,1)S(1)}, f16[4,96,512]{2,1,0:T(8,128)(2,1)S(1)}, u32[]{:S(2)}, u32[]{:S(2)}) collective-permute-start(f16[4,96,512]{2,1,0:T(8,128)(2,1)S(1)} %pad_maximum_fusion), channel_id=1, source_target_pairs={{0,6},{1,7},{2,4},{3,5},{4,2},{5,3},{6,0},{7,1},{8,14},{9,15},{10,... | collective-permute-start | bytes 1179656 | tf_op jit(solution)/shard_map/ppermute | solution.py:406
  54.1 17.9 %collective-permute-start.11 = (f16[4,96,512]{2,1,0:T(8,128)(2,1)S(1)}, f16[4,96,512]{2,1,0:T(8,128)(2,1)S(1)}, u32[]{:S(2)}, u32[]{:S(2)}) collective-permute-start(f16[4,96,512]{2,1,0:T(8,128)(2,1)S(1)} %pad_maximum_fusion), channel_id=1, source_target_pairs={{0,2},{1,3},{2,0},{3,1},{4,6},{5,7},{6,4},{7,5},{8,10},{9,11},{10,... | collective-permute-start | bytes 1179656 | tf_op jit(solution)/shard_map/ppermute | solution.py:340
  54.3 18.5 %collective-permute-start.10 = (f16[4,96,512]{2,1,0:T(8,128)(2,1)S(1)}, f16[4,96,512]{2,1,0:T(8,128)(2,1)S(1)}, u32[]{:S(2)}, u32[]{:S(2)}) collective-permute-start(f16[4,96,512]{2,1,0:T(8,128)(2,1)S(1)} %pad_maximum_fusion), channel_id=1, source_target_pairs={{0,4},{4,0},{8,12},{12,8},{16,20},{20,16},{24,28},{28,24},{1,5},{5... | collective-permute-start | bytes 1179656 | tf_op jit(solution)/shard_map/ppermute | solution.py:340
  72.8 7.7 %collective-permute-start.16 = (bf16[112,4096]{1,0:T(8,128)(2,1)S(1)}, bf16[112,4096]{1,0:T(8,128)(2,1)S(1)}, u32[]{:S(2)}, u32[]{:S(2)}) collective-permute-start(bf16[112,4096]{1,0:T(8,128)(2,1)S(1)} %collective-permute-done.4.refs_8_), channel_id=1, source_target_pairs={{2,3},{6,7},{10,11},{14,15},{18,19},{22,23},{26,27},{28,29},{29,28... | collective-permute-start | bytes 2752520 | tf_op jit(solution)/shard_map/ppermute | solution.py:359
  74.4 3.9 %collective-permute-start.15 = (f32[4,96,512]{2,1,0:T(8,128)S(1)}, f32[4,96,512]{2,1,0:T(8,128)S(1)}, u32[]{:S(2)}, u32[]{:S(2)}) collective-permute-start(f32[4,96,512]{2,1,0:T(8,128)S(1)} %convert_element_type.42.refs_4_), channel_id=1, source_target_pairs={{0,1},{1,0},{2,3},{3,2},{4,5},{5,4},{6,7},{7,6},{8,9},{9,8},{10,11... | collective-permute-start | bytes 2359304 | tf_op jit(solution)/shard_map/ppermute | solution.py:340
  75.7 3.8 %collective-permute-start.14 = (f32[4,96,512]{2,1,0:T(8,128)S(1)}, f32[4,96,512]{2,1,0:T(8,128)S(1)}, u32[]{:S(2)}, u32[]{:S(2)}) collective-permute-start(f32[4,96,512]{2,1,0:T(8,128)S(1)} %convert_element_type.41.refs_2_), channel_id=1, source_target_pairs={{0,1},{1,0},{2,3},{3,2},{4,5},{5,4},{6,7},{7,6},{8,9},{9,8},{10,11... | collective-permute-start | bytes 2359304 | tf_op jit(solution)/shard_map/ppermute | solution.py:340
  75.7 4.8 %collective-permute-start.13 = (f32[4,96,512]{2,1,0:T(8,128)S(1)}, f32[4,96,512]{2,1,0:T(8,128)S(1)}, u32[]{:S(2)}, u32[]{:S(2)}) collective-permute-start(f32[4,96,512]{2,1,0:T(8,128)S(1)} %convert_element_type.40.refs_0_), channel_id=1, source_target_pairs={{0,1},{1,0},{2,3},{3,2},{4,5},{5,4},{6,7},{7,6},{8,9},{9,8},{10,11... | collective-permute-start | bytes 2359304 | tf_op jit(solution)/shard_map/ppermute | solution.py:340

commit v5 on v4

--- a/solution.py
+++ b/solution.py
@@ -398,8 +398,7 @@
     mine, energy = lax.optimization_barrier((mine, energy))
 
     def both(x):
-        x = x.astype(jnp.float32)
-        return x, swap(x, "tm", 1)
+        return x.astype(jnp.float32), swap(x, "tm", 1).astype(jnp.float32)
 
     beside = swap(mine, "space", 1)
     far = swap(mine, "tm", 2)

time: 133 us -> 131 us (0.985)
  waiting for transfers between devices: 32.5 us -> 30.4 us
    ppermute x10, waiting for transfers between devices: 14.9 us -> 12.8 us  [swap(): lax.ppermute(x, axis, [(i, i ^ bit) for i in range(lax.axis_size(axis))])]
  transfers between devices with their start and end apart: 18 -> 18, of which waited for: 11 -> 11; matrix products, arithmetic and copies ran while one was open for 1% -> 2% of each run, Pallas kernels for 12% -> 12%
where the time goes in v5:
time: 131 us
  Pallas kernels  67.2 us (51%)
  waiting for transfers between devices  30.4 us (23%)
  starting transfers between devices  23.5 us (18%)
  matrix products  4.93 us (4%)
  other arithmetic  2.36 us (2%)
  local copies, waits for them, and re-layouts  1.98 us (2%)
    pallas_call x2, Pallas kernels, gram_call(): pl.pallas_call(functools.partial(gram_kernel, plan, snaps, shrink, closin...  67.2 us
    all_to_all x1, waiting for transfers between devices, shards(): part = lax.all_to_all(part, 'space', 0, 0, tiled=False)  16.4 us
    ppermute x10, waiting for transfers between devices, swap(): lax.ppermute(x, axis, [(i, i ^ bit) for i in range(lax.axis_size(axis))])  12.8 us
    ppermute x10, starting transfers between devices, swap(): lax.ppermute(x, axis, [(i, i ^ bit) for i in range(lax.axis_size(axis))])  9.85 us
    all_to_all x1, starting transfers between devices, shards(): part = lax.all_to_all(part, 'space', 0, 0, tiled=False)  5.56 us
    dot_general x1, matrix products, shards(): jnp.einsum('dr,ds->rs', pod_basis, snapshots, preferred_element_type=jnp....  4.93 us
    ppermute x3, starting transfers between devices, some(): return lax.ppermute(x, ('space', 'tm'), pairs)  3.86 us
    ppermute x3, starting transfers between devices, shards(): lax.ppermute(energy, ('space', 'tm'), crossing(*move))  2.65 us
  transfers between devices with their start and end apart: 18, of which 11 were waited for; matrix products, arithmetic and copies ran while one was open for 2% of the time, Pallas kernels for 12%

profile of v5, /device:TPU:3, one launch (start us, length us, event | category | flops | bytes accessed | tf_op | source)
XLA Modules:
  0.0 130.7 jit_solution(15474464630479271655)
XLA Ops:
  0.0 0.9 copy-done
  0.9 4.9 %fusion = f16[96,4096]{1,0:T(8,128)(2,1)S(1)} fusion(bf16[1024,96]{0,1:T(8,128)(2,1)S(1)} %copy-done, bf16[1024,4096]{1,0:T(8,128)(2,1)} %param.4), kind=kOutput, calls=%fused_computation.1 | convolution fusion | flops 806092800 | bytes 9371648 | tf_op jit(solution)/shard_map/dr,ds->rs/dot_general | solution.py:366
  5.9 1.0 copy.8
  6.9 5.6 %all-to-all-start = ((f16[8,96,512]{2,1,0:T(8,128)(2,1)}), f16[8,96,512]{2,1,0:T(8,128)(2,1)}, u32[]{:S(2)}, u32[]{:S(2)}) async-start(f16[8,96,512]{2,1,0:T(8,128)(2,1)} %bitcast.14), calls=%async_computation | async-start | bytes 1572864 | tf_op jit(solution)/shard_map/all_to_all | solution.py:369
  12.5 1.3 collective-permute-start
  13.8 1.3 collective-permute-start.4
  15.1 0.1 pad_add_fusion.where_ref
  15.2 16.4 %all-to-all-done = f16[8,96,512]{2,1,0:T(8,128)(2,1)} async-done(((f16[8,96,512]{2,1,0:T(8,128)(2,1)}), f16[8,96,512]{2,1,0:T(8,128)(2,1)}, u32[]{:S(2)}, u32[]{:S(2)}) %all-to-all-start) | async-done | bytes 786464 | tf_op jit(solution)/shard_map/all_to_all | solution.py:369
  31.6 1.3 convert_reduce_fusion
  32.9 0.0 collective-permute-done.refs_3_.refs_7_
  32.9 2.2 %collective-permute-start.3 = (f16[1,96,512]{2,1,0:T(8,128)(2,1)S(1)}, f16[1,96,512]{2,1,0:T(8,128)(2,1)S(1)}, u32[]{:S(2)}, u32[]{:S(2)}) collective-permute-start(f16[1,96,512]{2,1,0:T(8,128)(2,1)S(1)} %convert_bitcast_fusion), channel_id=1, source_target_pairs={{0,24},{4,28},{8,16},{12,20},{16,8},{20,12},{24,0},{28,4},{1,25},{... | collective-permute-start | bytes 294920 | tf_op jit(solution)/shard_map/ppermute | solution.py:340
  35.1 1.5 %collective-permute-start.1 = (f16[1,96,512]{2,1,0:T(8,128)(2,1)S(1)}, f16[1,96,512]{2,1,0:T(8,128)(2,1)S(1)}, u32[]{:S(2)}, u32[]{:S(2)}) collective-permute-start(f16[1,96,512]{2,1,0:T(8,128)(2,1)S(1)} %convert_bitcast_fusion), channel_id=1, source_target_pairs={{0,8},{4,12},{8,0},{12,4},{16,24},{20,28},{24,16},{28,20},{1,9},{5... | collective-permute-start | bytes 294920 | tf_op jit(solution)/shard_map/ppermute | solution.py:340
  36.5 1.8 %collective-permute-done.3 = f16[1,96,512]{2,1,0:T(8,128)(2,1)S(1)} collective-permute-done((f16[1,96,512]{2,1,0:T(8,128)(2,1)S(1)}, f16[1,96,512]{2,1,0:T(8,128)(2,1)S(1)}, u32[]{:S(2)}, u32[]{:S(2)}) %collective-permute-start.3) | collective-permute-done | bytes 98336 | tf_op jit(solution)/shard_map/ppermute | solution.py:340
  38.3 5.5 %collective-permute-done.2 = f16[1,96,512]{2,1,0:T(8,128)(2,1)S(1)} collective-permute-done((f16[1,96,512]{2,1,0:T(8,128)(2,1)S(1)}, f16[1,96,512]{2,1,0:T(8,128)(2,1)S(1)}, u32[]{:S(2)}, u32[]{:S(2)}) %collective-permute-start.2) | collective-permute-done | bytes 98336 | tf_op jit(solution)/shard_map/ppermute | solution.py:340
  43.9 0.0 collective-permute-done.1
  43.9 0.1 pad_maximum_fusion
  44.0 0.2 multiply_reduce_fusion
  44.2 1.4 %collective-permute-start.5 = (f32[1,96]{1,0:T(1,128)S(1)}, f32[1,96]{1,0:T(1,128)S(1)}, u32[]{:S(2)}, u32[]{:S(2)}) collective-permute-start(f32[1,96]{1,0:T(1,128)S(1)} %bitcast.16), channel_id=1, source_target_pairs={{0,1},{1,0},{2,3},{3,2},{4,5},{5,4},{6,7},{7,6},{8,9},{9,8},{10,11... | collective-permute-start | bytes 1160 | tf_op jit(solution)/shard_map/ppermute | solution.py:340
  45.6 0.8 collective-permute-done.5
  46.5 0.6 collective-permute-start.8
  47.1 0.8 collective-permute-start.7
  47.9 1.2 collective-permute-start.6
  49.1 0.6 collective-permute-done.8.refs_7_.refs_13_
  49.7 0.0 collective-permute-done.7.refs_6_.refs_12_
  49.7 0.5 collective-permute-done.6.refs_5_.refs_11_
  50.3 2.0 %collective-permute-start.9 = (f16[4,96,512]{2,1,0:T(8,128)(2,1)S(1)}, f16[4,96,512]{2,1,0:T(8,128)(2,1)S(1)}, u32[]{:S(2)}, u32[]{:S(2)}) collective-permute-start(f16[4,96,512]{2,1,0:T(8,128)(2,1)S(1)} %pad_maximum_fusion), channel_id=1, source_target_pairs={{0,1},{1,0},{2,3},{3,2},{4,5},{5,4},{6,7},{7,6},{8,9},{9,8},{10,11... | collective-permute-start | bytes 1179656 | tf_op jit(solution)/shard_map/ppermute | solution.py:340
  52.3 1.6 %collective-permute-start.12 = (f16[4,96,512]{2,1,0:T(8,128)(2,1)S(1)}, f16[4,96,512]{2,1,0:T(8,128)(2,1)S(1)}, u32[]{:S(2)}, u32[]{:S(2)}) collective-permute-start(f16[4,96,512]{2,1,0:T(8,128)(2,1)S(1)} %pad_maximum_fusion), channel_id=1, source_target_pairs={{0,6},{1,7},{2,4},{3,5},{4,2},{5,3},{6,0},{7,1},{8,14},{9,15},{10,... | collective-permute-start | bytes 1179656 | tf_op jit(solution)/shard_map/ppermute | solution.py:405
  53.9 0.2 collective-permute-start.11
  54.2 0.8 collective-permute-start.10
  54.9 0.1 convert_element_type.51.refs_0_
  55.0 0.1 convert_element_type.52.refs_1_
  55.1 15.4 %gram.1.refs_14_ = f32[1344,768]{1,0:T(8,128)S(1)} custom-call(s32[10]{0:T(128)S(1)} %pad_add_fusion.where_ref, f32[4,96,512]{2,1,0:T(8,128)S(1)} %convert_element_type.51.refs_0_, f32[4,96,512]{2,1,0:T(8,128)S(1)} %convert_element_type.52.refs_1_, bf16[112,4096]{1,0:T(8,128)(2,1)S(1)} %copy-done.1, ...), custom_call_target="tpu_custom_call" | custom-call | flops 16911433728 | bytes 20000000 | tf_op jit(solution)/shard_map/gram/pallas_call | solution.py:231
  70.5 1.4 %collective-permute-done.11 = f16[4,96,512]{2,1,0:T(8,128)(2,1)S(1)} collective-permute-done((f16[4,96,512]{2,1,0:T(8,128)(2,1)S(1)}, f16[4,96,512]{2,1,0:T(8,128)(2,1)S(1)}, u32[]{:S(2)}, u32[]{:S(2)}) %collective-permute-start.11) | collective-permute-done | bytes 393248 | tf_op jit(solution)/shard_map/ppermute | solution.py:340
  71.9 0.7 collective-permute-done.10
  72.6 1.3 collective-permute-start.16
  73.9 1.2 collective-permute-start.13
  75.2 0.1 collective-permute-start.14
  75.3 0.4 collective-permute-start.15
  75.7 0.1 convert_element_type.53.refs_0_
  75.8 0.1 convert_element_type.55.refs_2_
  75.9 0.1 convert_element_type.57.refs_4_
  76.0 1.6 %collective-permute-done.13 = f16[4,96,512]{2,1,0:T(8,128)(2,1)S(1)} collective-permute-done((f16[4,96,512]{2,1,0:T(8,128)(2,1)S(1)}, f16[4,96,512]{2,1,0:T(8,128)(2,1)S(1)}, u32[]{:S(2)}, u32[]{:S(2)}) %collective-permute-start.13) | collective-permute-done | bytes 393248 | tf_op jit(solution)/shard_map/ppermute | solution.py:340
  77.6 0.1 convert_element_type.54.refs_1_
  77.7 0.5 collective-permute-done.14
  78.1 0.1 convert_element_type.56.refs_3_
  78.2 0.5 collective-permute-done.15
  78.7 0.1 convert_element_type.58.refs_5_
  78.8 51.8 %close.1 = f32[1216,608]{1,0:T(8,128)} custom-call(s32[10]{0:T(128)S(1)} %pad_add_fusion.where_ref, f32[4,96,512]{2,1,0:T(8,128)S(1)} %convert_element_type.53.refs_0_, f32[4,96,512]{2,1,0:T(8,128)S(1)} %convert_element_type.54.refs_1_, f32[4,96,512]{2,1,0:T(8,128)S(1)} %convert_element_type.55.refs_2_, f32[4,96,512]{2,1,0:T(8,128)S(1)} %convert_element_type.56.refs_3_, ...), custom_call_target="tpu_custom_call" | custom-call | flops 50734301184 | bytes 20000000 | tf_op jit(solution)/shard_map/close/pallas_call | solution.py:231
  (13 shorter events, 0.0 us)
Async XLA Ops:
  0.0 0.9 copy-start
  0.0 15.1 %copy-start.2 = (s32[8]{0:T(128)S(1)}, s32[8]{0:T(128)}, u32[]{:S(2)}) copy-start(s32[8]{0:T(128)} %constant.15.clone) | copy-start | bytes 100
  0.9 11.5 %copy-start.1 = (bf16[112,4096]{1,0:T(8,128)(2,1)S(1)}, bf16[112,4096]{1,0:T(8,128)(2,1)}, u32[]{:S(2)}) copy-start(bf16[112,4096]{1,0:T(8,128)(2,1)} %refs_6_.1) | copy-start | bytes 2752516
  6.9 24.7 %all-to-all-start = ((f16[8,96,512]{2,1,0:T(8,128)(2,1)}), f16[8,96,512]{2,1,0:T(8,128)(2,1)}, u32[]{:S(2)}, u32[]{:S(2)}) async-start(f16[8,96,512]{2,1,0:T(8,128)(2,1)} %bitcast.14), calls=%async_computation | async-start | bytes 1572864 | tf_op jit(solution)/shard_map/all_to_all | solution.py:369
  12.5 20.4 %collective-permute-start = (bf16[112,4096]{1,0:T(8,128)(2,1)S(1)}, bf16[112,4096]{1,0:T(8,128)(2,1)S(1)}, u32[]{:S(2)}, u32[]{:S(2)}) collective-permute-start(bf16[112,4096]{1,0:T(8,128)(2,1)S(1)} %copy-done.1), channel_id=1, source_target_pairs={{2,3},{6,7},{10,11},{14,15},{18,19},{22,23},{26,27},{28,29},{29,28... | collective-permute-start | bytes 2752520 | tf_op jit(solution)/shard_map/ppermute | solution.py:359
  13.8 30.2 %collective-permute-start.4 = (bf16[112,4096]{1,0:T(8,128)(2,1)S(1)}, bf16[112,4096]{1,0:T(8,128)(2,1)S(1)}, u32[]{:S(2)}, u32[]{:S(2)}) collective-permute-start(bf16[112,4096]{1,0:T(8,128)(2,1)S(1)} %copy-done.1), channel_id=1, source_target_pairs={{0,2},{1,3},{4,6},{5,7},{8,10},{9,11},{12,14},{13,15},{16,18},{17,... | collective-permute-start | bytes 2752520 | tf_op jit(solution)/shard_map/ppermute | solution.py:359
  32.9 5.4 %collective-permute-start.3 = (f16[1,96,512]{2,1,0:T(8,128)(2,1)S(1)}, f16[1,96,512]{2,1,0:T(8,128)(2,1)S(1)}, u32[]{:S(2)}, u32[]{:S(2)}) collective-permute-start(f16[1,96,512]{2,1,0:T(8,128)(2,1)S(1)} %convert_bitcast_fusion), channel_id=1, source_target_pairs={{0,24},{4,28},{8,16},{12,20},{16,8},{20,12},{24,0},{28,4},{1,25},{... | collective-permute-start | bytes 294920 | tf_op jit(solution)/shard_map/ppermute | solution.py:340
  35.1 8.8 %collective-permute-start.2 = (f16[1,96,512]{2,1,0:T(8,128)(2,1)S(1)}, f16[1,96,512]{2,1,0:T(8,128)(2,1)S(1)}, u32[]{:S(2)}, u32[]{:S(2)}) collective-permute-start(f16[1,96,512]{2,1,0:T(8,128)(2,1)S(1)} %convert_bitcast_fusion), channel_id=1, source_target_pairs={{0,16},{4,20},{8,24},{12,28},{16,0},{20,4},{24,8},{28,12},{1,17},{... | collective-permute-start | bytes 294920 | tf_op jit(solution)/shard_map/ppermute | solution.py:340
  35.1 8.8 %collective-permute-start.1 = (f16[1,96,512]{2,1,0:T(8,128)(2,1)S(1)}, f16[1,96,512]{2,1,0:T(8,128)(2,1)S(1)}, u32[]{:S(2)}, u32[]{:S(2)}) collective-permute-start(f16[1,96,512]{2,1,0:T(8,128)(2,1)S(1)} %convert_bitcast_fusion), channel_id=1, source_target_pairs={{0,8},{4,12},{8,0},{12,4},{16,24},{20,28},{24,16},{28,20},{1,9},{5... | collective-permute-start | bytes 294920 | tf_op jit(solution)/shard_map/ppermute | solution.py:340
  44.2 2.3 %collective-permute-start.5 = (f32[1,96]{1,0:T(1,128)S(1)}, f32[1,96]{1,0:T(1,128)S(1)}, u32[]{:S(2)}, u32[]{:S(2)}) collective-permute-start(f32[1,96]{1,0:T(1,128)S(1)} %bitcast.16), channel_id=1, source_target_pairs={{0,1},{1,0},{2,3},{3,2},{4,5},{5,4},{6,7},{7,6},{8,9},{9,8},{10,11... | collective-permute-start | bytes 1160 | tf_op jit(solution)/shard_map/ppermute | solution.py:340
  46.5 3.3 %collective-permute-start.8 = (f32[1,96]{1,0:T(1,128)S(1)}, f32[1,96]{1,0:T(1,128)S(1)}, u32[]{:S(2)}, u32[]{:S(2)}) collective-permute-start(f32[1,96]{1,0:T(1,128)S(1)} %bitcast_add_fusion.refs_4_.refs_10_), channel_id=1, source_target_pairs={{0,6},{1,7},{2,4},{3,5},{4,2},{5,3},{6,0},{7,1},{8,14},{9,15},{10,... | collective-permute-start | bytes 1160 | tf_op jit(solution)/shard_map/ppermute | solution.py:397
  47.1 2.6 %collective-permute-start.7 = (f32[1,96]{1,0:T(1,128)S(1)}, f32[1,96]{1,0:T(1,128)S(1)}, u32[]{:S(2)}, u32[]{:S(2)}) collective-permute-start(f32[1,96]{1,0:T(1,128)S(1)} %bitcast_add_fusion.refs_4_.refs_10_), channel_id=1, source_target_pairs={{0,4},{1,5},{2,6},{3,7},{4,0},{5,1},{6,2},{7,3},{8,12},{9,13},{10,... | collective-permute-start | bytes 1160 | tf_op jit(solution)/shard_map/ppermute | solution.py:397
  47.9 2.4 %collective-permute-start.6 = (f32[1,96]{1,0:T(1,128)S(1)}, f32[1,96]{1,0:T(1,128)S(1)}, u32[]{:S(2)}, u32[]{:S(2)}) collective-permute-start(f32[1,96]{1,0:T(1,128)S(1)} %bitcast_add_fusion.refs_4_.refs_10_), channel_id=1, source_target_pairs={{0,2},{1,3},{2,0},{3,1},{4,6},{5,7},{6,4},{7,5},{8,10},{9,11},{10,... | collective-permute-start | bytes 1160 | tf_op jit(solution)/shard_map/ppermute | solution.py:397
  50.3 4.8 %collective-permute-start.9 = (f16[4,96,512]{2,1,0:T(8,128)(2,1)S(1)}, f16[4,96,512]{2,1,0:T(8,128)(2,1)S(1)}, u32[]{:S(2)}, u32[]{:S(2)}) collective-permute-start(f16[4,96,512]{2,1,0:T(8,128)(2,1)S(1)} %pad_maximum_fusion), channel_id=1, source_target_pairs={{0,1},{1,0},{2,3},{3,2},{4,5},{5,4},{6,7},{7,6},{8,9},{9,8},{10,11... | collective-permute-start | bytes 1179656 | tf_op jit(solution)/shard_map/ppermute | solution.py:340
  52.3 18.2 %collective-permute-start.12 = (f16[4,96,512]{2,1,0:T(8,128)(2,1)S(1)}, f16[4,96,512]{2,1,0:T(8,128)(2,1)S(1)}, u32[]{:S(2)}, u32[]{:S(2)}) collective-permute-start(f16[4,96,512]{2,1,0:T(8,128)(2,1)S(1)} %pad_maximum_fusion), channel_id=1, source_target_pairs={{0,6},{1,7},{2,4},{3,5},{4,2},{5,3},{6,0},{7,1},{8,14},{9,15},{10,... | collective-permute-start | bytes 1179656 | tf_op jit(solution)/shard_map/ppermute | solution.py:405
  53.9 18.0 %collective-permute-start.11 = (f16[4,96,512]{2,1,0:T(8,128)(2,1)S(1)}, f16[4,96,512]{2,1,0:T(8,128)(2,1)S(1)}, u32[]{:S(2)}, u32[]{:S(2)}) collective-permute-start(f16[4,96,512]{2,1,0:T(8,128)(2,1)S(1)} %pad_maximum_fusion), channel_id=1, source_target_pairs={{0,2},{1,3},{2,0},{3,1},{4,6},{5,7},{6,4},{7,5},{8,10},{9,11},{10,... | collective-permute-start | bytes 1179656 | tf_op jit(solution)/shard_map/ppermute | solution.py:340
  54.2 18.5 %collective-permute-start.10 = (f16[4,96,512]{2,1,0:T(8,128)(2,1)S(1)}, f16[4,96,512]{2,1,0:T(8,128)(2,1)S(1)}, u32[]{:S(2)}, u32[]{:S(2)}) collective-permute-start(f16[4,96,512]{2,1,0:T(8,128)(2,1)S(1)} %pad_maximum_fusion), channel_id=1, source_target_pairs={{0,4},{4,0},{8,12},{12,8},{16,20},{20,16},{24,28},{28,24},{1,5},{5... | collective-permute-start | bytes 1179656 | tf_op jit(solution)/shard_map/ppermute | solution.py:340
  72.6 6.1 %collective-permute-start.16 = (bf16[112,4096]{1,0:T(8,128)(2,1)S(1)}, bf16[112,4096]{1,0:T(8,128)(2,1)S(1)}, u32[]{:S(2)}, u32[]{:S(2)}) collective-permute-start(bf16[112,4096]{1,0:T(8,128)(2,1)S(1)} %collective-permute-done.4.refs_8_), channel_id=1, source_target_pairs={{2,3},{6,7},{10,11},{14,15},{18,19},{22,23},{26,27},{28,29},{29,28... | collective-permute-start | bytes 2752520 | tf_op jit(solution)/shard_map/ppermute | solution.py:359
  73.9 3.6 %collective-permute-start.13 = (f16[4,96,512]{2,1,0:T(8,128)(2,1)S(1)}, f16[4,96,512]{2,1,0:T(8,128)(2,1)S(1)}, u32[]{:S(2)}, u32[]{:S(2)}) collective-permute-start(f16[4,96,512]{2,1,0:T(8,128)(2,1)S(1)} %collective-permute-done.10), channel_id=1, source_target_pairs={{0,1},{1,0},{2,3},{3,2},{4,5},{5,4},{6,7},{7,6},{8,9},{9,8},{10,11... | collective-permute-start | bytes 1179656 | tf_op jit(solution)/shard_map/ppermute | solution.py:340
  75.2 2.9 %collective-permute-start.14 = (f16[4,96,512]{2,1,0:T(8,128)(2,1)S(1)}, f16[4,96,512]{2,1,0:T(8,128)(2,1)S(1)}, u32[]{:S(2)}, u32[]{:S(2)}) collective-permute-start(f16[4,96,512]{2,1,0:T(8,128)(2,1)S(1)} %collective-permute-done.11), channel_id=1, source_target_pairs={{0,1},{1,0},{2,3},{3,2},{4,5},{5,4},{6,7},{7,6},{8,9},{9,8},{10,11... | collective-permute-start | bytes 1179656 | tf_op jit(solution)/shard_map/ppermute | solution.py:340
  75.3 3.4 %collective-permute-start.15 = (f16[4,96,512]{2,1,0:T(8,128)(2,1)S(1)}, f16[4,96,512]{2,1,0:T(8,128)(2,1)S(1)}, u32[]{:S(2)}, u32[]{:S(2)}) collective-permute-start(f16[4,96,512]{2,1,0:T(8,128)(2,1)S(1)} %collective-permute-done.12), channel_id=1, source_target_pairs={{0,1},{1,0},{2,3},{3,2},{4,5},{5,4},{6,7},{7,6},{8,9},{9,8},{10,11... | collective-permute-start | bytes 1179656 | tf_op jit(solution)/shard_map/ppermute | solution.py:340
